TPU v7x, 128 devices: a whole 4x4x4 slice. The times are simulated.
128 devices in a mesh: dp: 8 (over z_hi, x), tensor: 16 (over y, z_lo, core).
Axes of the slice: x: 4, y: 4, z: 4 (z_hi: 2, z_lo: 2; z = z_hi * 2 + z_lo), core: 2. Of those that a mesh axis runs over, the one named last changes fastest.
Arguments:
- inputs: bfloat16 [16, 1024, 2048], P('dp', 'tensor'), may hold values from -6 to 6
- teacher: bfloat16 [16, 1024, 2048], P('dp', 'tensor'), may hold values from -6 to 6
- segment_ids: int32 [16, 1024], P('dp'), may hold values from 0 to 3, never falling along the last dimension, each value on 1 to 512 neighbouring positions
- padding: int32 [16, 1024], P('dp', 'tensor'), may hold values from 0 to 1, as said below
- attn_gain: float32 [2048], replicated, may hold values from 0.5 to 1.5
- qkv_weight: bfloat16 [2048, 3, 2048], P('dp', None, 'tensor'), may hold values from -0.125 to 0.125
- beta_weight: bfloat16 [2048, 16], P('dp', 'tensor'), may hold values from -0.125 to 0.125
- conv_taps: bfloat16 [4, 3, 16, 128], P(None, None, 'tensor', 'dp'), may hold values from -4 to 4
- head_gain: bfloat16 [16, 128], P('tensor', 'dp'), may hold values from 0.5 to 1.5
- out_weight: bfloat16 [2048, 2048], P('tensor', 'dp'), may hold values from -0.125 to 0.125
- mlp_gain: float32 [2048], replicated, may hold values from 0.5 to 1.5
- gate_weight: bfloat16 [2048, 5632], P('dp', 'tensor'), may hold values from -0.125 to 0.125
- up_weight: bfloat16 [2048, 5632], P('dp', 'tensor'), may hold values from -0.125 to 0.125
- down_weight: bfloat16 [5632, 2048], P('tensor', 'dp'), may hold values from -0.15625 to 0.15625
Outputs:
- block_out: bfloat16 [16, 1024, 2048], P('dp', 'tensor')
- loss: float32 [], replicated
- input_grad: float32 [16, 1024, 2048], P('dp', 'tensor')
- attn_gain_grad: float32 [2048], replicated
- qkv_grad: float32 [2048, 3, 2048], P('dp', None, 'tensor')
- beta_grad: float32 [2048, 16], P('dp', 'tensor')
- taps_grad: float32 [4, 3, 16, 128], P(None, None, 'tensor', 'dp')
- head_gain_grad: float32 [16, 128], P('tensor', 'dp')
- out_grad: float32 [2048, 2048], P('tensor', 'dp')
- mlp_gain_grad: float32 [2048], replicated
- gate_grad: float32 [2048, 5632], P('dp', 'tensor')
- up_grad: float32 [2048, 5632], P('dp', 'tensor')
- down_grad: float32 [5632, 2048], P('tensor', 'dp')
Inputs may be any that keep to these rules, and one draw needn't show every extreme that they name: `padding`: in each sequence the tokens that count form a leading run of 256 to 767 tokens; the rest are 0. `segment_ids`: document numbers never fall along a sequence; a document has 1 to 512 tokens.
All inputs are finite; a program needn't handle non-finite values.
Results may differ from a plain program's by a relative error of at most 0.029.
Values may be sent and summed in bfloat16 or wider, within the bound.
A program may use at most 192 MiB of HBM per device.

v0:
```python
import jax
import jax.numpy as jnp
from jax import lax
from jax.sharding import PartitionSpec as P

GROUP = 64


highest = lax.Precision.HIGHEST


def rms_norm(values, epsilon):
    return values * lax.rsqrt(jnp.mean(values * values, -1, keepdims=True) + epsilon)


def unit_norm(values):
    return values * lax.rsqrt(jnp.sum(values * values, -1, keepdims=True) + 1e-06)


def short_conv(fields, taps, segment):
    length = fields.shape[0]
    total = fields * taps[0]
    for offset in range(1, taps.shape[0]):
        blank_rows = jnp.zeros((offset,) + fields.shape[1:], fields.dtype)
        moved = jnp.concatenate([blank_rows, fields[: length - offset]], 0)
        earlier = jnp.concatenate(
            [jnp.full((offset,), -1, jnp.int32), segment[: length - offset]], 0
        )
        keep = (earlier == segment).astype(fields.dtype)
        total = total + moved * keep[:, None, None, None] * taps[offset]
    return total


def delta_block(carry, block):
    state, previous = carry
    query, keys, values, beta, segment = block
    size = segment.shape[0]
    dtype = state.dtype
    carried = (segment == previous).astype(dtype)
    same = (segment[:, None] == segment[None, :]).astype(dtype)
    strict = jnp.tril(jnp.ones((size, size), dtype), -1)
    within = jnp.tril(jnp.ones((size, size), dtype))
    gram = jnp.einsum("htk,hsk->hts", keys, keys, precision=highest)
    mixing = gram * beta[:, None, :] * (same * strict)
    recalled = jnp.einsum("htk,hvk->htv", keys, state, precision=highest)
    target = values - carried[None, :, None] * recalled
    system = jnp.eye(size, dtype=dtype)[None] + mixing
    updates = jax.vmap(
        lambda matrix, right: jax.scipy.linalg.solve_triangular(
            matrix, right, lower=True, unit_diagonal=True
        )
    )(system, target)
    weighted = updates * beta[:, :, None]
    scores = jnp.einsum("htk,hsk->hts", query, keys, precision=highest) * (same * within)
    output = carried[None, :, None] * jnp.einsum("htk,hvk->htv", query, state, precision=highest)
    output = output + jnp.einsum("hts,hsv->htv", scores, weighted, precision=highest)
    closing = (segment == segment[size - 1]).astype(dtype)
    new_state = carried[size - 1] * state + jnp.einsum(
        "hsv,hsk->hvk", weighted * closing[None, :, None], keys, precision=highest
    )
    return ((new_state, segment[size - 1]), output)


def mixer(projected, beta_logit, taps, head_gain, segment):
    length = projected.shape[0]
    heads = beta_logit.shape[1]
    width = taps.shape[-1]
    fields = projected.reshape(length, 3, heads, width)
    mixed = jax.nn.silu(short_conv(fields, taps, segment))
    query = unit_norm(mixed[:, 0]) * width ** (-0.5)
    keys = unit_norm(mixed[:, 1])
    values = mixed[:, 2]
    beta = jax.nn.sigmoid(beta_logit)
    blocks = length // GROUP

    def arrange(array):
        return jnp.transpose(array.reshape(blocks, GROUP, heads, width), (0, 2, 1, 3))

    beta_blocks = jnp.transpose(beta.reshape(blocks, GROUP, heads), (0, 2, 1))
    segment_blocks = segment.reshape(blocks, GROUP)
    start = (jnp.zeros((heads, width, width), projected.dtype), jnp.int32(-1))
    final, outputs = lax.scan(
        jax.checkpoint(delta_block),
        start,
        (arrange(query), arrange(keys), arrange(values), beta_blocks, segment_blocks),
    )
    raw = jnp.transpose(outputs, (0, 2, 1, 3)).reshape(length, heads, width)
    normed = rms_norm(raw, 1e-05) * head_gain
    return normed.reshape(length, heads * width)


def fetch(
    qkv_weight, beta_weight, conv_taps, head_gain, out_weight, gate_weight, up_weight, down_weight
):
    return (
        lax.all_gather(qkv_weight, "dp", axis=0, tiled=True),
        lax.all_gather(beta_weight, "dp", axis=0, tiled=True),
        lax.all_gather(conv_taps, "dp", axis=3, tiled=True),
        lax.all_gather(head_gain, "dp", axis=1, tiled=True),
        lax.all_gather(out_weight, "dp", axis=1, tiled=True),
        lax.all_gather(gate_weight, "dp", axis=0, tiled=True),
        lax.all_gather(up_weight, "dp", axis=0, tiled=True),
        lax.all_gather(down_weight, "dp", axis=1, tiled=True),
    )


def settle(qkv_part, beta_part, taps_part, gain_part, out_part, gate_part, up_part, down_part):
    return (
        lax.psum_scatter(
            qkv_part.astype(jnp.bfloat16), "dp", scatter_dimension=0, tiled=True
        ).astype(jnp.float32),
        lax.psum_scatter(
            beta_part.astype(jnp.bfloat16), "dp", scatter_dimension=0, tiled=True
        ).astype(jnp.float32),
        lax.psum_scatter(
            taps_part.astype(jnp.bfloat16), "dp", scatter_dimension=3, tiled=True
        ).astype(jnp.float32),
        lax.psum_scatter(
            gain_part.astype(jnp.bfloat16), "dp", scatter_dimension=1, tiled=True
        ).astype(jnp.float32),
        lax.psum_scatter(
            out_part.astype(jnp.bfloat16), "dp", scatter_dimension=1, tiled=True
        ).astype(jnp.float32),
        lax.psum_scatter(
            gate_part.astype(jnp.bfloat16), "dp", scatter_dimension=0, tiled=True
        ).astype(jnp.float32),
        lax.psum_scatter(
            up_part.astype(jnp.bfloat16), "dp", scatter_dimension=0, tiled=True
        ).astype(jnp.float32),
        lax.psum_scatter(
            down_part.astype(jnp.bfloat16), "dp", scatter_dimension=1, tiled=True
        ).astype(jnp.float32),
    )


def widened(array, dim, factor):
    shape = list(array.shape)
    shape[dim] = shape[dim] * factor
    return jnp.zeros(tuple(shape), jnp.float32)


def body(
    inputs,
    teacher,
    segment_ids,
    padding,
    attn_gain,
    qkv_weight,
    beta_weight,
    conv_taps,
    head_gain,
    out_weight,
    mlp_gain,
    gate_weight,
    up_weight,
    down_weight,
):
    length = segment_ids.shape[1]
    dp_count = lax.axis_size("dp")
    all_rows = inputs.shape[0] * length * dp_count
    valid = lax.psum(jnp.sum(padding), ("dp", "tensor"))
    scale = all_rows / valid.astype(jnp.float32)
    shards = (
        qkv_weight,
        beta_weight,
        conv_taps,
        head_gain,
        out_weight,
        gate_weight,
        up_weight,
        down_weight,
    )
    gather_dims = (0, 0, 3, 1, 1, 0, 0, 1)
    totals = tuple((widened(weight, dim, dp_count) for weight, dim in zip(shards, gather_dims)))
    zero_gain = jnp.zeros(attn_gain.shape, jnp.float32)

    def micro_step(carry, batch):
        totals, squares, attn_sum, mlp_sum = carry
        tokens, target, segment, mask = batch
        weights_now = fetch(
            qkv_weight,
            beta_weight,
            conv_taps,
            head_gain,
            out_weight,
            gate_weight,
            up_weight,
            down_weight,
        )
        qkv_full, beta_full, taps_full, gain_full, out_full, gate_full, up_full, down_full = (
            weights_now
        )
        tokens32 = tokens.astype(jnp.float32)
        attn_scale = lax.rsqrt(jnp.mean(tokens32 * tokens32, -1, keepdims=True) + 1e-06)
        attn_unit = tokens32 * attn_scale
        normed = (attn_unit * attn_gain).astype(jnp.bfloat16)
        gathered = lax.all_gather(normed, "tensor", axis=0, tiled=True)
        projected = jnp.einsum(
            "sd,dcf->scf", gathered, qkv_full, preferred_element_type=jnp.float32
        )
        beta_logit = jnp.dot(gathered, beta_full, preferred_element_type=jnp.float32)

        def local_mixer(projected_in, beta_in, taps_in, gain_in):
            return mixer(projected_in, beta_in, taps_in, gain_in, segment)

        heads_out, mixer_back = jax.vjp(
            local_mixer,
            projected,
            beta_logit,
            taps_full.astype(jnp.float32),
            gain_full.astype(jnp.float32),
        )
        heads_low = heads_out.astype(jnp.bfloat16)
        attention = lax.psum_scatter(
            jnp.dot(heads_low, out_full, preferred_element_type=jnp.float32).astype(jnp.bfloat16),
            "tensor",
            scatter_dimension=0,
            tiled=True,
        ).astype(jnp.float32)
        hidden = tokens32 + attention
        mlp_scale = lax.rsqrt(jnp.mean(hidden * hidden, -1, keepdims=True) + 1e-06)
        mlp_unit = hidden * mlp_scale
        ffn_in = (mlp_unit * mlp_gain).astype(jnp.bfloat16)
        ffn_all = lax.all_gather(ffn_in, "tensor", axis=0, tiled=True)
        gate = jnp.dot(ffn_all, gate_full, preferred_element_type=jnp.float32)
        up = jnp.dot(ffn_all, up_full, preferred_element_type=jnp.float32)
        sigma = jax.nn.sigmoid(gate)
        act = (gate * sigma * up).astype(jnp.bfloat16)
        output = hidden + lax.psum_scatter(
            jnp.dot(act, down_full, preferred_element_type=jnp.float32).astype(jnp.bfloat16),
            "tensor",
            scatter_dimension=0,
            tiled=True,
        ).astype(jnp.float32)
        diff = output - target.astype(jnp.float32)
        mask32 = mask.astype(jnp.float32)
        squares = squares + jnp.sum(jnp.sum(diff * diff, -1) * mask32)
        block_grad = (scale * mask32)[:, None] * diff
        weights_back = fetch(
            qkv_weight,
            beta_weight,
            conv_taps,
            head_gain,
            out_weight,
            gate_weight,
            up_weight,
            down_weight,
        )
        qkv_back, beta_back, taps_back, gain_back, out_back, gate_back, up_back, down_back = (
            weights_back
        )
        ffn_grad_all = lax.all_gather(block_grad.astype(jnp.bfloat16), "tensor", axis=0, tiled=True)
        down_part = jnp.einsum("sf,sd->fd", act, ffn_grad_all, preferred_element_type=jnp.float32)
        act_grad = jnp.einsum(
            "sd,fd->sf", ffn_grad_all, down_back, preferred_element_type=jnp.float32
        )
        gate_low = (act_grad * up * sigma * (1.0 + gate * (1.0 - sigma))).astype(jnp.bfloat16)
        up_low = (act_grad * gate * sigma).astype(jnp.bfloat16)
        gate_part = jnp.einsum("sd,sf->df", ffn_all, gate_low, preferred_element_type=jnp.float32)
        up_part = jnp.einsum("sd,sf->df", ffn_all, up_low, preferred_element_type=jnp.float32)
        total = jnp.einsum("sf,df->sd", gate_low, gate_back, preferred_element_type=jnp.float32)
        mlp_grad = lax.psum_scatter(
            (
                total + jnp.einsum("sf,df->sd", up_low, up_back, preferred_element_type=jnp.float32)
            ).astype(jnp.bfloat16),
            "tensor",
            scatter_dimension=0,
            tiled=True,
        ).astype(jnp.float32)
        mlp_sum = mlp_sum + jnp.sum(mlp_grad * mlp_unit, 0)
        mlp_inner = mlp_grad * mlp_gain
        hidden_grad = block_grad + mlp_scale * (
            mlp_inner - mlp_unit * jnp.mean(mlp_inner * mlp_unit, -1, keepdims=True)
        )
        attention_all = lax.all_gather(
            hidden_grad.astype(jnp.bfloat16), "tensor", axis=0, tiled=True
        )
        out_part = jnp.einsum(
            "sf,sd->fd", heads_low, attention_all, preferred_element_type=jnp.float32
        )
        heads_grad = jnp.einsum(
            "sd,fd->sf", attention_all, out_back, preferred_element_type=jnp.float32
        )
        projected_grad, beta_logit_grad, taps_part, gain_part = mixer_back(heads_grad)
        projected_low = projected_grad.astype(jnp.bfloat16)
        beta_low = beta_logit_grad.astype(jnp.bfloat16)
        qkv_part = jnp.einsum(
            "sd,scf->dcf", gathered, projected_low, preferred_element_type=jnp.float32
        )
        beta_part = jnp.einsum("sd,sh->dh", gathered, beta_low, preferred_element_type=jnp.float32)
        total = jnp.einsum(
            "scf,dcf->sd", projected_low, qkv_back, preferred_element_type=jnp.float32
        )
        normed_grad = lax.psum_scatter(
            (
                total
                + jnp.einsum("sh,dh->sd", beta_low, beta_back, preferred_element_type=jnp.float32)
            ).astype(jnp.bfloat16),
            "tensor",
            scatter_dimension=0,
            tiled=True,
        ).astype(jnp.float32)
        attn_sum = attn_sum + jnp.sum(normed_grad * attn_unit, 0)
        attn_inner = normed_grad * attn_gain
        input_grad = hidden_grad + attn_scale * (
            attn_inner - attn_unit * jnp.mean(attn_inner * attn_unit, -1, keepdims=True)
        )
        parts = (qkv_part, beta_part, taps_part, gain_part, out_part, gate_part, up_part, down_part)
        totals = tuple((old + new for old, new in zip(totals, parts)))
        return ((totals, squares, attn_sum, mlp_sum), (output.astype(jnp.bfloat16), input_grad))

    start = (totals, jnp.zeros((), jnp.float32), zero_gain, zero_gain)
    finals, outputs = lax.scan(micro_step, start, (inputs, teacher, segment_ids, padding))
    totals, squares, attn_sum, mlp_sum = finals
    block_out, input_grad = outputs
    totals = settle(
        totals[0], totals[1], totals[2], totals[3], totals[4], totals[5], totals[6], totals[7]
    )
    attn_total, mlp_total, square_total = lax.psum((attn_sum, mlp_sum, squares), ("dp", "tensor"))
    loss = square_total / (valid.astype(jnp.float32) * inputs.shape[2])
    return (
        block_out,
        loss,
        input_grad,
        attn_total,
        totals[0],
        totals[1],
        totals[2],
        totals[3],
        totals[4],
        mlp_total,
        totals[5],
        totals[6],
        totals[7],
    )


def solution(mesh):
    in_specs = (
        P("dp", "tensor", None),
        P("dp", "tensor", None),
        P("dp", None),
        P("dp", "tensor"),
        P(),
        P("dp", None, "tensor"),
        P("dp", "tensor"),
        P(None, None, "tensor", "dp"),
        P("tensor", "dp"),
        P("tensor", "dp"),
        P(),
        P("dp", "tensor"),
        P("dp", "tensor"),
        P("tensor", "dp"),
    )
    out_specs = (
        P("dp", "tensor", None),
        P(),
        P("dp", "tensor", None),
        P(),
        P("dp", None, "tensor"),
        P("dp", "tensor"),
        P(None, None, "tensor", "dp"),
        P("tensor", "dp"),
        P("tensor", "dp"),
        P(),
        P("dp", "tensor"),
        P("dp", "tensor"),
        P("tensor", "dp"),
    )
    return jax.shard_map(body, mesh=mesh, in_specs=in_specs, out_specs=out_specs, check_vma=False)
```

profile of v0, /device:TPU:0, one launch (start us, length us, event | category | flops | bytes accessed | tf_op | source)
XLA Modules:
  0.0 3572.0 jit_solution(11940812805327868886)
XLA Ops:
  9.4 68.2 %psum.28 = s32[]{:T(128)} all-reduce(s32[]{:T(128)} %reduce_sum.286), channel_id=1, replica_groups=mesh['dp'=8,'tensor'=16] {'dp','tensor'}, use_global_device_ids=true, to_apply=%region_1.0 | all-reduce | flops 1 | bytes 8 | tf_op jit(solution)/shard_map/psum | solution.py:161
  79.7 2898.0 %while.135 = (s32[]{:T(128)}, f32[2048,3,128]{2,0,1:T(8,128)}, f32[2048,1]{0,1:T(1,128)}, f32[4,3,1,128]{3,2,1,0:T(1,128)}, f32[1,128]{1,0:T(1,128)}, /*index=5*...) while((s32[]{:T(128)}, f32[2048,3,128]{2,0,1:T(8,128)}, ...), condition=%wide.region_32.34_spmd.clone, body=%wide.region_2.33_spmd.clone.sunk | while | flops 20024219648 | bytes 558299264 | solution.py:313
  220.5 276.7 %while.136 = (s32[]{:T(128)}, f32[1,128,128]{2,1,0:T(8,128)S(1)}, s32[]{:T(128)}, f32[16,1,64,128]{3,2,1,0:T(8,128)}, f32[16,1,128,128]{3,2,1,0:T(8,128)}, /*ind...) while((s32[]{:T(128)}, f32[1,128,128]{2,1,0:T(8,128)S(1)}, ...), condition=%wide.region_7.8_spmd.clone, body=%wide.region_6.7_spmd.clone.sunk | while | flops 63140160 | bytes 960217 | solution.py:82
  505.5 63.9 %reduce-scatter.35.cloned.1.call-done = bf16[64,2048]{1,0:T(8,128)(2,1)} async-done(((bf16[1024,2048]{1,0:T(8,128)(2,1)}), bf16[64,2048]{1,0:T(8,128)(2,1)}) %reduce-scatter.35.cloned.1.call-update) | async-done | bytes 262160 | tf_op jit(solution)/shard_map/while/body/eval_jaxpr/reduce_scatter | solution.py:214
  574.1 47.6 %all-gather.15.cloned.1.call-done = bf16[2048,352]{0,1:T(8,128)(2,1)} async-done(((bf16[256,352]{0,1:T(8,128)(2,1)}), bf16[2048,352]{0,1:T(8,128)(2,1)}) %all-gather.15.cloned.1.call-update) | async-done | bytes 1441808 | tf_op jit(solution)/shard_map/while/body/eval_jaxpr/all_gather | solution.py:101
  665.5 48.5 %all-gather.17.cloned.1.call-done = bf16[2048,352]{0,1:T(8,128)(2,1)} async-done(((bf16[256,352]{0,1:T(8,128)(2,1)}), bf16[2048,352]{0,1:T(8,128)(2,1)}) %all-gather.17.cloned.1.call-update) | async-done | bytes 1441808 | tf_op jit(solution)/shard_map/while/body/eval_jaxpr/all_gather | solution.py:102
  720.2 46.5 %all-gather.19.cloned.1.call-done = bf16[352,2048]{1,0:T(8,128)(2,1)} async-done(((bf16[352,256]{1,0:T(8,128)(2,1)}), bf16[352,2048]{1,0:T(8,128)(2,1)}) %all-gather.19.cloned.1.call-update) | async-done | bytes 1441808 | tf_op jit(solution)/shard_map/while/body/eval_jaxpr/all_gather | solution.py:103
  773.4 65.7 %reduce-scatter.37.cloned.1.call-done = bf16[64,2048]{1,0:T(8,128)(2,1)} async-done(((bf16[1024,2048]{1,0:T(8,128)(2,1)}), bf16[64,2048]{1,0:T(8,128)(2,1)}) %reduce-scatter.37.cloned.1.call-update) | async-done | bytes 262160 | tf_op jit(solution)/shard_map/while/body/eval_jaxpr/reduce_scatter | solution.py:229
  890.6 67.3 %reduce-scatter.39.cloned.1.call-done = bf16[64,2048]{1,0:T(8,128)(2,1)} async-done(((bf16[1024,2048]{1,0:T(8,128)(2,1)}), bf16[64,2048]{1,0:T(8,128)(2,1)}) %reduce-scatter.39.cloned.1.call-update) | async-done | bytes 262160 | tf_op jit(solution)/shard_map/while/body/eval_jaxpr/reduce_scatter | solution.py:262
  1007.3 429.0 %while.137 = (s32[]{:T(128)}, f32[1,128,128]{2,1,0:T(8,128)S(1)}, f32[16,1,64,128]{3,2,1,0:T(8,128)}, f32[16,1,64,128]{3,2,1,0:T(8,128)}, f32[16,1,64,128]{3,2,1...) while((s32[]{:T(128)}, f32[1,128,128]{2,1,0:T(8,128)S(1)}, ...), condition=%wide.region_18.19_spmd.clone, body=%wide.region_15.18_spmd.clone.sunk | while | flops 160874752 | bytes 2876935 | solution.py:82
  1669.5 276.7 %while.136 = (s32[]{:T(128)}, f32[1,128,128]{2,1,0:T(8,128)S(1)}, s32[]{:T(128)}, f32[16,1,64,128]{3,2,1,0:T(8,128)}, f32[16,1,128,128]{3,2,1,0:T(8,128)}, /*ind...) while((s32[]{:T(128)}, f32[1,128,128]{2,1,0:T(8,128)S(1)}, ...), condition=%wide.region_7.8_spmd.clone, body=%wide.region_6.7_spmd.clone.sunk | while | flops 63140160 | bytes 960217 | solution.py:82
  1954.4 62.5 %reduce-scatter.35.cloned.1.call-done = bf16[64,2048]{1,0:T(8,128)(2,1)} async-done(((bf16[1024,2048]{1,0:T(8,128)(2,1)}), bf16[64,2048]{1,0:T(8,128)(2,1)}) %reduce-scatter.35.cloned.1.call-update) | async-done | bytes 262160 | tf_op jit(solution)/shard_map/while/body/eval_jaxpr/reduce_scatter | solution.py:214
  2021.8 47.5 %all-gather.15.cloned.1.call-done = bf16[2048,352]{0,1:T(8,128)(2,1)} async-done(((bf16[256,352]{0,1:T(8,128)(2,1)}), bf16[2048,352]{0,1:T(8,128)(2,1)}) %all-gather.15.cloned.1.call-update) | async-done | bytes 1441808 | tf_op jit(solution)/shard_map/while/body/eval_jaxpr/all_gather | solution.py:101
  2113.0 48.5 %all-gather.17.cloned.1.call-done = bf16[2048,352]{0,1:T(8,128)(2,1)} async-done(((bf16[256,352]{0,1:T(8,128)(2,1)}), bf16[2048,352]{0,1:T(8,128)(2,1)}) %all-gather.17.cloned.1.call-update) | async-done | bytes 1441808 | tf_op jit(solution)/shard_map/while/body/eval_jaxpr/all_gather | solution.py:102
  2220.9 65.7 %reduce-scatter.37.cloned.1.call-done = bf16[64,2048]{1,0:T(8,128)(2,1)} async-done(((bf16[1024,2048]{1,0:T(8,128)(2,1)}), bf16[64,2048]{1,0:T(8,128)(2,1)}) %reduce-scatter.37.cloned.1.call-update) | async-done | bytes 262160 | tf_op jit(solution)/shard_map/while/body/eval_jaxpr/reduce_scatter | solution.py:229
  2337.9 67.5 %reduce-scatter.39.cloned.1.call-done = bf16[64,2048]{1,0:T(8,128)(2,1)} async-done(((bf16[1024,2048]{1,0:T(8,128)(2,1)}), bf16[64,2048]{1,0:T(8,128)(2,1)}) %reduce-scatter.39.cloned.1.call-update) | async-done | bytes 262160 | tf_op jit(solution)/shard_map/while/body/eval_jaxpr/reduce_scatter | solution.py:262
  2455.1 429.0 %while.137 = (s32[]{:T(128)}, f32[1,128,128]{2,1,0:T(8,128)S(1)}, f32[16,1,64,128]{3,2,1,0:T(8,128)}, f32[16,1,64,128]{3,2,1,0:T(8,128)}, f32[16,1,64,128]{3,2,1...) while((s32[]{:T(128)}, f32[1,128,128]{2,1,0:T(8,128)S(1)}, ...), condition=%wide.region_18.19_spmd.clone, body=%wide.region_15.18_spmd.clone.sunk | while | flops 160874752 | bytes 2876935 | solution.py:82
  2997.1 66.0 %all-reduce.17 = (f32[]{:T(128)}, f32[2048]{0:T(1024)}, f32[2048]{0:T(1024)}) all-reduce(f32[]{:T(128)} %get-tuple-element.997, f32[2048]{0:T(1024)S(1)} %copy-done.68, f32[2048]{0:T(1024)S(1)} %copy-done.65), channel_id=1, replica_groups=mesh['dp'=8,'tensor'=16] {'dp','tensor'}, use_global_device_ids=true, to_apply=%region_33.35 | all-reduce | flops 4097 | bytes 32776 | tf_op jit(solution)/shard_map/psum | solution.py:319
  3110.2 71.8 %reduce-scatter.29.cloned.1.call-done = bf16[256,1]{1,0:T(8,128)(2,1)} async-done(((bf16[2048,1]{1,0:T(8,128)(2,1)}), bf16[256,1]{1,0:T(8,128)(2,1)}) %reduce-scatter.29.cloned.1.call-update) | async-done | bytes 528
  3183.5 72.5 %reduce-scatter.21.cloned.1.call-done = bf16[128,256]{1,0:T(8,128)(2,1)} async-done(((bf16[128,2048]{1,0:T(8,128)(2,1)}), bf16[128,256]{1,0:T(8,128)(2,1)}) %reduce-scatter.21.cloned.1.call-update) | async-done | bytes 65552 | tf_op jit(solution)/shard_map/reduce_scatter | solution.py:121
  3257.5 74.5 %reduce-scatter.23.cloned.1.call-done = bf16[256,352]{0,1:T(8,128)(2,1)} async-done(((bf16[2048,352]{0,1:T(8,128)(2,1)}), bf16[256,352]{0,1:T(8,128)(2,1)}) %reduce-scatter.23.cloned.1.call-update) | async-done | bytes 180240 | tf_op jit(solution)/shard_map/reduce_scatter | solution.py:124
  3333.7 74.7 %reduce-scatter.25.cloned.1.call-done = bf16[256,352]{0,1:T(8,128)(2,1)} async-done(((bf16[2048,352]{0,1:T(8,128)(2,1)}), bf16[256,352]{0,1:T(8,128)(2,1)}) %reduce-scatter.25.cloned.1.call-update) | async-done | bytes 180240 | tf_op jit(solution)/shard_map/reduce_scatter | solution.py:127
  3410.1 74.2 %reduce-scatter.27.cloned.1.call-done = bf16[352,256]{1,0:T(8,128)(2,1)} async-done(((bf16[352,2048]{1,0:T(8,128)(2,1)}), bf16[352,256]{1,0:T(8,128)(2,1)}) %reduce-scatter.27.cloned.1.call-update) | async-done | bytes 180240 | tf_op jit(solution)/shard_map/reduce_scatter | solution.py:130
  3486.0 75.3 %reduce-scatter.19.cloned.1.call-done = bf16[256,3,128]{2,0,1:T(8,128)(2,1)} async-done(((bf16[2048,3,128]{2,0,1:T(8,128)(2,1)}), bf16[256,3,128]{2,0,1:T(8,128)(2,1)}) %reduce-scatter.19.cloned.1.call-update) | async-done | bytes 196624 | tf_op jit(solution)/shard_map/reduce_scatter | solution.py:109
  (2304 shorter events, 2310.4 us)
Async XLA Ops:
  80.0 121.4 %all-gather.9.cloned.1.call-start = ((), (), s32[]{:S(2)}) async-start(), calls=%async_computation.20 | async-start | bytes 1769472 | tf_op jit(solution)/shard_map/while/body/eval_jaxpr/all_gather | solution.py:96
  80.7 120.7 %all-gather.11.cloned.1.call-start = ((), (), s32[]{:S(2)}) async-start(), calls=%async_computation.21 | async-start | bytes 4456448 | tf_op jit(solution)/shard_map/while/body/eval_jaxpr/all_gather | solution.py:197
  84.3 485.1 %reduce-scatter.35.cloned.1.call-start = ((), (), s32[]{:S(2)}) async-start(), calls=%async_computation.22 | async-start | bytes 4456448 | tf_op jit(solution)/shard_map/while/body/eval_jaxpr/reduce_scatter | solution.py:214
  504.9 116.9 %all-gather.15.cloned.1.call-start = ((), (), s32[]{:S(2)}) async-start(), calls=%async_computation.24 | async-start | bytes 1622016 | tf_op jit(solution)/shard_map/while/body/eval_jaxpr/all_gather | solution.py:101
  505.4 154.6 %all-gather.13.cloned.1.call-start = ((), (), s32[]{:S(2)}) async-start(), calls=%async_computation.23 | async-start | bytes 4456448 | tf_op jit(solution)/shard_map/while/body/eval_jaxpr/all_gather | solution.py:224
  572.5 141.5 %all-gather.17.cloned.1.call-start = ((), (), s32[]{:S(2)}) async-start(), calls=%async_computation.25 | async-start | bytes 1622016 | tf_op jit(solution)/shard_map/while/body/eval_jaxpr/all_gather | solution.py:102
  573.1 193.6 %all-gather.19.cloned.1.call-start = ((), (), s32[]{:S(2)}) async-start(), calls=%async_computation.26 | async-start | bytes 1622016 | tf_op jit(solution)/shard_map/while/body/eval_jaxpr/all_gather | solution.py:103
  573.8 265.3 %reduce-scatter.37.cloned.1.call-start = ((), (), s32[]{:S(2)}) async-start(), calls=%async_computation.27 | async-start | bytes 4456448 | tf_op jit(solution)/shard_map/while/body/eval_jaxpr/reduce_scatter | solution.py:229
  962.5 560.4 %reduce-scatter.41.cloned.1.call-start = ((), (), s32[]{:S(2)}) async-start(), calls=%async_computation.31 | async-start | bytes 4456448 | tf_op jit(solution)/shard_map/while/body/eval_jaxpr/reduce_scatter | solution.py:294
  1526.3 124.0 %all-gather.9.cloned.1.call-start = ((), (), s32[]{:S(2)}) async-start(), calls=%async_computation.20 | async-start | bytes 1769472 | tf_op jit(solution)/shard_map/while/body/eval_jaxpr/all_gather | solution.py:96
  1527.1 123.3 %all-gather.11.cloned.1.call-start = ((), (), s32[]{:S(2)}) async-start(), calls=%async_computation.21 | async-start | bytes 4456448 | tf_op jit(solution)/shard_map/while/body/eval_jaxpr/all_gather | solution.py:197
  1530.7 486.2 %reduce-scatter.35.cloned.1.call-start = ((), (), s32[]{:S(2)}) async-start(), calls=%async_computation.22 | async-start | bytes 4456448 | tf_op jit(solution)/shard_map/while/body/eval_jaxpr/reduce_scatter | solution.py:214
  1954.4 153.2 %all-gather.13.cloned.1.call-start = ((), (), s32[]{:S(2)}) async-start(), calls=%async_computation.23 | async-start | bytes 4456448 | tf_op jit(solution)/shard_map/while/body/eval_jaxpr/all_gather | solution.py:224
  2020.0 141.5 %all-gather.17.cloned.1.call-start = ((), (), s32[]{:S(2)}) async-start(), calls=%async_computation.25 | async-start | bytes 1622016 | tf_op jit(solution)/shard_map/while/body/eval_jaxpr/all_gather | solution.py:102
  2020.6 193.6 %all-gather.19.cloned.1.call-start = ((), (), s32[]{:S(2)}) async-start(), calls=%async_computation.26 | async-start | bytes 1622016 | tf_op jit(solution)/shard_map/while/body/eval_jaxpr/all_gather | solution.py:103
  2021.4 265.3 %reduce-scatter.37.cloned.1.call-start = ((), (), s32[]{:S(2)}) async-start(), calls=%async_computation.27 | async-start | bytes 4456448 | tf_op jit(solution)/shard_map/while/body/eval_jaxpr/reduce_scatter | solution.py:229
  2409.9 560.7 %reduce-scatter.41.cloned.1.call-start = ((), (), s32[]{:S(2)}) async-start(), calls=%async_computation.31 | async-start | bytes 4456448 | tf_op jit(solution)/shard_map/while/body/eval_jaxpr/reduce_scatter | solution.py:294
  2979.3 129.4 %reduce-scatter.31.cloned.1.call-start = ((), (), s32[]{:S(2)}) async-start(), calls=%async_computation.18 | async-start | bytes 36864
  2982.1 200.0 %reduce-scatter.29.cloned.1.call-start = ((), (), s32[]{:S(2)}) async-start(), calls=%async_computation.17 | async-start | bytes 589824
  2983.9 272.1 %reduce-scatter.21.cloned.1.call-start = ((), (), s32[]{:S(2)}) async-start(), calls=%async_computation.13 | async-start | bytes 589824 | tf_op jit(solution)/shard_map/reduce_scatter | solution.py:121
  2984.9 347.2 %reduce-scatter.23.cloned.1.call-start = ((), (), s32[]{:S(2)}) async-start(), calls=%async_computation.14 | async-start | bytes 1622016 | tf_op jit(solution)/shard_map/reduce_scatter | solution.py:124
  2988.1 420.3 %reduce-scatter.25.cloned.1.call-start = ((), (), s32[]{:S(2)}) async-start(), calls=%async_computation.15 | async-start | bytes 1622016 | tf_op jit(solution)/shard_map/reduce_scatter | solution.py:127
  2991.6 492.7 %reduce-scatter.27.cloned.1.call-start = ((), (), s32[]{:S(2)}) async-start(), calls=%async_computation.16 | async-start | bytes 1622016 | tf_op jit(solution)/shard_map/reduce_scatter | solution.py:130
  2993.0 568.2 %reduce-scatter.19.cloned.1.call-start = ((), (), s32[]{:S(2)}) async-start(), calls=%async_computation.12 | async-start | bytes 1769472 | tf_op jit(solution)/shard_map/reduce_scatter | solution.py:109
  (174 other events, 7654.0 us)
Sparse Core Ops, SparseCore 0:
  83.4 47.3 all-gather.8
  133.3 36.9 all-gather.10
  505.0 64.3 reduce-scatter.34
  571.6 50.0 all-gather.14
  624.0 36.0 all-gather.12
  662.4 51.6 all-gather.16
  716.4 50.2 all-gather.18
  772.9 66.1 reduce-scatter.36
  841.5 35.9 all-gather.20
  890.2 67.6 reduce-scatter.38
  962.6 35.8 all-gather.22
  1455.1 67.7 reduce-scatter.40
  1529.8 49.6 all-gather.8
  1581.8 36.8 all-gather.10
  1953.9 62.9 reduce-scatter.34
  2019.2 50.0 all-gather.14
  2071.5 36.0 all-gather.12
  2109.9 51.6 all-gather.16
  2163.9 50.2 all-gather.18
  2220.4 66.1 reduce-scatter.36
  2289.0 35.9 all-gather.20
  2337.8 67.5 reduce-scatter.38
  2410.0 36.1 all-gather.22
  2902.9 67.6 reduce-scatter.40
Sparse Core Ops, SparseCore 1:
  2982.1 60.9 reduce-scatter.32
  3047.2 61.4 reduce-scatter.30
  3112.1 69.9 reduce-scatter.28
  3186.1 69.9 reduce-scatter.20
  3259.8 72.2 reduce-scatter.22
  3336.3 72.1 reduce-scatter.24
  3412.0 72.2 reduce-scatter.26
  3488.4 72.8 reduce-scatter.18
where the time goes:
time: 3600 us; the launch traced here: 3570 us
  waiting for transfers between devices  1470 us (41%)
  other arithmetic  714 us (20%)
  matrix products  617 us (17%)
  blocking collectives  359 us (10%)
  local copies, waits for them, and re-layouts  359 us (10%)
    another operation x224, other arithmetic, delta_block(): jax.scipy.linalg.solve_triangular(matrix, right, lower=True, unit_diagona...  476 us
    reduce_scatter x2, waiting for transfers between devices, micro_step(): lax.psum_scatter((total + jnp.einsum('sf,df->sd', up_low, up_back, prefer...  135 us
    reduce_scatter x2, waiting for transfers between devices, micro_step(): lax.psum_scatter(jnp.dot(act, down_full, preferred_element_type=jnp.float...  131 us
    reduce_scatter x2, waiting for transfers between devices, micro_step(): lax.psum_scatter(jnp.dot(heads_low, out_full, preferred_element_type=jnp....  126 us
    squeeze x160, local copies, waits for them, and re-layouts, mixer(): lax.scan(jax.checkpoint(delta_block), start, (arrange(query), arrange(key...  119 us
    unnamed x11, waiting for transfers between devices  116 us
    dot_general x96, matrix products, delta_block(): jnp.einsum('hsv,hsk->hvk', weighted * closing[None, :, None], keys, preci...  108 us
    all_gather x2, waiting for transfers between devices, fetch(): lax.all_gather(up_weight, 'dp', axis=0, tiled=True)  97 us
  transfers between devices with their start and end apart: 32, of which 27 were waited for; matrix products, arithmetic and copies ran while one was open for 3% of the time, Pallas kernels for 0%

commit v1 on v0

v1 whole, which is shorter than its diff:
```python
import jax
import jax.numpy as jnp
from jax import lax
from jax.experimental import pallas as pl
from jax.experimental.pallas import tpu as pltpu
from jax.sharding import PartitionSpec as P

CHUNK = 128
WIDE = 512
PARAMS = pltpu.CompilerParams(vmem_limit_bytes=56 << 20)


def nn(a, b):
    return jnp.dot(a, b, preferred_element_type=jnp.float32)


def nt(a, b):
    return lax.dot_general(a, b, (((1,), (1,)), ((), ())), preferred_element_type=jnp.float32)


def tn(a, b):
    return lax.dot_general(a, b, (((0,), (0,)), ((), ())), preferred_element_type=jnp.float32)


def low(value):
    return value.astype(jnp.bfloat16)


def split(value):
    high = low(value)
    return high, low(value - high.astype(jnp.float32))


def fine(product, a, b):
    a_high, a_rest = a
    b_high, b_rest = b
    return product(a_high, b_high) + (product(a_high, b_rest) + product(a_rest, b_high))


def grid_masks():
    row = lax.broadcasted_iota(jnp.int32, (CHUNK, CHUNK), 0)
    column = lax.broadcasted_iota(jnp.int32, (CHUNK, CHUNK), 1)
    return row, column


def rows_of(index, sequence):
    first = pl.multiple_of(index * 256 + sequence * 64, 64)
    second = pl.multiple_of(index * 256 + 128 + sequence * 64, 64)
    return first, second


def load(ref, index, sequence, lanes=slice(None)):
    first, second = rows_of(index, sequence)
    return jnp.concatenate([ref[pl.ds(first, 64), lanes], ref[pl.ds(second, 64), lanes]], 0)


def store(ref, index, sequence, value, lanes=slice(None)):
    first, second = rows_of(index, sequence)
    ref[pl.ds(first, 64), lanes] = value[:64]
    ref[pl.ds(second, 64), lanes] = value[64:]


def columns_of(pos_ref, index, sequence):
    line = pos_ref[pl.ds(index * 2 + sequence, 1), :]
    return line, jnp.broadcast_to(line, (CHUNK, CHUNK)).T


def convolve(proj_ref, taps_ref, index, sequence, place):
    fields = slice(0, 384)
    current = load(proj_ref, index, sequence, fields)
    before = pl.multiple_of(jnp.maximum(index * 256 - 128 + sequence * 64 + 56, 0), 8)
    window = jnp.concatenate([proj_ref[pl.ds(before, 8), fields], current], 0)
    total = current * taps_ref[0:1, :]
    moved = [current]
    for offset in range(1, 4):
        keep = (place[:, 0:1] >= offset).astype(jnp.float32)
        shifted = window[8 - offset : 8 - offset + CHUNK] * keep
        moved.append(shifted)
        total = total + shifted * taps_ref[offset : offset + 1, :]
    return total, moved


def activate(total):
    sigma = jax.nn.sigmoid(total)
    act = total * sigma
    query, keys, values = act[:, :128], act[:, 128:256], act[:, 256:]
    query_scale = lax.rsqrt(jnp.sum(query * query, -1, keepdims=True) + 1e-06)
    key_scale = lax.rsqrt(jnp.sum(keys * keys, -1, keepdims=True) + 1e-06)
    return sigma, query * query_scale, query_scale, keys * key_scale, key_scale, values


def inverse(mixing, row, column):
    eye = (row == column).astype(jnp.float32)
    total = eye - jnp.where((row // 2) == (column // 2), mixing, 0.0)
    size = 2
    while size < CHUNK:
        corner = (
            ((row // (2 * size)) == (column // (2 * size)))
            & (((row // size) % 2) == 1)
            & (((column // size) % 2) == 0)
        )
        held = split(total)
        inner = split(fine(nn, held, split(jnp.where(corner, mixing, 0.0))))
        total = total - fine(nn, inner, held)
        size *= 2
    return total


def mixer_forward(
    proj_ref, pos_ref, taps_ref, gain_ref,
    heads_ref, query_ref, key_ref, inv_ref, kc_ref, score_ref, step_ref, state_ref, update_ref, raw_ref,
    free_ref, shift_ref,
):
    row, column = grid_masks()
    depth = row - column

    def prepare(index, carry):
        for sequence in range(2):
            line, place = columns_of(pos_ref, index, sequence)
            total, _ = convolve(proj_ref, taps_ref, index, sequence, place)
            beta = jax.nn.sigmoid(load(proj_ref, index, sequence, slice(384, 512)))
            _, query, _, keys, _, values = activate(total)
            query = query * 128 ** (-0.5)
            last = line[:, 127:128]
            within = (depth >= 0) & (depth.astype(jnp.float32) <= place)
            carried = place > row.astype(jnp.float32)
            closing = (127 - row).astype(jnp.float32) <= last
            gram = fine(nt, split(keys), split(keys * beta))
            solved = low(inverse(jnp.where(within & (depth > 0), gram, 0.0), row, column))
            right = jnp.concatenate([low(jnp.where(carried, keys, 0.0)), low(values)], 1)
            both = nn(solved, right)
            key_low = low(keys)
            query_low = low(query)
            score = jnp.where(within, nt(query_low, key_low), 0.0)
            weight = jnp.where(closing, beta, 0.0)
            ends = tn(key_low, low(jnp.concatenate([weight, weight], 1) * both))
            through = jnp.where((row == column) & (last > 127.0), 1.0, 0.0)
            block = index * 2 + sequence
            store(query_ref, index, sequence, query_low)
            store(key_ref, index, sequence, key_low)
            inv_ref[block] = solved
            kc_ref[block] = low(both[:, :128])
            free_ref[block] = both[:, 128:]
            score_ref[block] = low(score)
            step_ref[block] = low(through - ends[:, :128])
            shift_ref[block] = ends[:, 128:]
        return carry

    lax.fori_loop(0, 8, prepare, 0)

    def advance(index, states):
        new = []
        for sequence in range(2):
            block = index * 2 + sequence
            state_low = low(states[sequence])
            state_ref[block] = state_low
            new.append(nn(step_ref[block], state_low) + shift_ref[block])
        return tuple(new)

    zero = jnp.zeros((CHUNK, CHUNK), jnp.float32)
    states = (zero, zero)
    for index in range(8):
        states = advance(index, states)

    def finish(index, carry):
        for sequence in range(2):
            block = index * 2 + sequence
            _, place = columns_of(pos_ref, index, sequence)
            carried = place > row.astype(jnp.float32)
            beta = jax.nn.sigmoid(load(proj_ref, index, sequence, slice(384, 512)))
            state = state_ref[block]
            update = free_ref[block] - nn(kc_ref[block], state)
            output = jnp.where(carried, nn(load(query_ref, index, sequence), state), 0.0)
            output = output + nn(score_ref[block], low(beta * update))
            scale = lax.rsqrt(jnp.mean(output * output, -1, keepdims=True) + 1e-05)
            update_ref[block] = update
            raw_ref[block] = output
            store(heads_ref, index, sequence, low(output * scale * gain_ref[0:1, :]))
        return carry

    lax.fori_loop(0, 8, finish, 0)


def mixer_backward(
    grad_ref, proj_ref, pos_ref, taps_ref, gain_ref,
    query_ref, key_ref, inv_ref, kc_ref, score_ref, step_ref, state_ref, update_ref, raw_ref,
    out_ref, taps_grad_ref, gain_grad_ref,
    back_ref, pull_ref, flow_ref, enter_ref, pre_ref, place_ref,
):
    row, column = grid_masks()
    depth = row - column
    taps_grad_ref[...] = jnp.zeros_like(taps_grad_ref)
    gain_grad_ref[...] = jnp.zeros_like(gain_grad_ref)

    def prepare(index, carry):
        for sequence in range(2):
            block = index * 2 + sequence
            _, place = columns_of(pos_ref, index, sequence)
            carried = place > row.astype(jnp.float32)
            beta = jax.nn.sigmoid(load(proj_ref, index, sequence, slice(384, 512)))
            grad = load(grad_ref, index, sequence)
            output = raw_ref[block]
            scale = lax.rsqrt(jnp.mean(output * output, -1, keepdims=True) + 1e-05)
            unit = output * scale
            inner = grad * gain_ref[0:1, :]
            gain_grad_ref[0:1, :] += jnp.sum(grad * unit, 0, keepdims=True)
            back = scale * (inner - unit * jnp.mean(inner * unit, -1, keepdims=True))
            back_low = low(back)
            pull = tn(score_ref[block], back_low)
            left = jnp.concatenate([load(query_ref, index, sequence), kc_ref[block]], 0)
            right = jnp.concatenate([jnp.where(carried, back_low, 0.0), low(-beta * pull)], 0)
            enter_ref[block] = tn(left, right)
            back_ref[block] = back_low
            pull_ref[block] = pull
        return carry

    lax.fori_loop(0, 8, prepare, 0)

    def retreat(step, flows):
        index = 7 - step
        new = []
        for sequence in range(2):
            block = index * 2 + sequence
            flow_low = low(flows[sequence])
            flow_ref[block] = flow_low
            new.append(tn(step_ref[block], flow_low) + enter_ref[block])
        return tuple(new)

    zero = jnp.zeros((CHUNK, CHUNK), jnp.float32)
    flows = (zero, zero)
    for step in range(8):
        flows = retreat(step, flows)

    def collect(index, carry):
        for sequence in range(2):
            block = index * 2 + sequence
            line, place = columns_of(pos_ref, index, sequence)
            total, moved = convolve(proj_ref, taps_ref, index, sequence, place)
            sigma, query, query_scale, keys, key_scale, values = activate(total)
            beta = jax.nn.sigmoid(load(proj_ref, index, sequence, slice(384, 512)))
            last = line[:, 127:128]
            within = (depth >= 0) & (depth.astype(jnp.float32) <= place)
            later = (depth < 0) & ((-depth).astype(jnp.float32) <= line)
            carried = place > row.astype(jnp.float32)
            closing = (127 - row).astype(jnp.float32) <= last
            query_low = load(query_ref, index, sequence)
            key_low = load(key_ref, index, sequence)
            update = update_ref[block]
            weighted = beta * update
            flow = flow_ref[block]
            state = state_ref[block]
            back = back_ref[block]
            weight_grad = pull_ref[block] + jnp.where(closing, nn(key_low, flow), 0.0)
            score_grad = low(jnp.where(within, nt(back, low(weighted)), 0.0))
            right_grad = tn(inv_ref[block], low(beta * weight_grad))
            right_low = low(right_grad)
            mixing_grad = jnp.where(later, -nt(low(update), right_low), 0.0)
            gram = nt(key_low, key_low)
            beta_grad = jnp.sum(weight_grad * update + mixing_grad * gram, -1, keepdims=True)
            gram_grad = low(beta * mixing_grad)
            key_grad = nt(
                jnp.concatenate(
                    [low(jnp.where(closing, weighted, 0.0)), low(jnp.where(carried, -right_grad, 0.0))], 1
                ),
                jnp.concatenate([flow, state], 1),
            )
            key_grad = key_grad + tn(
                jnp.concatenate([score_grad, gram_grad], 0), jnp.concatenate([query_low, key_low], 0)
            )
            key_grad = key_grad + nn(gram_grad, key_low)
            query_grad = nt(jnp.where(carried, back, 0.0), state) + nn(score_grad, key_low)
            query_grad = query_grad * 128 ** (-0.5)
            query_act = query_scale * (
                query_grad - query * jnp.sum(query * query_grad, -1, keepdims=True)
            )
            key_act = key_scale * (key_grad - keys * jnp.sum(keys * key_grad, -1, keepdims=True))
            act_grad = jnp.concatenate([query_act, key_act, right_grad], 1)
            pre_grad = act_grad * (sigma * (1.0 + total * (1.0 - sigma)))
            for offset in range(4):
                taps_grad_ref[offset : offset + 1, :] += jnp.sum(
                    pre_grad * moved[offset], 0, keepdims=True
                )
            store(pre_ref, index, sequence, pre_grad)
            store(place_ref, index, sequence, place)
            logit_grad = jnp.where(column == 0, beta_grad * beta * (1.0 - beta), 0.0)
            store(out_ref, index, sequence, low(logit_grad), slice(384, 512))
        return carry

    lax.fori_loop(0, 8, collect, 0)

    def spread(index, carry):
        for sequence in range(2):
            after = pl.multiple_of(jnp.minimum(index * 256 + 256, 1792) + sequence * 64, 64)
            live = jnp.where(index == 7, 0.0, 1.0)
            current = load(pre_ref, index, sequence)
            window = jnp.concatenate([current, pre_ref[pl.ds(after, 8), :] * live], 0)
            place = load(place_ref, index, sequence)
            places = jnp.concatenate([place, place_ref[pl.ds(after, 8), :]], 0)[:, 0:1]
            total = current * taps_ref[0:1, :]
            for offset in range(1, 4):
                masked = window * (places >= offset).astype(jnp.float32)
                total = total + masked[offset : offset + CHUNK] * taps_ref[offset : offset + 1, :]
            store(out_ref, index, sequence, low(total), slice(0, 384))
        return carry

    lax.fori_loop(0, 8, spread, 0)


def saved_shapes():
    rows = jax.ShapeDtypeStruct((2048, CHUNK), jnp.bfloat16)
    small = jax.ShapeDtypeStruct((16, CHUNK, CHUNK), jnp.bfloat16)
    wide = jax.ShapeDtypeStruct((16, CHUNK, CHUNK), jnp.float32)
    return (rows, rows, small, small, small, small, small, wide, wide)


def run_forward(proj, pos, taps, gain):
    heads = jax.ShapeDtypeStruct((2048, CHUNK), jnp.bfloat16)
    return pl.pallas_call(
        mixer_forward,
        out_shape=(heads,) + saved_shapes(),
        in_specs=[pl.BlockSpec(memory_space=pltpu.VMEM)] * 4,
        out_specs=[pl.BlockSpec(memory_space=pltpu.VMEM)] * 10,
        scratch_shapes=[
            pltpu.VMEM((16, CHUNK, CHUNK), jnp.float32),
            pltpu.VMEM((16, CHUNK, CHUNK), jnp.float32),
        ],
        compiler_params=PARAMS,
        cost_estimate=pl.CostEstimate(flops=16 << 30, bytes_accessed=16 << 20, transcendentals=0),
        name="mixer_forward",
    )(proj, pos, taps, gain)


def run_backward(grad, proj, pos, taps, gain, saved):
    return pl.pallas_call(
        mixer_backward,
        out_shape=(
            jax.ShapeDtypeStruct((2048, WIDE), jnp.bfloat16),
            jax.ShapeDtypeStruct((8, 384), jnp.float32),
            jax.ShapeDtypeStruct((8, CHUNK), jnp.float32),
        ),
        in_specs=[pl.BlockSpec(memory_space=pltpu.VMEM)] * 14,
        out_specs=[pl.BlockSpec(memory_space=pltpu.VMEM)] * 3,
        scratch_shapes=[
            pltpu.VMEM((16, CHUNK, CHUNK), jnp.bfloat16),
            pltpu.VMEM((16, CHUNK, CHUNK), jnp.float32),
            pltpu.VMEM((16, CHUNK, CHUNK), jnp.bfloat16),
            pltpu.VMEM((16, CHUNK, CHUNK), jnp.float32),
            pltpu.VMEM((2048, 384), jnp.float32),
            pltpu.VMEM((2048, CHUNK), jnp.float32),
        ],
        compiler_params=PARAMS,
        cost_estimate=pl.CostEstimate(flops=32 << 30, bytes_accessed=16 << 20, transcendentals=0),
        name="mixer_backward",
    )(grad, proj, pos, taps, gain, *saved)


def token_places(segment):
    length = segment.shape[1]
    before = jnp.sum((segment[:, None, :] < segment[:, :, None]).astype(jnp.int32), -1)
    place = jnp.arange(length, dtype=jnp.int32)[None, :] - before
    return jnp.transpose(place.reshape(2, 8, CHUNK), (1, 0, 2)).reshape(16, CHUNK).astype(jnp.float32)


def pad_lanes(array, width):
    return jnp.pad(array, ((0, 0), (0, width - array.shape[1])))


def f32(value):
    return value.astype(jnp.float32)


def body(
    inputs, teacher, segment_ids, padding, attn_gain, qkv_weight, beta_weight, conv_taps, head_gain,
    out_weight, mlp_gain, gate_weight, up_weight, down_weight,
):
    hidden_units = gate_weight.shape[1]
    rows = 128
    features = inputs.shape[2]
    valid = f32(lax.psum(jnp.sum(padding), ("dp", "tensor")))
    scale = 16 * 1024 / valid

    small = jnp.concatenate([conv_taps.reshape(12, 16), head_gain.reshape(1, 16)], 0).reshape(1, 208)
    small = jnp.pad(small, ((0, 7), (0, WIDE - 208)))
    mix_shard = jnp.concatenate(
        [qkv_weight.reshape(256, 384), jnp.broadcast_to(beta_weight, (256, CHUNK))], 1
    )
    mix_all = lax.all_gather(jnp.concatenate([mix_shard, small], 0), "dp", axis=0)
    mix_full = mix_all[:, :256].reshape(2048, WIDE)
    small_all = f32(jnp.transpose(mix_all[:, 256, :208].reshape(8, 13, 16), (1, 0, 2)).reshape(13, CHUNK))
    taps = jnp.pad(small_all[:12].reshape(4, 384), ((0, 4), (0, 0)))
    gain = jnp.pad(small_all[12:], ((0, 7), (0, 0)))

    tokens = f32(inputs.reshape(rows, features))
    attn_scale = lax.rsqrt(jnp.mean(tokens * tokens, -1, keepdims=True) + 1e-06)
    attn_unit = tokens * attn_scale
    normed = (attn_unit * attn_gain).astype(jnp.bfloat16)
    gathered = lax.all_gather(normed, "tensor", axis=0, tiled=True)

    ffn_shard = jnp.concatenate(
        [pad_lanes(gate_weight, 384), pad_lanes(up_weight, 384), pad_lanes(jnp.transpose(down_weight), 384)], 1
    )
    ffn_full = lax.all_gather(ffn_shard, "dp", axis=0, tiled=True)
    gate_up, down_t = ffn_full[:, :768], ffn_full[:, 768:]
    out_all = lax.all_gather(lax.all_gather(jnp.transpose(out_weight), "dp", axis=0, tiled=True), "tensor", axis=1, tiled=True)

    proj = nn(gathered, mix_full)
    pos = token_places(segment_ids)
    heads, *saved = run_forward(proj, pos, taps, gain)
    spread = lax.all_to_all(heads.reshape(16, rows, CHUNK), "tensor", 0, 0, tiled=True)
    heads_rows = jnp.transpose(spread, (1, 0, 2)).reshape(rows, features)
    hidden = tokens + nt(heads_rows, out_all)

    mlp_scale = lax.rsqrt(jnp.mean(hidden * hidden, -1, keepdims=True) + 1e-06)
    mlp_unit = hidden * mlp_scale
    ffn_in = (mlp_unit * mlp_gain).astype(jnp.bfloat16)
    ffn_all = lax.all_gather(ffn_in, "tensor", axis=0, tiled=True)
    both = nn(ffn_all, gate_up)
    gate, up = both[:, :384], both[:, 384:]
    sigma = jax.nn.sigmoid(gate)
    act = (gate * sigma * up).astype(jnp.bfloat16)
    output = hidden + f32(
        lax.psum_scatter(nt(act, down_t).astype(jnp.bfloat16), "tensor", scatter_dimension=0, tiled=True)
    )
    diff = output - f32(teacher.reshape(rows, features))
    mask = f32(padding.reshape(rows, 1))
    squares = jnp.sum(jnp.sum(diff * diff, -1, keepdims=True) * mask)
    block_grad = scale * mask * diff

    ffn_grad_all = lax.all_gather(block_grad.astype(jnp.bfloat16), "tensor", axis=0, tiled=True)
    act_grad = nn(ffn_grad_all, down_t)
    gate_low = (act_grad * up * sigma * (1.0 + gate * (1.0 - sigma))).astype(jnp.bfloat16)
    up_low = (act_grad * gate * sigma).astype(jnp.bfloat16)
    both_low = jnp.concatenate([gate_low, up_low], 1)
    mlp_grad = f32(
        lax.psum_scatter(nt(both_low, gate_up).astype(jnp.bfloat16), "tensor", scatter_dimension=0, tiled=True)
    )
    ffn_part = jnp.concatenate([tn(ffn_all, both_low), tn(ffn_grad_all, act)], 1).astype(jnp.bfloat16)
    ffn_grads = f32(lax.psum_scatter(ffn_part, "dp", scatter_dimension=0, tiled=True))

    mlp_sum = jnp.sum(mlp_grad * mlp_unit, 0)
    mlp_inner = mlp_grad * mlp_gain
    hidden_grad = block_grad + mlp_scale * (
        mlp_inner - mlp_unit * jnp.mean(mlp_inner * mlp_unit, -1, keepdims=True)
    )
    attention_low = hidden_grad.astype(jnp.bfloat16)
    heads_grad_rows = nn(attention_low, out_all).astype(jnp.bfloat16)
    heads_grad = lax.all_to_all(
        jnp.transpose(heads_grad_rows.reshape(rows, 16, CHUNK), (1, 0, 2)), "tensor", 0, 0, tiled=True
    ).reshape(2048, CHUNK)
    attention_all = lax.all_gather(attention_low, "tensor", axis=0, tiled=True)
    out_part = tn(attention_all, heads).astype(jnp.bfloat16)

    proj_low, taps_part, gain_part = run_backward(f32(heads_grad), proj, pos, taps, gain, saved)
    attn_grad = f32(
        lax.psum_scatter(
            nt(proj_low, jnp.where(jnp.arange(WIDE) <= 384, mix_full, 0)).astype(jnp.bfloat16),
            "tensor", scatter_dimension=0, tiled=True,
        )
    )
    mix_part = tn(gathered, proj_low)[:, :385]
    small_part = jnp.concatenate([taps_part[:4].reshape(12, CHUNK), gain_part[:1]], 0)
    small_part = jnp.transpose(small_part.reshape(13, 8, 16), (1, 0, 2)).reshape(8, 208)
    small_part = jnp.pad(small_part, ((0, 0), (0, 48))).reshape(2048, 1)
    mix_part = jnp.concatenate([mix_part, small_part, jnp.zeros((2048, 126), jnp.float32)], 1)
    mix_part = jnp.concatenate([mix_part.astype(jnp.bfloat16), out_part], 1)
    mix_grads = f32(lax.psum_scatter(mix_part, "dp", scatter_dimension=0, tiled=True))

    attn_sum = jnp.sum(attn_grad * attn_unit, 0)
    attn_inner = attn_grad * attn_gain
    input_grad = hidden_grad + attn_scale * (
        attn_inner - attn_unit * jnp.mean(attn_inner * attn_unit, -1, keepdims=True)
    )
    attn_total, mlp_total, square_total = lax.psum((attn_sum, mlp_sum, squares), ("dp", "tensor"))
    loss = square_total / (valid * features)
    small_grad = mix_grads[:208, 385].reshape(13, 16)
    shape = (2, 64, features)
    return (
        output.astype(jnp.bfloat16).reshape(shape),
        loss,
        input_grad.reshape(shape),
        attn_total,
        mix_grads[:, :384].reshape(256, 3, CHUNK),
        mix_grads[:, 384:385],
        small_grad[:12].reshape(4, 3, 1, 16),
        small_grad[12:].reshape(1, 16),
        jnp.transpose(mix_grads[:, 512:]),
        mlp_total,
        ffn_grads[:, :hidden_units],
        ffn_grads[:, 384 : 384 + hidden_units],
        jnp.transpose(ffn_grads[:, 768 : 768 + hidden_units]),
    )


def solution(mesh):
    in_specs = (
        P("dp", "tensor", None),
        P("dp", "tensor", None),
        P("dp", None),
        P("dp", "tensor"),
        P(),
        P("dp", None, "tensor"),
        P("dp", "tensor"),
        P(None, None, "tensor", "dp"),
        P("tensor", "dp"),
        P("tensor", "dp"),
        P(),
        P("dp", "tensor"),
        P("dp", "tensor"),
        P("tensor", "dp"),
    )
    out_specs = (
        P("dp", "tensor", None),
        P(),
        P("dp", "tensor", None),
        P(),
        P("dp", None, "tensor"),
        P("dp", "tensor"),
        P(None, None, "tensor", "dp"),
        P("tensor", "dp"),
        P("tensor", "dp"),
        P(),
        P("dp", "tensor"),
        P("dp", "tensor"),
        P("tensor", "dp"),
    )
    return jax.shard_map(body, mesh=mesh, in_specs=in_specs, out_specs=out_specs, check_vma=False)
```

time: 3600 us -> 976 us (0.27)
  waiting for transfers between devices: 1470 us -> 521 us
  other arithmetic: 714 us -> 28.9 us
  matrix products: 617 us -> 97.9 us
  local copies, waits for them, and re-layouts: 359 us -> 26.4 us
  blocking collectives: 359 us -> 186 us
  Pallas kernels: 0 us -> 75.4 us
    reduce_scatter x13 -> x5, waiting for transfers between devices: 844 us -> 267 us  [the longest x1 95.5 us: body(): lax.psum_scatter(nt(both_low, gate_up).astype(jnp.bfloat16), 'tensor', sc...]
    another operation x264 -> x1, other arithmetic: 479 us -> 0.01 us  [the longest x224 476 us: delta_block(): jax.scipy.linalg.solve_triangular(matrix, right, lower=True, unit_diagona...]
    dot_general x738 -> x12, matrix products: 569 us -> 97.9 us  [the longest x4 35.8 us: nn(): return jnp.dot(a, b, preferred_element_type=jnp.float32)]
    all_gather x16 -> x7, waiting for transfers between devices: 502 us -> 230 us  [the longest x1 59.8 us: body(): ffn_full = lax.all_gather(ffn_shard, 'dp', axis=0, tiled=True)]
    all_gather x6 -> x1, blocking collectives: 179 us -> 38.8 us  [body(): lax.all_gather(jnp.transpose(out_weight), 'dp', axis=0, tiled=True)]
    convert_element_type x126 -> x10, other arithmetic: 141 us -> 12.9 us  [the longest x4 4.06 us: f32(): return value.astype(jnp.float32)]
    squeeze x160 -> x0, local copies, waits for them, and re-layouts: 119 us -> none  [mixer(): lax.scan(jax.checkpoint(delta_block), start, (arrange(query), arrange(key...]
    unnamed x11 -> x12, waiting for transfers between devices: 116 us -> 0.2 us
  transfers between devices with their start and end apart: 32 -> 14, of which waited for: 27 -> 12; matrix products, arithmetic and copies ran while one was open for 3% -> 9% of each run, Pallas kernels for 0% -> 8%
where the time goes in v1:
time: 976 us; the launch traced here: 968 us
  waiting for transfers between devices  521 us (53%)
  blocking collectives  186 us (19%)
  matrix products  97.9 us (10%)
  Pallas kernels  75.4 us (8%)
  other arithmetic  28.9 us (3%)
  local copies, waits for them, and re-layouts  26.4 us (3%)
  between operations  17.4 us (2%)
  starting transfers between devices  13.9 us (1%)
    reduce_scatter x1, waiting for transfers between devices, body(): lax.psum_scatter(nt(both_low, gate_up).astype(jnp.bfloat16), 'tensor', sc...  95.5 us
    reduce_scatter x1, waiting for transfers between devices, body(): lax.psum_scatter(nt(proj_low, jnp.where(jnp.arange(WIDE) <= 384, mix_full...  92.1 us
    psum x1, blocking collectives, body(): lax.psum((attn_sum, mlp_sum, squares), ('dp', 'tensor'))  75.2 us
    psum x1, blocking collectives, body(): valid = f32(lax.psum(jnp.sum(padding), ('dp', 'tensor')))  72.5 us
    all_gather x1, waiting for transfers between devices, body(): ffn_full = lax.all_gather(ffn_shard, 'dp', axis=0, tiled=True)  59.8 us
    all_gather x1, waiting for transfers between devices, body(): lax.all_gather(block_grad.astype(jnp.bfloat16), 'tensor', axis=0, tiled=T...  53.6 us
    all_gather x1, waiting for transfers between devices, body(): ffn_all = lax.all_gather(ffn_in, 'tensor', axis=0, tiled=True)  53 us
    reduce_scatter x1, waiting for transfers between devices, body(): lax.psum_scatter(ffn_part, 'dp', scatter_dimension=0, tiled=True)  50.1 us
  transfers between devices with their start and end apart: 14, of which 12 were waited for; matrix products, arithmetic and copies ran while one was open for 9% of the time, Pallas kernels for 8%

profile of v1, /device:TPU:0, one launch (start us, length us, event | category | flops | bytes accessed | tf_op | source)
XLA Modules:
  0.0 967.7 jit_solution(15461993629027768396)
XLA Ops:
  15.1 38.8 %all_gather.30 = bf16[2048,128]{0,1:T(8,128)(2,1)} all-gather(bf16[256,128]{0,1:T(8,128)(2,1)S(1)} %bitcast.102), channel_id=1, replica_groups=mesh['dp'=8,'tensor'=16] {'dp'}, dimensions={0}, use_global_device_ids=true | all-gather | bytes 589824 | tf_op jit(solution)/shard_map/all_gather | solution.py:404
  56.7 13.8 %all-gather.21.cloned.1.call-done = bf16[2112,512]{1,0:T(8,128)(2,1)} async-done(((bf16[264,512]{1,0:T(8,128)(2,1)}), bf16[2112,512]{1,0:T(8,128)(2,1)}) %all-gather.21.cloned.1.call-update) | async-done | bytes 2162704 | tf_op jit(solution)/shard_map/all_gather | solution.py:387
  74.7 49.3 %all-gather.9.cloned.1.call-done = bf16[2048,2048]{1,0:T(8,128)(2,1)} async-done(((bf16[128,2048]{1,0:T(8,128)(2,1)}), bf16[2048,2048]{1,0:T(8,128)(2,1)}) %all-gather.9.cloned.1.call-update) | async-done | bytes 8388624 | tf_op jit(solution)/shard_map/all_gather | solution.py:397
  124.0 9.5 fusion.40.proj_ref
  133.4 48.3 %mixer_forward.1 = (bf16[2048,128]{1,0:T(8,128)(2,1)}, bf16[2048,128]{1,0:T(8,128)(2,1)}, bf16[2048,128]{1,0:T(8,128)(2,1)}, bf16[16,128,128]{2,1,0:T(8,128)(2,1...) custom-call(f32[2048,512]{1,0:T(8,128)} %fusion.40.proj_ref, ...), custom_call_target="tpu_custom_call" | custom-call | flops 17179869184 | bytes 16777216 | tf_op jit(solution)/shard_map/mixer_forward/pallas_call | solution.py:318
  188.9 10.8 %all-to-all-done = bf16[16,128,128]{1,2,0:T(8,128)(2,1)S(1)} async-done(((bf16[16,128,128]{1,2,0:T(8,128)(2,1)}), bf16[16,128,128]{1,2,0:T(8,128)(2,1)S(1)}, u32[]{:S(2)}, u32[]{:S(2)}) %all-to-all-start) | async-done | bytes 524320 | tf_op jit(solution)/shard_map/all_to_all | solution.py:409
  205.8 59.8 %all-gather.15.cloned.1.call-done = bf16[2048,1152]{0,1:T(8,128)(2,1)} async-done(((bf16[256,1152]{0,1:T(8,128)(2,1)}), bf16[2048,1152]{0,1:T(8,128)(2,1)}) %all-gather.15.cloned.1.call-update) | async-done | bytes 4718608 | tf_op jit(solution)/shard_map/all_gather | solution.py:402
  265.7 53.0 %all-gather.13.cloned.1.call-done = bf16[2048,2048]{1,0:T(8,128)(2,1)} async-done(((bf16[128,2048]{1,0:T(8,128)(2,1)}), bf16[2048,2048]{1,0:T(8,128)(2,1)}) %all-gather.13.cloned.1.call-update) | async-done | bytes 8388624 | tf_op jit(solution)/shard_map/all_gather | solution.py:416
  318.6 10.1 %fusion.1 = f32[2048,768]{0,1:T(8,128)S(1)} fusion(bf16[2048,2048]{1,0:T(8,128)(2,1)} %all-gather.13.cloned.1.call-done, bf16[2048,1152]{0,1:T(8,128)(2,1)} %all-gather.15.cloned.1.call-done), kind=kOutput, calls=%fused_computation.14 | convolution fusion | flops 6442450944 | bytes 17825792 | tf_op jit(solution)/shard_map/dot_general | solution.py:14
  333.6 8.2 convolution_convert_fusion.2
  343.1 72.5 %psum.29 = s32[]{:T(128)} all-reduce(s32[]{:T(128)} %reduce_sum.101), channel_id=1, replica_groups=mesh['dp'=8,'tensor'=16] {'dp','tensor'}, use_global_device_ids=true, to_apply=%region_8.9 | all-reduce | flops 1 | bytes 8 | tf_op jit(solution)/shard_map/psum | solution.py:379
  416.4 23.2 %reduce-scatter.6.cloned.1.call-done = bf16[128,2048]{1,0:T(8,128)(2,1)} async-done(((bf16[2048,2048]{1,0:T(8,128)(2,1)}), bf16[128,2048]{1,0:T(8,128)(2,1)}) %reduce-scatter.6.cloned.1.call-update) | async-done | bytes 524304 | tf_op jit(solution)/shard_map/reduce_scatter | solution.py:422
  442.3 53.6 %all-gather.17.cloned.1.call-done = bf16[2048,2048]{1,0:T(8,128)(2,1)} async-done(((bf16[128,2048]{1,0:T(8,128)(2,1)}), bf16[2048,2048]{1,0:T(8,128)(2,1)}) %all-gather.17.cloned.1.call-update) | async-done | bytes 8388624 | tf_op jit(solution)/shard_map/all_gather | solution.py:429
  495.9 9.8 %multiply_convert_fusion.1 = (bf16[2048,384]{0,1:T(8,128)(2,1)S(1)}, bf16[2048,384]{0,1:T(8,128)(2,1)S(1)}) fusion(f32[2048,768]{0,1:T(8,128)} %copy-done.1, bf16[2048,2048]{1,0:T(8,128)(2,1)} %all-gather.17.cloned.1.call-done, bf16[2048,1152]{0,1:T(8,128)(2,1)} %all-gather.15.cloned.1.call-done), kind=kOutput, calls=%fused_computation.9 | convolution fusion | flops 3231449088 | bytes 19398656 | tf_op jit(solution)/shard_map/dot_general | solution.py:14
  507.3 10.8 %convolution_convert_fusion.1 = bf16[2048,2048]{1,0:T(8,128)(2,1)} fusion(bf16[2048,1152]{0,1:T(8,128)(2,1)} %all-gather.15.cloned.1.call-done, bf16[2048,384]{0,1:T(8,128)(2,1)S(1)} %get-tuple-element.128, bf16[2048,384]{0,1:T(8,128)(2,1)S(1)} %get-tuple-element.127), kind=kOutput, calls=%fused_computation.2 | convolution fusion | flops 6452936704 | bytes 14680064 | tf_op jit(solution)/shard_map/dot_general | solution.py:18
  518.2 95.5 %reduce-scatter.8.cloned.1.call-done = bf16[128,2048]{1,0:T(8,128)(2,1)} async-done(((bf16[2048,2048]{1,0:T(8,128)(2,1)}), bf16[128,2048]{1,0:T(8,128)(2,1)}) %reduce-scatter.8.cloned.1.call-update) | async-done | bytes 524304 | tf_op jit(solution)/shard_map/reduce_scatter | solution.py:435
  625.9 9.1 convolution_convert_fusion.3
  653.2 14.2 %all-to-all-done.1 = bf16[16,128,128]{2,1,0:T(8,128)(2,1)S(1)} async-done(((bf16[16,128,128]{2,1,0:T(8,128)(2,1)}), bf16[16,128,128]{2,1,0:T(8,128)(2,1)S(1)}, u32[]{:S(2)}, u32[]{:S(2)}) %all-to-all-start.1) | async-done | bytes 524320 | tf_op jit(solution)/shard_map/all_to_all | solution.py:447
  668.5 27.1 %mixer_backward.1 = (bf16[2048,512]{1,0:T(8,128)(2,1)}, f32[8,384]{1,0:T(8,128)}, f32[8,128]{1,0:T(8,128)}) custom-call(f32[2048,128]{1,0:T(8,128)} %bitcast_convert_fusion.grad_ref, f32[2048,512]{1,0:T(8,128)} %fusion.40.proj_ref, f32[16,128]{1,0:T(8,128)} %bitcast.106, f32[8,384]{1,0:T(8,128)} %pad.28.taps_ref, f32[8,128]{1,0:T(8,128)} %pad.29.gain_ref, ...), custom_call_target="tpu_custom_call" | custom-call | flops 34359738368 | bytes 16777216 | tf_op jit(solution)/shard_map/mixer_backward/pallas_call | solution.py:334
  695.6 8.4 convolution_convert_fusion
  705.5 8.7 fusion.41
  722.0 50.1 %reduce-scatter.14.cloned.1.call-done = bf16[256,1152]{0,1:T(8,128)(2,1)} async-done(((bf16[2048,1152]{0,1:T(8,128)(2,1)}), bf16[256,1152]{0,1:T(8,128)(2,1)}) %reduce-scatter.14.cloned.1.call-update) | async-done | bytes 589840 | tf_op jit(solution)/shard_map/reduce_scatter | solution.py:438
  776.0 92.1 %reduce-scatter.10.cloned.1.call-done = bf16[128,2048]{1,0:T(8,128)(2,1)} async-done(((bf16[2048,2048]{1,0:T(8,128)(2,1)}), bf16[128,2048]{1,0:T(8,128)(2,1)}) %reduce-scatter.10.cloned.1.call-update) | async-done | bytes 524304 | tf_op jit(solution)/shard_map/reduce_scatter | solution.py:455
  869.6 75.2 %all-reduce.7 = (f32[]{:T(128)}, f32[2048]{0:T(1024)}, f32[2048]{0:T(1024)}) all-reduce(f32[]{:T(128)} %multiply_reduce_fusion.3, f32[2048]{0:T(1024)S(1)} %get-tuple-element.119, f32[2048]{0:T(1024)S(1)} %get-tuple-element.117), channel_id=1, replica_groups=mesh['dp'=8,'tensor'=16] {'dp','tensor'}, use_global_device_ids=true, to_apply=%region_6.7 | all-reduce | flops 4097 | bytes 32776 | tf_op jit(solution)/shard_map/psum | solution.py:473
  (154 shorter events, 98.6 us)
Async XLA Ops:
  7.2 46.8 %copy-start.10 = (bf16[352,256]{1,0:T(8,128)(2,1)S(1)}, bf16[352,256]{1,0:T(8,128)(2,1)}, u32[]{:S(2)}) copy-start(bf16[352,256]{1,0:T(8,128)(2,1)} %param.27) | copy-start | bytes 540676
  7.2 46.8 %copy-start.12 = (bf16[256,352]{0,1:T(8,128)(2,1)S(1)}, bf16[256,352]{0,1:T(8,128)(2,1)}, u32[]{:S(2)}) copy-start(bf16[256,352]{0,1:T(8,128)(2,1)} %param.25) | copy-start | bytes 540676
  7.2 46.8 %copy-start.11 = (bf16[256,352]{0,1:T(8,128)(2,1)S(1)}, bf16[256,352]{0,1:T(8,128)(2,1)}, u32[]{:S(2)}) copy-start(bf16[256,352]{0,1:T(8,128)(2,1)} %param.26) | copy-start | bytes 540676
  7.2 63.3 %all-gather.21.cloned.1.call-start = ((), (), s32[]{:S(2)}) async-start(), calls=%async_computation.18 | async-start | bytes 2433024 | tf_op jit(solution)/shard_map/all_gather | solution.py:387
  11.6 112.4 %all-gather.9.cloned.1.call-start = ((), (), s32[]{:S(2)}) async-start(), calls=%async_computation.7 | async-start | bytes 8912896 | tf_op jit(solution)/shard_map/all_gather | solution.py:397
  15.0 173.8 %all-gather.11.cloned.1.call-start = ((), (), s32[]{:S(2)}) async-start(), calls=%async_computation.8 | async-start | bytes 8912896 | tf_op jit(solution)/shard_map/all_gather | solution.py:404
  53.9 211.7 %all-gather.15.cloned.1.call-start = ((), (), s32[]{:S(2)}) async-start(), calls=%async_computation.10 | async-start | bytes 5308416 | tf_op jit(solution)/shard_map/all_gather | solution.py:402
  72.3 61.1 %copy-start.6 = (bf16[8,256,512]{2,1,0:T(8,128)(2,1)}, bf16[8,256,512]{2,1,0:T(8,128)(2,1)S(1)}, u32[]{:S(2)}) copy-start(bf16[8,256,512]{2,1,0:T(8,128)(2,1)S(1)} %slice.92) | copy-start | bytes 6291460
  133.4 66.2 %copy-start = (bf16[2,64,2048]{2,1,0:T(8,128)(2,1)S(1)}, bf16[2,64,2048]{2,1,0:T(8,128)(2,1)}, u32[]{:S(2)}) copy-start(bf16[2,64,2048]{2,1,0:T(8,128)(2,1)} %param.14) | copy-start | bytes 1572868
  183.8 15.9 %all-to-all-start = ((bf16[16,128,128]{1,2,0:T(8,128)(2,1)}), bf16[16,128,128]{1,2,0:T(8,128)(2,1)S(1)}, u32[]{:S(2)}, u32[]{:S(2)}) async-start(bf16[16,128,128]{1,2,0:T(8,128)(2,1)} %copy.80), calls=%async_computation | async-start | bytes 1048576 | tf_op jit(solution)/shard_map/all_to_all | solution.py:409
  188.8 129.8 %all-gather.13.cloned.1.call-start = ((), (), s32[]{:S(2)}) async-start(), calls=%async_computation.9 | async-start | bytes 8912896 | tf_op jit(solution)/shard_map/all_gather | solution.py:416
  205.5 234.1 %reduce-scatter.6.cloned.1.call-start = ((), (), s32[]{:S(2)}) async-start(), calls=%async_computation.11 | async-start | bytes 8912896 | tf_op jit(solution)/shard_map/reduce_scatter | solution.py:422
  341.8 97.8 %copy-start.3 = (bf16[2,64,2048]{2,1,0:T(8,128)(2,1)S(1)}, bf16[2,64,2048]{2,1,0:T(8,128)(2,1)}, u32[]{:S(2)}) copy-start(bf16[2,64,2048]{2,1,0:T(8,128)(2,1)} %param.15) | copy-start | bytes 1572868
  341.8 154.0 %all-gather.17.cloned.1.call-start = ((), (), s32[]{:S(2)}) async-start(), calls=%async_computation.12 | async-start | bytes 8912896 | tf_op jit(solution)/shard_map/all_gather | solution.py:429
  441.7 172.0 %reduce-scatter.8.cloned.1.call-start = ((), (), s32[]{:S(2)}) async-start(), calls=%async_computation.13 | async-start | bytes 8912896 | tf_op jit(solution)/shard_map/reduce_scatter | solution.py:435
  518.1 95.6 %copy-start.4 = (bf16[128,2048]{1,0:T(8,128)(2,1)S(1)}, bf16[128,2048]{1,0:T(8,128)(2,1)}, u32[]{:S(2)}) copy-start(bf16[128,2048]{1,0:T(8,128)(2,1)} %reduce-scatter.6.cloned.1.call-done) | copy-start | bytes 1572868
  518.2 196.2 %all-gather.19.cloned.1.call-start = ((), (), s32[]{:S(2)}) async-start(), calls=%async_computation.15 | async-start | bytes 8912896 | tf_op jit(solution)/shard_map/all_gather | solution.py:450
  618.2 153.9 %reduce-scatter.14.cloned.1.call-start = ((), (), s32[]{:S(2)}) async-start(), calls=%async_computation.17 | async-start | bytes 5308416 | tf_op jit(solution)/shard_map/reduce_scatter | solution.py:438
  645.9 21.5 %all-to-all-start.1 = ((bf16[16,128,128]{2,1,0:T(8,128)(2,1)}), bf16[16,128,128]{2,1,0:T(8,128)(2,1)S(1)}, u32[]{:S(2)}, u32[]{:S(2)}) async-start(bf16[16,128,128]{2,1,0:T(8,128)(2,1)} %bitcast.86), calls=%async_computation.3 | async-start | bytes 1048576 | tf_op jit(solution)/shard_map/all_to_all | solution.py:447
  653.2 214.9 %reduce-scatter.10.cloned.1.call-start = ((), (), s32[]{:S(2)}) async-start(), calls=%async_computation.14 | async-start | bytes 8912896 | tf_op jit(solution)/shard_map/reduce_scatter | solution.py:455
  704.1 249.4 %reduce-scatter.12.cloned.1.call-start = ((), (), s32[]{:S(2)}) async-start(), calls=%async_computation.16 | async-start | bytes 2949120 | tf_op jit(solution)/shard_map/reduce_scatter | solution.py:466
  722.0 146.1 %copy-start.14 = (f32[2048]{0:T(1024)S(1)}, f32[2048]{0:T(1024)}, u32[]{:S(2)}) copy-start(f32[2048]{0:T(1024)} %param.18) | copy-start | bytes 24580
  722.0 146.1 %copy-start.19 = (f32[128]{0:T(128)S(1)}, f32[128]{0:T(128)}, u32[]{:S(2)}) copy-start(f32[128]{0:T(128)} %copy-done.18) | copy-start | bytes 1540
  722.0 223.4 %copy-start.5 = (f32[128,2048]{1,0:T(8,128)S(1)}, f32[128,2048]{1,0:T(8,128)}, u32[]{:S(2)}) copy-start(f32[128,2048]{1,0:T(8,128)} %get-tuple-element.126) | copy-start | bytes 3145732
  (15 other events, 151.8 us)
Sparse Core Ops, SparseCore 0:
  11.7 58.7 all-gather.20
  72.8 51.1 all-gather.8
  125.7 52.9 all-gather.10
  180.7 84.8 all-gather.14
  267.8 50.7 all-gather.12
  341.9 97.5 reduce-scatter.5
  441.9 53.9 all-gather.16
  518.3 95.3 reduce-scatter.7
  618.3 60.7 all-gather.18
  682.9 89.1 reduce-scatter.13
  774.6 93.3 reduce-scatter.9
  872.3 81.1 reduce-scatter.11

commit v2 on v1

--- a/solution.py
+++ b/solution.py
@@ -5,6 +5,7 @@
 from jax.experimental.pallas import tpu as pltpu
 from jax.sharding import PartitionSpec as P
 
+MESH = pl.DeviceIdType.MESH
 CHUNK = 128
 WIDE = 512
 PARAMS = pltpu.CompilerParams(vmem_limit_bytes=56 << 20)
@@ -354,6 +355,441 @@
     )(grad, proj, pos, taps, gain, *saved)
 
 
+def spot(y, z, core):
+    return (y * 2 + z) * 2 + core
+
+
+class Neighbours:
+    def __init__(self):
+        index = lax.axis_index("tensor")
+        self.core = index % 2
+        self.z = (index // 2) % 2
+        self.y = index // 4
+        up, down, far = (self.y + 1) % 4, (self.y + 3) % 4, (self.y + 2) % 4
+        other = 1 - self.z
+        self.up = spot(up, self.z, self.core)
+        self.down = spot(down, self.z, self.core)
+        self.side = spot(self.y, other, self.core)
+        self.twin = spot(self.y, self.z, 1 - self.core)
+        self.chips = {
+            "own": self.y * 2 + self.z,
+            "side": self.y * 2 + other,
+            "down": down * 2 + self.z,
+            "up": up * 2 + self.z,
+            "downside": down * 2 + other,
+            "upside": up * 2 + other,
+            "far": far * 2 + self.z,
+            "farside": far * 2 + other,
+        }
+
+    def mine(self, name):
+        return self.chips[name] * 2 + self.core
+
+    def twins(self, name):
+        return self.chips[name] * 2 + 1 - self.core
+
+    def chip_at(self, step):
+        quarter = step // 2
+        shift = quarter + quarter // 2 - 2 * (quarter // 3)
+        return ((self.y + shift) % 4) * 2 + (self.z + step % 2) % 2
+
+
+def greet(devices):
+    barrier = pltpu.get_barrier_semaphore()
+    for device in devices:
+        pl.semaphore_signal(barrier, inc=1, device_id=device, device_id_type=MESH)
+    pl.semaphore_wait(barrier, len(devices))
+
+
+def remote(source, target, send_sem, recv_sem, device):
+    return pltpu.make_async_remote_copy(
+        src_ref=source, dst_ref=target, send_sem=send_sem, recv_sem=recv_sem,
+        device_id=device, device_id_type=MESH,
+    )
+
+
+TOP, BOTTOM, WHOLE = pl.ds(0, 64), pl.ds(64, 64), pl.ds(0, 128)
+NAMES = ("own", "side", "down", "up", "downside", "upside", "far", "farside")
+
+
+class Gather:
+    copies = 17
+
+    def __init__(self, near, buffer, sends, receives):
+        self.near, self.buffer, self.sends, self.receives = near, buffer, sends, receives
+
+    def send(self, key, block, rows, device):
+        piece = self.buffer.at[block, rows]
+        copy = remote(piece, piece, self.sends.at[key], self.receives.at[key], {"tensor": device})
+        copy.start()
+
+    def arrive(self, key, block, rows=WHOLE):
+        piece = self.buffer.at[block, rows]
+        remote(
+            piece, piece, self.sends.at[key], self.receives.at[key], {"tensor": self.near.twin}
+        ).wait_recv()
+
+    def to_twin(self, name):
+        self.send(9 + NAMES.index(name), self.near.mine(name), WHOLE, self.near.twin)
+
+    def from_twin(self, name):
+        self.arrive(9 + NAMES.index(name), self.near.twins(name))
+
+    def start(self):
+        near = self.near
+        own = near.mine("own")
+        self.send(1, own, WHOLE, near.up)
+        self.send(2, own, WHOLE, near.down)
+        self.send(0, own, WHOLE, near.side)
+        self.to_twin("own")
+
+    def second(self):
+        near = self.near
+        self.arrive(1, near.mine("down"))
+        self.send(5, near.mine("down"), TOP, near.up)
+        self.arrive(2, near.mine("up"))
+        self.send(6, near.mine("up"), BOTTOM, near.down)
+        self.arrive(0, near.mine("side"))
+        self.send(3, near.mine("side"), WHOLE, near.up)
+        self.send(4, near.mine("side"), WHOLE, near.down)
+        self.to_twin("side")
+        self.to_twin("up")
+        self.to_twin("down")
+
+    def third(self):
+        near = self.near
+        far = near.mine("far")
+        self.arrive(5, far, TOP)
+        self.send(7, far, TOP, near.side)
+        self.arrive(6, far, BOTTOM)
+        self.send(8, far, BOTTOM, near.side)
+        self.to_twin("far")
+
+    def fourth(self):
+        near = self.near
+        self.arrive(4, near.mine("upside"))
+        self.to_twin("upside")
+        self.arrive(3, near.mine("downside"))
+        self.to_twin("downside")
+
+    def fifth(self):
+        far = self.near.mine("farside")
+        self.arrive(7, far, TOP)
+        self.arrive(8, far, BOTTOM)
+        self.to_twin("farside")
+
+    def finish(self):
+        near = self.near
+        names = ("own", "own", "own", "side", "side", "down", "up", "far", "far") + NAMES
+        for key, name in enumerate(names):
+            rows = {5: TOP, 6: BOTTOM, 7: TOP, 8: BOTTOM}.get(key, WHOLE)
+            piece = self.buffer.at[near.mine(name), rows]
+            remote(
+                piece, piece, self.sends.at[key], self.receives.at[key], {"tensor": near.twin}
+            ).wait_send()
+
+    def before(self, step):
+        @pl.when(step == 0)
+        def _():
+            self.from_twin("own")
+
+        @pl.when(step == 1)
+        def _():
+            self.second()
+            self.from_twin("side")
+
+        @pl.when(step == 2)
+        def _():
+            self.from_twin("up")
+
+        @pl.when(step == 3)
+        def _():
+            self.third()
+            self.fourth()
+            self.from_twin("upside")
+
+        @pl.when(step == 4)
+        def _():
+            self.from_twin("down")
+
+        @pl.when(step == 5)
+        def _():
+            self.from_twin("downside")
+
+        @pl.when(step == 6)
+        def _():
+            self.from_twin("far")
+
+        @pl.when(step == 7)
+        def _():
+            self.fifth()
+            self.from_twin("farside")
+
+
+def add_rows(target, sources, count=128):
+    def piece(index, carry):
+        rows = pl.ds(pl.multiple_of(index * 16, 16), 16)
+        total = target[rows].astype(jnp.float32)
+        for source in sources:
+            total = total + source[rows].astype(jnp.float32)
+        target[rows] = total.astype(target.dtype)
+        return carry
+
+    lax.fori_loop(0, count // 16, piece, 0)
+
+
+class Scatter:
+    slots = 8
+    copies = 16
+
+    def __init__(self, near, part, twin_part, slot, sends, receives):
+        self.near, self.part, self.twin_part, self.slot = near, part, twin_part, slot
+        self.sends, self.receives = sends, receives
+
+    def describe(self, key, source, target, device):
+        return remote(source, target, self.sends.at[key], self.receives.at[key], {"tensor": device})
+
+    def twin_copy(self, chip):
+        return self.describe(
+            8 + chip, self.part.at[chip * 2 + 1 - self.near.core], self.twin_part.at[chip], self.near.twin
+        )
+
+    def to_twin(self, chip):
+        self.twin_copy(chip).start()
+
+    def chip_sum(self, name):
+        chip = self.near.chips[name]
+        self.twin_copy(chip).wait_recv()
+        add_rows(self.part.at[chip * 2 + self.near.core], [self.twin_part.at[chip]])
+
+    def outgoing(self):
+        near, part, slot = self.near, self.part, self.slot
+        return (
+            (0, part.at[near.mine("farside")], slot.at[0], near.side),
+            (1, part.at[near.mine("far"), TOP], slot.at[1, TOP], near.down),
+            (2, part.at[near.mine("far"), BOTTOM], slot.at[2, BOTTOM], near.up),
+            (3, part.at[near.mine("downside")], slot.at[3], near.down),
+            (4, part.at[near.mine("upside")], slot.at[4], near.up),
+            (5, part.at[near.mine("down")], slot.at[5], near.down),
+            (6, part.at[near.mine("up")], slot.at[6], near.up),
+            (7, part.at[near.mine("side")], slot.at[7], near.side),
+        )
+
+    def send(self, key):
+        self.describe(*self.outgoing()[key]).start()
+
+    def arrive(self, key):
+        self.describe(*self.outgoing()[key]).wait_recv()
+
+    def first(self):
+        self.chip_sum("farside")
+        self.send(0)
+        self.chip_sum("downside")
+        self.send(3)
+        self.chip_sum("upside")
+        self.send(4)
+        self.chip_sum("far")
+        self.chip_sum("down")
+        self.chip_sum("up")
+        self.chip_sum("side")
+
+    def second(self):
+        near, part, slot = self.near, self.part, self.slot
+        self.arrive(0)
+        add_rows(part.at[near.mine("far")], [slot.at[0]])
+        self.send(1)
+        self.send(2)
+
+    def third(self):
+        near, part, slot = self.near, self.part, self.slot
+        self.arrive(3)
+        self.arrive(4)
+        add_rows(part.at[near.mine("side")], [slot.at[3], slot.at[4]])
+        self.send(7)
+        self.arrive(1)
+        add_rows(part.at[near.mine("down"), TOP], [slot.at[1, TOP]], 64)
+        self.send(5)
+        self.arrive(2)
+        add_rows(part.at[near.mine("up"), BOTTOM], [slot.at[2, BOTTOM]], 64)
+        self.send(6)
+
+    def fourth(self):
+        near = self.near
+        chip = near.chips["own"]
+        self.twin_copy(chip).wait_recv()
+        for key in (7, 5, 6):
+            self.arrive(key)
+        return self.part.at[chip * 2 + near.core], self.twin_part.at[chip]
+
+    def total(self, rows):
+        near = self.near
+        chip = near.chips["own"]
+        value = self.part[chip * 2 + near.core, rows].astype(jnp.float32)
+        value = value + self.twin_part[chip, rows].astype(jnp.float32)
+        for key in (5, 6, 7):
+            value = value + self.slot[key, rows].astype(jnp.float32)
+        return value
+
+    def finish(self):
+        for chip in range(8):
+            self.twin_copy(chip).wait_send()
+        for copy in self.outgoing():
+            self.describe(*copy).wait_send()
+
+
+HIDDEN = 384
+
+
+def sigmoid(value):
+    return 1.0 / (1.0 + jnp.exp(-value))
+
+
+def ffn_kernel(
+    input_ref, hidden_ref, teacher_ref, mask_ref, gate_up_ref, down_ref,
+    block_ref, grad_ref, back_ref, square_ref, weight_ref,
+    tokens, grads, both, act_t, both_t, part, twin_part, slot,
+    gather_send, gather_recv, scatter_send, scatter_recv,
+    again_send, again_recv, return_send, return_recv,
+):
+    near = Neighbours()
+    neighbours = [{"tensor": device} for device in (near.up, near.down, near.side, near.twin)]
+    own = near.mine("own")
+    tokens[own] = input_ref[...]
+    greet(neighbours)
+    gather = Gather(near, tokens, gather_send, gather_recv)
+    gather.start()
+    scatter = Scatter(near, part, twin_part, slot, scatter_send, scatter_recv)
+
+    def rows_at(buffer, chip):
+        return jnp.concatenate([buffer[chip * 2], buffer[chip * 2 + 1]], 0)
+
+    def forward(step, carry):
+        gather.before(step)
+        chip = near.chip_at(step)
+        rows = pl.ds(pl.multiple_of(chip * 256, 256), 256)
+        product = nn(rows_at(tokens, chip), gate_up_ref[...])
+        both[rows, :] = product
+        gate, up = product[:, :HIDDEN], product[:, HIDDEN:]
+        act = low(gate * sigmoid(gate) * up)
+        act_t[:, rows] = act.T
+        partial = low(nt(act, down_ref[...]))
+        part[chip * 2] = partial[:128]
+        part[chip * 2 + 1] = partial[128:]
+        scatter.to_twin(chip)
+        return carry
+
+    lax.fori_loop(0, 8, forward, 0)
+    scatter.first()
+    scatter.second()
+    scatter.third()
+    scatter.fourth()
+
+    def middle(index, squares):
+        rows = pl.ds(pl.multiple_of(index * 16, 16), 16)
+        output = hidden_ref[rows] + scatter.total(rows)
+        block_ref[rows] = low(output)
+        diff = output - teacher_ref[rows].astype(jnp.float32)
+        weight = mask_ref[0, rows, 0:1]
+        grad = mask_ref[1, rows, 0:1] * diff
+        grad_ref[rows] = grad
+        grads[own, rows] = low(grad)
+        return squares + weight * jnp.sum(diff * diff, -1, keepdims=True)
+
+    squares = lax.fori_loop(0, 8, middle, jnp.zeros((16, 1), jnp.float32))
+    square_ref[...] = jnp.broadcast_to(jnp.sum(squares, 0, keepdims=True), (8, 128))
+    gather.finish()
+    scatter.finish()
+
+    again = Gather(near, grads, again_send, again_recv)
+    again.start()
+    back = Scatter(near, part, twin_part, slot, return_send, return_recv)
+
+    def backward(step, carry):
+        again.before(step)
+        chip = near.chip_at(step)
+        rows = pl.ds(pl.multiple_of(chip * 256, 256), 256)
+        act_grad = nn(rows_at(grads, chip), down_ref[...])
+        gate, up = both[rows, :HIDDEN], both[rows, HIDDEN:]
+        sigma = sigmoid(gate)
+        gate_low = low(act_grad * up * sigma * (1.0 + gate * (1.0 - sigma)))
+        up_low = low(act_grad * gate * sigma)
+        both_low = jnp.concatenate([gate_low, up_low], 1)
+        both_t[:, rows] = both_low.T
+        partial = low(nt(both_low, gate_up_ref[...]))
+        part[chip * 2] = partial[:128]
+        part[chip * 2 + 1] = partial[128:]
+        back.to_twin(chip)
+        return carry
+
+    lax.fori_loop(0, 8, backward, 0)
+    back.first()
+
+    def weights(step, carry):
+        @pl.when(step == 2)
+        def _():
+            back.second()
+
+        @pl.when(step == 4)
+        def _():
+            back.third()
+
+        lanes = pl.ds(pl.multiple_of(step * 256, 256), 256)
+        for source, values, first, count in ((both_t, tokens, 0, 2 * HIDDEN), (act_t, grads, 2 * HIDDEN, HIDDEN)):
+            column = values[:, :, lanes].reshape(2048, 256)
+            weight_ref[pl.ds(first, count), lanes] = low(nn(source[...], column))
+        return carry
+
+    lax.fori_loop(0, 8, weights, 0)
+    back.fourth()
+
+    def ending(index, carry):
+        rows = pl.ds(pl.multiple_of(index * 16, 16), 16)
+        back_ref[rows] = back.total(rows)
+        return carry
+
+    lax.fori_loop(0, 8, ending, 0)
+    again.finish()
+    back.finish()
+
+
+def run_ffn(ffn_in, hidden, teacher, mask, gate_up, down_t):
+    rows, features = ffn_in.shape
+    wide = jax.ShapeDtypeStruct((rows, features), jnp.float32)
+    vmem = pl.BlockSpec(memory_space=pltpu.VMEM)
+    semaphores = []
+    for _ in range(2):
+        for count in (Gather.copies, Gather.copies, Scatter.copies, Scatter.copies):
+            semaphores.append(pltpu.SemaphoreType.DMA((count,)))
+    return pl.pallas_call(
+        ffn_kernel,
+        out_shape=(
+            jax.ShapeDtypeStruct((rows, features), jnp.bfloat16),
+            wide,
+            wide,
+            jax.ShapeDtypeStruct((8, 128), jnp.float32),
+            jax.ShapeDtypeStruct((3 * HIDDEN, features), jnp.bfloat16),
+        ),
+        in_specs=[vmem] * 6,
+        out_specs=[vmem] * 5,
+        scratch_shapes=[
+            pltpu.VMEM((16, 128, 2048), jnp.bfloat16),
+            pltpu.VMEM((16, 128, 2048), jnp.bfloat16),
+            pltpu.VMEM((2048, 2 * HIDDEN), jnp.float32),
+            pltpu.VMEM((HIDDEN, 2048), jnp.bfloat16),
+            pltpu.VMEM((2 * HIDDEN, 2048), jnp.bfloat16),
+            pltpu.VMEM((16, 128, 2048), jnp.bfloat16),
+            pltpu.VMEM((8, 128, 2048), jnp.bfloat16),
+            pltpu.VMEM((8, 128, 2048), jnp.bfloat16),
+        ]
+        + semaphores,
+        compiler_params=pltpu.CompilerParams(
+            collective_id=1, has_side_effects=True, vmem_limit_bytes=63 << 20
+        ),
+        cost_estimate=pl.CostEstimate(flops=160 << 30, bytes_accessed=16 << 20, transcendentals=0),
+        name="feed_forward",
+    )(ffn_in, hidden, teacher, mask, gate_up, down_t)
+
+
 def token_places(segment):
     length = segment.shape[1]
     before = jnp.sum((segment[:, None, :] < segment[:, :, None]).astype(jnp.int32), -1)
@@ -413,29 +849,13 @@
     mlp_scale = lax.rsqrt(jnp.mean(hidden * hidden, -1, keepdims=True) + 1e-06)
     mlp_unit = hidden * mlp_scale
     ffn_in = (mlp_unit * mlp_gain).astype(jnp.bfloat16)
-    ffn_all = lax.all_gather(ffn_in, "tensor", axis=0, tiled=True)
-    both = nn(ffn_all, gate_up)
-    gate, up = both[:, :384], both[:, 384:]
-    sigma = jax.nn.sigmoid(gate)
-    act = (gate * sigma * up).astype(jnp.bfloat16)
-    output = hidden + f32(
-        lax.psum_scatter(nt(act, down_t).astype(jnp.bfloat16), "tensor", scatter_dimension=0, tiled=True)
+    mask = f32(padding.reshape(rows, 1))
+    masks = jnp.broadcast_to(jnp.stack([mask, scale * mask]), (2, rows, CHUNK))
+    output, block_grad, mlp_grad, square_tile, ffn_part = run_ffn(
+        ffn_in, hidden, teacher.reshape(rows, features), masks, gate_up, down_t
     )
-    diff = output - f32(teacher.reshape(rows, features))
-    mask = f32(padding.reshape(rows, 1))
-    squares = jnp.sum(jnp.sum(diff * diff, -1, keepdims=True) * mask)
-    block_grad = scale * mask * diff
-
-    ffn_grad_all = lax.all_gather(block_grad.astype(jnp.bfloat16), "tensor", axis=0, tiled=True)
-    act_grad = nn(ffn_grad_all, down_t)
-    gate_low = (act_grad * up * sigma * (1.0 + gate * (1.0 - sigma))).astype(jnp.bfloat16)
-    up_low = (act_grad * gate * sigma).astype(jnp.bfloat16)
-    both_low = jnp.concatenate([gate_low, up_low], 1)
-    mlp_grad = f32(
-        lax.psum_scatter(nt(both_low, gate_up).astype(jnp.bfloat16), "tensor", scatter_dimension=0, tiled=True)
-    )
-    ffn_part = jnp.concatenate([tn(ffn_all, both_low), tn(ffn_grad_all, act)], 1).astype(jnp.bfloat16)
-    ffn_grads = f32(lax.psum_scatter(ffn_part, "dp", scatter_dimension=0, tiled=True))
+    squares = square_tile[0, 0]
+    ffn_grads = f32(lax.psum_scatter(ffn_part, "dp", scatter_dimension=1, tiled=True))
 
     mlp_sum = jnp.sum(mlp_grad * mlp_unit, 0)
     mlp_inner = mlp_grad * mlp_gain
@@ -475,7 +895,7 @@
     small_grad = mix_grads[:208, 385].reshape(13, 16)
     shape = (2, 64, features)
     return (
-        output.astype(jnp.bfloat16).reshape(shape),
+        output.reshape(shape),
         loss,
         input_grad.reshape(shape),
         attn_total,
@@ -485,9 +905,9 @@
         small_grad[12:].reshape(1, 16),
         jnp.transpose(mix_grads[:, 512:]),
         mlp_total,
-        ffn_grads[:, :hidden_units],
-        ffn_grads[:, 384 : 384 + hidden_units],
-        jnp.transpose(ffn_grads[:, 768 : 768 + hidden_units]),
+        jnp.transpose(ffn_grads[:hidden_units]),
+        jnp.transpose(ffn_grads[384 : 384 + hidden_units]),
+        ffn_grads[768 : 768 + hidden_units],
     )
 
 

time: 976 us -> 794 us (0.81)
  waiting for transfers between devices: 521 us -> 244 us
  Pallas kernels: 75.4 us -> 246 us
  matrix products: 97.9 us -> 42.2 us
    pallas_call x0 -> x1, Pallas kernels: none -> 170 us  [run_ffn(): pl.pallas_call(ffn_kernel, out_shape=(jax.ShapeDtypeStruct((rows, feature...]
    all_gather x2 -> x0, waiting for transfers between devices: 107 us -> none  [the longest x1 53.6 us: body(): lax.all_gather(block_grad.astype(jnp.bfloat16), 'tensor', axis=0, tiled=T...]
    reduce_scatter x3 -> x1, waiting for transfers between devices: 169 us -> 67.3 us  [body(): lax.psum_scatter(ffn_part, 'dp', scatter_dimension=1, tiled=True)]
    all_gather x1, waiting for transfers between devices: 59.8 us -> 0.02 us  [body(): ffn_full = lax.all_gather(ffn_shard, 'dp', axis=0, tiled=True)]
    dot_general x4 -> x2, matrix products: 35.8 us -> 15.8 us  [nn(): return jnp.dot(a, b, preferred_element_type=jnp.float32)]
    dot_general x4 -> x2, matrix products: 32.2 us -> 13.2 us  [nt(): lax.dot_general(a, b, (((1,), (1,)), ((), ())), preferred_element_type=jn...]
    dot_general x4 -> x2, matrix products: 29.9 us -> 13.3 us  [tn(): lax.dot_general(a, b, (((0,), (0,)), ((), ())), preferred_element_type=jn...]
    all_to_all x1, waiting for transfers between devices: 10.8 us -> 0.01 us  [body(): lax.all_to_all(heads.reshape(16, rows, CHUNK), 'tensor', 0, 0, tiled=True)]
  transfers between devices with their start and end apart: 14 -> 10, of which waited for: 12 -> 6; matrix products, arithmetic and copies ran while one was open for 9% -> 9% of each run, Pallas kernels for 8% -> 10%
where the time goes in v2:
time: 794 us; the launch traced here: 792 us
  Pallas kernels  246 us (31%)
  waiting for transfers between devices  244 us (31%)
  blocking collectives  181 us (23%)
  matrix products  42.2 us (5%)
  local copies, waits for them, and re-layouts  31.1 us (4%)
  other arithmetic  21.7 us (3%)
  between operations  17.1 us (2%)
  starting transfers between devices  9.14 us (1%)
    pallas_call x1, Pallas kernels, run_ffn(): pl.pallas_call(ffn_kernel, out_shape=(jax.ShapeDtypeStruct((rows, feature...  170 us
    reduce_scatter x1, waiting for transfers between devices, body(): lax.psum_scatter(nt(proj_low, jnp.where(jnp.arange(WIDE) <= 384, mix_full...  92.5 us
    psum x1, blocking collectives, body(): lax.psum((attn_sum, mlp_sum, squares), ('dp', 'tensor'))  74.8 us
    psum x1, blocking collectives, body(): valid = f32(lax.psum(jnp.sum(padding), ('dp', 'tensor')))  67.9 us
    reduce_scatter x1, waiting for transfers between devices, body(): lax.psum_scatter(ffn_part, 'dp', scatter_dimension=1, tiled=True)  67.3 us
    all_gather x1, waiting for transfers between devices, body(): gathered = lax.all_gather(normed, 'tensor', axis=0, tiled=True)  49.3 us
    pallas_call x1, Pallas kernels, run_forward(): pl.pallas_call(mixer_forward, out_shape=(heads,) + saved_shapes(), in_spe...  48.2 us
    all_gather x1, blocking collectives, body(): lax.all_gather(jnp.transpose(out_weight), 'dp', axis=0, tiled=True)  38.4 us
  transfers between devices with their start and end apart: 10, of which 6 were waited for; matrix products, arithmetic and copies ran while one was open for 9% of the time, Pallas kernels for 10%

profile of v2, /device:TPU:0, one launch (start us, length us, event | category | flops | bytes accessed | tf_op | source)
XLA Modules:
  0.0 792.3 jit_solution(12124708794129403429)
XLA Ops:
  15.5 38.4 %all_gather.24 = bf16[2048,128]{0,1:T(8,128)(2,1)} all-gather(bf16[256,128]{0,1:T(8,128)(2,1)S(1)} %bitcast.91), channel_id=1, replica_groups=mesh['dp'=8,'tensor'=16] {'dp'}, dimensions={0}, use_global_device_ids=true | all-gather | bytes 589824 | tf_op jit(solution)/shard_map/all_gather | solution.py:840
  55.8 14.8 %all-gather.15.cloned.1.call-done = bf16[2112,512]{1,0:T(8,128)(2,1)} async-done(((bf16[264,512]{1,0:T(8,128)(2,1)}), bf16[2112,512]{1,0:T(8,128)(2,1)}) %all-gather.15.cloned.1.call-update) | async-done | bytes 2162704 | tf_op jit(solution)/shard_map/all_gather | solution.py:823
  74.7 49.3 %all-gather.7.cloned.1.call-done = bf16[2048,2048]{1,0:T(8,128)(2,1)} async-done(((bf16[128,2048]{1,0:T(8,128)(2,1)}), bf16[2048,2048]{1,0:T(8,128)(2,1)}) %all-gather.7.cloned.1.call-update) | async-done | bytes 8388624 | tf_op jit(solution)/shard_map/all_gather | solution.py:833
  124.0 9.5 %fusion.24.proj_ref = f32[2048,512]{1,0:T(8,128)} fusion(bf16[2048,2048]{1,0:T(8,128)(2,1)} %all-gather.7.cloned.1.call-done, bf16[2048,512]{1,0:T(8,128)(2,1)S(1)} %bitcast.79), kind=kOutput, calls=%fused_computation.69 | convolution fusion | flops 4294967296 | bytes 14680064 | tf_op jit(solution)/shard_map/dot_general | solution.py:15
  133.5 48.2 %mixer_forward.1 = (bf16[2048,128]{1,0:T(8,128)(2,1)}, bf16[2048,128]{1,0:T(8,128)(2,1)}, bf16[2048,128]{1,0:T(8,128)(2,1)}, bf16[16,128,128]{2,1,0:T(8,128)(2,1...) custom-call(f32[2048,512]{1,0:T(8,128)} %fusion.24.proj_ref, ...), custom_call_target="tpu_custom_call" | custom-call | flops 17179869184 | bytes 16777216 | tf_op jit(solution)/shard_map/mixer_forward/pallas_call | solution.py:319
  183.8 5.0 all-to-all-start
  189.5 67.9 %psum.28 = s32[]{:T(128)} all-reduce(s32[]{:T(128)} %get-tuple-element.138), channel_id=1, replica_groups=mesh['dp'=8,'tensor'=16] {'dp','tensor'}, use_global_device_ids=true, to_apply=%region_4.5 | all-reduce | flops 1 | bytes 8 | tf_op jit(solution)/shard_map/psum | solution.py:815
  258.3 3.7 slice.92.gate_up_ref
  262.0 2.8 slice.93.down_ref
  264.8 4.8 multiply_reduce_fusion.2
  272.2 170.4 %feed_forward.1 = (bf16[128,2048]{1,0:T(8,128)(2,1)}, f32[128,2048]{1,0:T(8,128)}, f32[128,2048]{1,0:T(8,128)}, f32[8,128]{1,0:T(8,128)}, bf16[1152,2048]{1,0:T(8,128)(2,1)}) custom-call(bf16[128,2048]{1,0:T(8,128)(2,1)} %multiply_convert_fusion.input_ref, f32[128,2048]{1,0:T(8,128)} %copy-done, bf16[128,2048]{1,0:T(8,128)(2,1)} %bitcast.97, ...), custom_call_target="tpu_custom_call" | custom-call | flops 171798691840 | bytes 16777216 | tf_op jit(solution)/shard_map/feed_forward/pallas_call | solution.py:763
  444.8 2.3 fusion.22
  448.1 6.3 fusion.4
  455.4 3.6 all-to-all-start.1
  459.3 13.9 %all-to-all-done.1 = bf16[16,128,128]{2,1,0:T(8,128)(2,1)S(1)} async-done(((bf16[16,128,128]{2,1,0:T(8,128)(2,1)}), bf16[16,128,128]{2,1,0:T(8,128)(2,1)S(1)}, u32[]{:S(2)}, u32[]{:S(2)}) %all-to-all-start.1) | async-done | bytes 524320 | tf_op jit(solution)/shard_map/all_to_all | solution.py:867
  474.3 27.2 %mixer_backward.1 = (bf16[2048,512]{1,0:T(8,128)(2,1)}, f32[8,384]{1,0:T(8,128)}, f32[8,128]{1,0:T(8,128)}) custom-call(f32[2048,128]{1,0:T(8,128)} %bitcast_convert_fusion.grad_ref, f32[2048,512]{1,0:T(8,128)} %fusion.24.proj_ref, f32[16,128]{1,0:T(8,128)} %bitcast.95, f32[8,384]{1,0:T(8,128)} %pad.28.taps_ref, f32[8,128]{1,0:T(8,128)} %pad.29.gain_ref, ...), custom_call_target="tpu_custom_call" | custom-call | flops 34359738368 | bytes 16777216 | tf_op jit(solution)/shard_map/mixer_backward/pallas_call | solution.py:335
  501.4 8.4 %convolution_convert_fusion = bf16[2048,2048]{1,0:T(8,128)(2,1)} fusion(bf16[2048,512]{1,0:T(8,128)(2,1)} %get-tuple-element.45, bf16[2048,512]{1,0:T(8,128)(2,1)S(1)} %bitcast.80, pred[512]{0:T(512)(128)(4,1)S(1)} %iota_compare_fusion.5), kind=kOutput, calls=%fused_computation.1 | convolution fusion | flops 4300210176 | bytes 12583424 | tf_op jit(solution)/shard_map/dot_general | solution.py:19
  511.2 8.6 %fusion.25 = bf16[2048,512]{0,1:T(8,128)(2,1)S(1)} fusion(bf16[2048,2048]{1,0:T(8,128)(2,1)} %all-gather.7.cloned.1.call-done, bf16[2048,512]{1,0:T(8,128)(2,1)} %get-tuple-element.45), kind=kOutput, calls=%fused_computation.70 | convolution fusion | flops 4294967296 | bytes 12582912 | tf_op jit(solution)/shard_map/dot_general | solution.py:23
  520.8 4.7 convolution_convert_fusion.1
  528.8 67.3 %reduce-scatter.8.cloned.1.call-done = bf16[1152,256]{1,0:T(8,128)(2,1)} async-done(((bf16[1152,2048]{1,0:T(8,128)(2,1)}), bf16[1152,256]{1,0:T(8,128)(2,1)}) %reduce-scatter.8.cloned.1.call-update) | async-done | bytes 589840 | tf_op jit(solution)/shard_map/reduce_scatter | solution.py:858
  599.9 92.5 %reduce-scatter.4.cloned.1.call-done = bf16[128,2048]{1,0:T(8,128)(2,1)} async-done(((bf16[2048,2048]{1,0:T(8,128)(2,1)}), bf16[128,2048]{1,0:T(8,128)(2,1)}) %reduce-scatter.4.cloned.1.call-update) | async-done | bytes 524304 | tf_op jit(solution)/shard_map/reduce_scatter | solution.py:875
  693.9 74.8 %all-reduce.7 = (f32[]{:T(128)}, f32[2048]{0:T(1024)}, f32[2048]{0:T(1024)}) all-reduce(f32[]{:T(128)} %bitcast.15, f32[2048]{0:T(1024)S(1)} %get-tuple-element.129, f32[2048]{0:T(1024)S(1)} %get-tuple-element.127), channel_id=1, replica_groups=mesh['dp'=8,'tensor'=16] {'dp','tensor'}, use_global_device_ids=true, to_apply=%region_5.6 | all-reduce | flops 4097 | bytes 32776 | tf_op jit(solution)/shard_map/psum | solution.py:893
  769.4 2.5 fusion.11
  771.9 5.6 reduce-scatter.6.cloned.1.call-done
  (142 shorter events, 42.7 us)
Async XLA Ops:
  7.2 6.8 copy-start.10
  7.2 7.0 copy-start.11
  7.2 7.1 copy-start.12
  7.2 63.3 %all-gather.15.cloned.1.call-start = ((), (), s32[]{:S(2)}) async-start(), calls=%async_computation.12 | async-start | bytes 2433024 | tf_op jit(solution)/shard_map/all_gather | solution.py:823
  11.6 112.5 %all-gather.7.cloned.1.call-start = ((), (), s32[]{:S(2)}) async-start(), calls=%async_computation.5 | async-start | bytes 8912896 | tf_op jit(solution)/shard_map/all_gather | solution.py:833
  12.9 41.1 %copy-start.19 = (f32[128]{0:T(128)}, f32[128]{0:T(128)S(1)}, u32[]{:S(2)}) copy-start(f32[128]{0:T(128)S(1)} %rsqrt.20) | copy-start | bytes 1540
  12.9 41.1 %copy-start.18 = (s32[2,1024]{1,0:T(2,128)S(1)}, s32[2,1024]{1,0:T(2,128)}, u32[]{:S(2)}) copy-start(s32[2,1024]{1,0:T(2,128)} %param.16) | copy-start | bytes 24580
  14.0 244.3 %all-gather.11.cloned.1.call-start = ((), (), s32[]{:S(2)}) async-start(), calls=%async_computation.7 | async-start | bytes 5308416 | tf_op jit(solution)/shard_map/all_gather | solution.py:838
  15.5 249.3 %all-gather.9.cloned.1.call-start = ((), (), s32[]{:S(2)}) async-start(), calls=%async_computation.6 | async-start | bytes 8912896 | tf_op jit(solution)/shard_map/all_gather | solution.py:840
  72.4 61.1 %copy-start.6 = (bf16[8,256,512]{2,1,0:T(8,128)(2,1)}, bf16[8,256,512]{2,1,0:T(8,128)(2,1)S(1)}, u32[]{:S(2)}) copy-start(bf16[8,256,512]{2,1,0:T(8,128)(2,1)S(1)} %slice.88) | copy-start | bytes 6291460
  133.5 55.4 %copy-start.24 = (s32[2,64]{1,0:T(2,128)S(1)}, s32[2,64]{1,0:T(2,128)}, u32[]{:S(2)}) copy-start(s32[2,64]{1,0:T(2,128)} %param.17) | copy-start | bytes 1540
  183.8 80.9 %all-to-all-start = ((bf16[16,128,128]{1,2,0:T(8,128)(2,1)}), bf16[16,128,128]{1,2,0:T(8,128)(2,1)S(1)}, u32[]{:S(2)}, u32[]{:S(2)}) async-start(bf16[16,128,128]{1,2,0:T(8,128)(2,1)} %copy.95), calls=%async_computation | async-start | bytes 1048576 | tf_op jit(solution)/shard_map/all_to_all | solution.py:845
  188.8 331.0 %all-gather.13.cloned.1.call-start = ((), (), s32[]{:S(2)}) async-start(), calls=%async_computation.9 | async-start | bytes 8912896 | tf_op jit(solution)/shard_map/all_gather | solution.py:870
  272.2 170.4 %copy-start.16 = (f32[2048]{0:T(1024)S(1)}, f32[2048]{0:T(1024)}, u32[]{:S(2)}) copy-start(f32[2048]{0:T(1024)} %param.24) | copy-start | bytes 24580
  272.2 170.4 %copy-start.22 = (f32[128]{0:T(128)S(1)}, f32[128]{0:T(128)}, u32[]{:S(2)}) copy-start(f32[128]{0:T(128)} %copy-done.21) | copy-start | bytes 1540
  447.1 149.0 %reduce-scatter.8.cloned.1.call-start = ((), (), s32[]{:S(2)}) async-start(), calls=%async_computation.11 | async-start | bytes 5308416 | tf_op jit(solution)/shard_map/reduce_scatter | solution.py:858
  455.4 17.8 %all-to-all-start.1 = ((bf16[16,128,128]{2,1,0:T(8,128)(2,1)}), bf16[16,128,128]{2,1,0:T(8,128)(2,1)S(1)}, u32[]{:S(2)}, u32[]{:S(2)}) async-start(bf16[16,128,128]{2,1,0:T(8,128)(2,1)} %bitcast.75), calls=%async_computation.1 | async-start | bytes 1048576 | tf_op jit(solution)/shard_map/all_to_all | solution.py:867
  459.0 233.4 %reduce-scatter.4.cloned.1.call-start = ((), (), s32[]{:S(2)}) async-start(), calls=%async_computation.8 | async-start | bytes 8912896 | tf_op jit(solution)/shard_map/reduce_scatter | solution.py:875
  474.3 27.2 %copy-start.7 = (bf16[8,256,512]{2,1,0:T(8,128)(2,1)S(1)}, bf16[8,256,512]{2,1,0:T(8,128)(2,1)}, u32[]{:S(2)}) copy-start(bf16[8,256,512]{2,1,0:T(8,128)(2,1)} %copy-done.6) | copy-start | bytes 6291460
  509.9 267.6 %reduce-scatter.6.cloned.1.call-start = ((), (), s32[]{:S(2)}) async-start(), calls=%async_computation.10 | async-start | bytes 2949120 | tf_op jit(solution)/shard_map/reduce_scatter | solution.py:886
  527.5 164.9 %copy-start.3 = (bf16[2,64,2048]{2,1,0:T(8,128)(2,1)S(1)}, bf16[2,64,2048]{2,1,0:T(8,128)(2,1)}, u32[]{:S(2)}) copy-start(bf16[2,64,2048]{2,1,0:T(8,128)(2,1)} %param.14) | copy-start | bytes 1572868
  527.5 164.9 %copy-start.14 = (f32[2048]{0:T(1024)S(1)}, f32[2048]{0:T(1024)}, u32[]{:S(2)}) copy-start(f32[2048]{0:T(1024)} %param.18) | copy-start | bytes 24580
  527.5 164.9 %copy-start.20 = (f32[128]{0:T(128)S(1)}, f32[128]{0:T(128)}, u32[]{:S(2)}) copy-start(f32[128]{0:T(128)} %copy-done.19) | copy-start | bytes 1540
  769.4 14.2 %copy-start.8 = (bf16[128,2048]{1,0:T(8,128)(2,1)S(1)}, bf16[128,2048]{1,0:T(8,128)(2,1)}, u32[]{:S(2)}) copy-start(bf16[128,2048]{1,0:T(8,128)(2,1)} %get-tuple-element.32) | copy-start | bytes 1572868
  (11 other events, 32.2 us)
Sparse Core Ops, SparseCore 0:
  11.7 58.8 all-gather.14
  72.9 51.1 all-gather.6
  126.3 77.2 all-gather.10
  205.2 50.5 all-gather.8
  447.2 55.8 all-gather.12
  507.0 89.0 reduce-scatter.7
  598.7 93.6 reduce-scatter.3
  696.7 80.6 reduce-scatter.5

commit v3 on v2

--- a/solution.py
+++ b/solution.py
@@ -8,6 +8,8 @@
 MESH = pl.DeviceIdType.MESH
 CHUNK = 128
 WIDE = 512
+GROUPED = 4
+PAIRED = 2
 PARAMS = pltpu.CompilerParams(vmem_limit_bytes=56 << 20)
 
 
@@ -90,9 +92,10 @@
     return sigma, query * query_scale, query_scale, keys * key_scale, key_scale, values
 
 
-def inverse(mixing, row, column):
+def inverses(mixings, row, column):
     eye = (row == column).astype(jnp.float32)
-    total = eye - jnp.where((row // 2) == (column // 2), mixing, 0.0)
+    pair = (row // 2) == (column // 2)
+    totals = [eye - jnp.where(pair, mixing, 0.0) for mixing in mixings]
     size = 2
     while size < CHUNK:
         corner = (
@@ -100,54 +103,72 @@
             & (((row // size) % 2) == 1)
             & (((column // size) % 2) == 0)
         )
-        held = split(total)
-        inner = split(fine(nn, held, split(jnp.where(corner, mixing, 0.0))))
-        total = total - fine(nn, inner, held)
+        corners = [low(jnp.where(corner, mixing, 0.0)) for mixing in mixings]
+        helds = [low(total) for total in totals]
+        inners = [low(nn(held, part)) for held, part in zip(helds, corners)]
+        totals = [total - nn(inner, held) for total, inner, held in zip(totals, inners, helds)]
         size *= 2
-    return total
+    helds = [split(total) for total in totals]
+    rests = [
+        low(eye - total - fine(nn, split(mixing), held))
+        for total, mixing, held in zip(totals, mixings, helds)
+    ]
+    return [total + nn(held[0], rest) for total, held, rest in zip(totals, helds, rests)]
 
 
 def mixer_forward(
     proj_ref, pos_ref, taps_ref, gain_ref,
     heads_ref, query_ref, key_ref, inv_ref, kc_ref, score_ref, step_ref, state_ref, update_ref, raw_ref,
-    free_ref, shift_ref,
+    free_ref, shift_ref, after_prepare, after_advance,
 ):
     row, column = grid_masks()
     depth = row - column
 
-    def prepare(index, carry):
-        for sequence in range(2):
+    def prepare(double, carry):
+        streams = [(double * GROUPED + item // 2, item % 2) for item in range(2 * GROUPED)]
+        lines, queries, keys_all, values_all, betas, withins, carrieds, mixings = ([] for _ in range(8))
+        for index, sequence in streams:
             line, place = columns_of(pos_ref, index, sequence)
             total, _ = convolve(proj_ref, taps_ref, index, sequence, place)
-            beta = jax.nn.sigmoid(load(proj_ref, index, sequence, slice(384, 512)))
             _, query, _, keys, _, values = activate(total)
-            query = query * 128 ** (-0.5)
-            last = line[:, 127:128]
-            within = (depth >= 0) & (depth.astype(jnp.float32) <= place)
-            carried = place > row.astype(jnp.float32)
-            closing = (127 - row).astype(jnp.float32) <= last
-            gram = fine(nt, split(keys), split(keys * beta))
-            solved = low(inverse(jnp.where(within & (depth > 0), gram, 0.0), row, column))
-            right = jnp.concatenate([low(jnp.where(carried, keys, 0.0)), low(values)], 1)
-            both = nn(solved, right)
-            key_low = low(keys)
-            query_low = low(query)
-            score = jnp.where(within, nt(query_low, key_low), 0.0)
-            weight = jnp.where(closing, beta, 0.0)
-            ends = tn(key_low, low(jnp.concatenate([weight, weight], 1) * both))
-            through = jnp.where((row == column) & (last > 127.0), 1.0, 0.0)
+            lines.append(line[:, 127:128])
+            queries.append(low(query * 128 ** (-0.5)))
+            keys_all.append(keys)
+            values_all.append(low(values))
+            betas.append(jax.nn.sigmoid(load(proj_ref, index, sequence, slice(384, 512))))
+            withins.append((depth >= 0) & (depth.astype(jnp.float32) <= place))
+            carrieds.append(place > row.astype(jnp.float32))
+        grams = [fine(nt, split(keys), split(keys * beta)) for keys, beta in zip(keys_all, betas)]
+        mixings = [jnp.where(within & (depth > 0), gram, 0.0) for within, gram in zip(withins, grams)]
+        solved_all = [low(solved) for solved in inverses(mixings, row, column)]
+        boths = [
+            nn(solved, jnp.concatenate([low(jnp.where(carried, keys, 0.0)), values], 1))
+            for solved, carried, keys, values in zip(solved_all, carrieds, keys_all, values_all)
+        ]
+        key_lows = [low(keys) for keys in keys_all]
+        scores = [nt(query, key_low) for query, key_low in zip(queries, key_lows)]
+        weights = [
+            jnp.where((127 - row).astype(jnp.float32) <= last, beta, 0.0)
+            for last, beta in zip(lines, betas)
+        ]
+        ends_all = [
+            tn(key_low, low(jnp.concatenate([weight, weight], 1) * both))
+            for key_low, weight, both in zip(key_lows, weights, boths)
+        ]
+        for item, (index, sequence) in enumerate(streams):
             block = index * 2 + sequence
-            store(query_ref, index, sequence, query_low)
-            store(key_ref, index, sequence, key_low)
-            inv_ref[block] = solved
-            kc_ref[block] = low(both[:, :128])
-            free_ref[block] = both[:, 128:]
-            score_ref[block] = low(score)
-            step_ref[block] = low(through - ends[:, :128])
-            shift_ref[block] = ends[:, 128:]
+            through = jnp.where((row == column) & (lines[item] > 127.0), 1.0, 0.0)
+            store(query_ref, index, sequence, queries[item])
+            store(key_ref, index, sequence, key_lows[item])
+            inv_ref[block] = solved_all[item]
+            kc_ref[block] = low(boths[item][:, :128])
+            free_ref[block] = boths[item][:, 128:]
+            score_ref[block] = low(jnp.where(withins[item], scores[item], 0.0))
+            step_ref[block] = low(through - ends_all[item][:, :128])
+            shift_ref[block] = ends_all[item][:, 128:]
         return carry
 
-    lax.fori_loop(0, 8, prepare, 0)
+    lax.fori_loop(0, 8 // GROUPED, prepare, 0)
 
     def advance(index, states):
         new = []
@@ -159,63 +180,80 @@
         return tuple(new)
 
     zero = jnp.zeros((CHUNK, CHUNK), jnp.float32)
+    after_prepare()
     states = (zero, zero)
     for index in range(8):
         states = advance(index, states)
-
-    def finish(index, carry):
-        for sequence in range(2):
-            block = index * 2 + sequence
+    after_advance()
+
+    def finish(double, carry):
+        streams = [(double * GROUPED + item // 2, item % 2) for item in range(2 * GROUPED)]
+        blocks = [index * 2 + sequence for index, sequence in streams]
+        states = [state_ref[block] for block in blocks]
+        recalls = [nn(kc_ref[block], state) for block, state in zip(blocks, states)]
+        reads = [nn(load(query_ref, *stream), state) for stream, state in zip(streams, states)]
+        updates = [free_ref[block] - recall for block, recall in zip(blocks, recalls)]
+        weighted = [
+            low(jax.nn.sigmoid(load(proj_ref, *stream, slice(384, 512))) * update)
+            for stream, update in zip(streams, updates)
+        ]
+        mixed = [nn(score_ref[block], weight) for block, weight in zip(blocks, weighted)]
+        for item, (index, sequence) in enumerate(streams):
             _, place = columns_of(pos_ref, index, sequence)
-            carried = place > row.astype(jnp.float32)
-            beta = jax.nn.sigmoid(load(proj_ref, index, sequence, slice(384, 512)))
-            state = state_ref[block]
-            update = free_ref[block] - nn(kc_ref[block], state)
-            output = jnp.where(carried, nn(load(query_ref, index, sequence), state), 0.0)
-            output = output + nn(score_ref[block], low(beta * update))
+            output = jnp.where(place > row.astype(jnp.float32), reads[item], 0.0) + mixed[item]
             scale = lax.rsqrt(jnp.mean(output * output, -1, keepdims=True) + 1e-05)
-            update_ref[block] = update
-            raw_ref[block] = output
+            update_ref[blocks[item]] = low(updates[item])
+            raw_ref[blocks[item]] = output
             store(heads_ref, index, sequence, low(output * scale * gain_ref[0:1, :]))
         return carry
 
-    lax.fori_loop(0, 8, finish, 0)
+    lax.fori_loop(0, 8 // GROUPED, finish, 0)
 
 
 def mixer_backward(
     grad_ref, proj_ref, pos_ref, taps_ref, gain_ref,
     query_ref, key_ref, inv_ref, kc_ref, score_ref, step_ref, state_ref, update_ref, raw_ref,
     out_ref, taps_grad_ref, gain_grad_ref,
-    back_ref, pull_ref, flow_ref, enter_ref, pre_ref, place_ref,
+    back_ref, pull_ref, flow_ref, enter_ref, pre_ref, after_prepare, after_collect,
 ):
     row, column = grid_masks()
     depth = row - column
     taps_grad_ref[...] = jnp.zeros_like(taps_grad_ref)
     gain_grad_ref[...] = jnp.zeros_like(gain_grad_ref)
 
-    def prepare(index, carry):
-        for sequence in range(2):
-            block = index * 2 + sequence
-            _, place = columns_of(pos_ref, index, sequence)
-            carried = place > row.astype(jnp.float32)
-            beta = jax.nn.sigmoid(load(proj_ref, index, sequence, slice(384, 512)))
-            grad = load(grad_ref, index, sequence)
+    def prepare(double, carry):
+        streams = [(double * GROUPED + item // 2, item % 2) for item in range(2 * GROUPED)]
+        blocks = [index * 2 + sequence for index, sequence in streams]
+        back_lows = []
+        for (index, sequence), block in zip(streams, blocks):
+            grad = load(grad_ref, index, sequence).astype(jnp.float32)
             output = raw_ref[block]
             scale = lax.rsqrt(jnp.mean(output * output, -1, keepdims=True) + 1e-05)
             unit = output * scale
             inner = grad * gain_ref[0:1, :]
             gain_grad_ref[0:1, :] += jnp.sum(grad * unit, 0, keepdims=True)
             back = scale * (inner - unit * jnp.mean(inner * unit, -1, keepdims=True))
-            back_low = low(back)
-            pull = tn(score_ref[block], back_low)
-            left = jnp.concatenate([load(query_ref, index, sequence), kc_ref[block]], 0)
-            right = jnp.concatenate([jnp.where(carried, back_low, 0.0), low(-beta * pull)], 0)
-            enter_ref[block] = tn(left, right)
+            back_lows.append(low(back))
+        pulls = [tn(score_ref[block], back_low) for block, back_low in zip(blocks, back_lows)]
+        rights = []
+        for (index, sequence), back_low, pull in zip(streams, back_lows, pulls):
+            _, place = columns_of(pos_ref, index, sequence)
+            carried = place > row.astype(jnp.float32)
+            beta = jax.nn.sigmoid(load(proj_ref, index, sequence, slice(384, 512)))
+            rights.append(
+                jnp.concatenate([jnp.where(carried, back_low, 0.0), low(-beta * pull)], 0)
+            )
+        enters = [
+            tn(jnp.concatenate([load(query_ref, *stream), kc_ref[block]], 0), right)
+            for stream, block, right in zip(streams, blocks, rights)
+        ]
+        for block, back_low, pull, enter in zip(blocks, back_lows, pulls, enters):
+            enter_ref[block] = enter
             back_ref[block] = back_low
             pull_ref[block] = pull
         return carry
 
-    lax.fori_loop(0, 8, prepare, 0)
+    lax.fori_loop(0, 8 // GROUPED, prepare, 0)
 
     def retreat(step, flows):
         index = 7 - step
@@ -228,66 +266,101 @@
         return tuple(new)
 
     zero = jnp.zeros((CHUNK, CHUNK), jnp.float32)
+    after_prepare()
     flows = (zero, zero)
     for step in range(8):
         flows = retreat(step, flows)
 
-    def collect(index, carry):
-        for sequence in range(2):
-            block = index * 2 + sequence
+    def collect(double, carry):
+        streams = [(double * PAIRED + item // 2, item % 2) for item in range(2 * PAIRED)]
+        blocks = [index * 2 + sequence for index, sequence in streams]
+        lines, places, betas, carrieds, closings = ([] for _ in range(5))
+        for index, sequence in streams:
             line, place = columns_of(pos_ref, index, sequence)
-            total, moved = convolve(proj_ref, taps_ref, index, sequence, place)
-            sigma, query, query_scale, keys, key_scale, values = activate(total)
-            beta = jax.nn.sigmoid(load(proj_ref, index, sequence, slice(384, 512)))
-            last = line[:, 127:128]
-            within = (depth >= 0) & (depth.astype(jnp.float32) <= place)
-            later = (depth < 0) & ((-depth).astype(jnp.float32) <= line)
-            carried = place > row.astype(jnp.float32)
-            closing = (127 - row).astype(jnp.float32) <= last
-            query_low = load(query_ref, index, sequence)
-            key_low = load(key_ref, index, sequence)
-            update = update_ref[block]
-            weighted = beta * update
-            flow = flow_ref[block]
-            state = state_ref[block]
-            back = back_ref[block]
-            weight_grad = pull_ref[block] + jnp.where(closing, nn(key_low, flow), 0.0)
-            score_grad = low(jnp.where(within, nt(back, low(weighted)), 0.0))
-            right_grad = tn(inv_ref[block], low(beta * weight_grad))
-            right_low = low(right_grad)
-            mixing_grad = jnp.where(later, -nt(low(update), right_low), 0.0)
-            gram = nt(key_low, key_low)
-            beta_grad = jnp.sum(weight_grad * update + mixing_grad * gram, -1, keepdims=True)
-            gram_grad = low(beta * mixing_grad)
-            key_grad = nt(
+            lines.append(line)
+            places.append(place)
+            betas.append(jax.nn.sigmoid(load(proj_ref, index, sequence, slice(384, 512))))
+            carrieds.append(place > row.astype(jnp.float32))
+            closings.append((127 - row).astype(jnp.float32) <= line[:, 127:128])
+        queries = [load(query_ref, *stream) for stream in streams]
+        keys_all = [load(key_ref, *stream) for stream in streams]
+        updates = [update_ref[block].astype(jnp.float32) for block in blocks]
+        weighted = [beta * update for beta, update in zip(betas, updates)]
+        flows = [flow_ref[block] for block in blocks]
+        states = [state_ref[block] for block in blocks]
+        backs = [back_ref[block] for block in blocks]
+        key_flows = [nn(keys, flow) for keys, flow in zip(keys_all, flows)]
+        score_grads = [nt(back, low(weight)) for back, weight in zip(backs, weighted)]
+        grams = [nt(keys, keys) for keys in keys_all]
+        weight_grads = [
+            pull_ref[block] + jnp.where(closing, key_flow, 0.0)
+            for block, closing, key_flow in zip(blocks, closings, key_flows)
+        ]
+        right_grads = [
+            tn(inv_ref[block], low(beta * weight_grad))
+            for block, beta, weight_grad in zip(blocks, betas, weight_grads)
+        ]
+        score_lows = [
+            low(jnp.where((depth >= 0) & (depth.astype(jnp.float32) <= place), score_grad, 0.0))
+            for place, score_grad in zip(places, score_grads)
+        ]
+        query_grads = [
+            nt(jnp.where(carried, back, 0.0), state) + nn(score_low, keys)
+            for carried, back, state, score_low, keys in zip(
+                carrieds, backs, states, score_lows, keys_all
+            )
+        ]
+        mixing_grads = [
+            jnp.where((depth < 0) & ((-depth).astype(jnp.float32) <= line), -nt(low(update), low(right_grad)), 0.0)
+            for line, update, right_grad in zip(lines, updates, right_grads)
+        ]
+        gram_lows = [low(beta * mixing_grad) for beta, mixing_grad in zip(betas, mixing_grads)]
+        key_grads = [
+            nt(
                 jnp.concatenate(
-                    [low(jnp.where(closing, weighted, 0.0)), low(jnp.where(carried, -right_grad, 0.0))], 1
+                    [low(jnp.where(closing, weight, 0.0)), low(jnp.where(carried, -right_grad, 0.0))], 1
                 ),
                 jnp.concatenate([flow, state], 1),
             )
-            key_grad = key_grad + tn(
-                jnp.concatenate([score_grad, gram_grad], 0), jnp.concatenate([query_low, key_low], 0)
+            for closing, weight, carried, right_grad, flow, state in zip(
+                closings, weighted, carrieds, right_grads, flows, states
             )
-            key_grad = key_grad + nn(gram_grad, key_low)
-            query_grad = nt(jnp.where(carried, back, 0.0), state) + nn(score_grad, key_low)
-            query_grad = query_grad * 128 ** (-0.5)
+        ]
+        key_grads = [
+            key_grad
+            + tn(jnp.concatenate([score_low, gram_low], 0), jnp.concatenate([query, keys], 0))
+            + nn(gram_low, keys)
+            for key_grad, score_low, gram_low, query, keys in zip(
+                key_grads, score_lows, gram_lows, queries, keys_all
+            )
+        ]
+        for item, (index, sequence) in enumerate(streams):
+            total, moved = convolve(proj_ref, taps_ref, index, sequence, places[item])
+            sigma, query, query_scale, keys, key_scale, _ = activate(total)
+            beta = betas[item]
+            beta_grad = jnp.sum(
+                weight_grads[item] * updates[item] + mixing_grads[item] * grams[item], -1, keepdims=True
+            )
+            query_grad = query_grads[item] * 128 ** (-0.5)
             query_act = query_scale * (
                 query_grad - query * jnp.sum(query * query_grad, -1, keepdims=True)
             )
-            key_act = key_scale * (key_grad - keys * jnp.sum(keys * key_grad, -1, keepdims=True))
-            act_grad = jnp.concatenate([query_act, key_act, right_grad], 1)
+            key_act = key_scale * (
+                key_grads[item] - keys * jnp.sum(keys * key_grads[item], -1, keepdims=True)
+            )
+            act_grad = jnp.concatenate([query_act, key_act, right_grads[item]], 1)
             pre_grad = act_grad * (sigma * (1.0 + total * (1.0 - sigma)))
             for offset in range(4):
                 taps_grad_ref[offset : offset + 1, :] += jnp.sum(
                     pre_grad * moved[offset], 0, keepdims=True
                 )
             store(pre_ref, index, sequence, pre_grad)
-            store(place_ref, index, sequence, place)
             logit_grad = jnp.where(column == 0, beta_grad * beta * (1.0 - beta), 0.0)
             store(out_ref, index, sequence, low(logit_grad), slice(384, 512))
         return carry
 
-    lax.fori_loop(0, 8, collect, 0)
+    lax.fori_loop(0, 8 // PAIRED, collect, 0)
+    after_collect()
 
     def spread(index, carry):
         for sequence in range(2):
@@ -295,8 +368,9 @@
             live = jnp.where(index == 7, 0.0, 1.0)
             current = load(pre_ref, index, sequence)
             window = jnp.concatenate([current, pre_ref[pl.ds(after, 8), :] * live], 0)
-            place = load(place_ref, index, sequence)
-            places = jnp.concatenate([place, place_ref[pl.ds(after, 8), :]], 0)[:, 0:1]
+            _, place = columns_of(pos_ref, index, sequence)
+            _, follow = columns_of(pos_ref, jnp.minimum(index + 1, 7), sequence)
+            places = jnp.concatenate([place, follow[0:8]], 0)[:, 0:1]
             total = current * taps_ref[0:1, :]
             for offset in range(1, 4):
                 masked = window * (places >= offset).astype(jnp.float32)
@@ -311,48 +385,7 @@
     rows = jax.ShapeDtypeStruct((2048, CHUNK), jnp.bfloat16)
     small = jax.ShapeDtypeStruct((16, CHUNK, CHUNK), jnp.bfloat16)
     wide = jax.ShapeDtypeStruct((16, CHUNK, CHUNK), jnp.float32)
-    return (rows, rows, small, small, small, small, small, wide, wide)
-
-
-def run_forward(proj, pos, taps, gain):
-    heads = jax.ShapeDtypeStruct((2048, CHUNK), jnp.bfloat16)
-    return pl.pallas_call(
-        mixer_forward,
-        out_shape=(heads,) + saved_shapes(),
-        in_specs=[pl.BlockSpec(memory_space=pltpu.VMEM)] * 4,
-        out_specs=[pl.BlockSpec(memory_space=pltpu.VMEM)] * 10,
-        scratch_shapes=[
-            pltpu.VMEM((16, CHUNK, CHUNK), jnp.float32),
-            pltpu.VMEM((16, CHUNK, CHUNK), jnp.float32),
-        ],
-        compiler_params=PARAMS,
-        cost_estimate=pl.CostEstimate(flops=16 << 30, bytes_accessed=16 << 20, transcendentals=0),
-        name="mixer_forward",
-    )(proj, pos, taps, gain)
-
-
-def run_backward(grad, proj, pos, taps, gain, saved):
-    return pl.pallas_call(
-        mixer_backward,
-        out_shape=(
-            jax.ShapeDtypeStruct((2048, WIDE), jnp.bfloat16),
-            jax.ShapeDtypeStruct((8, 384), jnp.float32),
-            jax.ShapeDtypeStruct((8, CHUNK), jnp.float32),
-        ),
-        in_specs=[pl.BlockSpec(memory_space=pltpu.VMEM)] * 14,
-        out_specs=[pl.BlockSpec(memory_space=pltpu.VMEM)] * 3,
-        scratch_shapes=[
-            pltpu.VMEM((16, CHUNK, CHUNK), jnp.bfloat16),
-            pltpu.VMEM((16, CHUNK, CHUNK), jnp.float32),
-            pltpu.VMEM((16, CHUNK, CHUNK), jnp.bfloat16),
-            pltpu.VMEM((16, CHUNK, CHUNK), jnp.float32),
-            pltpu.VMEM((2048, 384), jnp.float32),
-            pltpu.VMEM((2048, CHUNK), jnp.float32),
-        ],
-        compiler_params=PARAMS,
-        cost_estimate=pl.CostEstimate(flops=32 << 30, bytes_accessed=16 << 20, transcendentals=0),
-        name="mixer_backward",
-    )(grad, proj, pos, taps, gain, *saved)
+    return (rows, rows, small, small, small, small, small, small, wide)
 
 
 def spot(y, z, core):
@@ -567,12 +600,12 @@
         return (
             (0, part.at[near.mine("farside")], slot.at[0], near.side),
             (1, part.at[near.mine("far"), TOP], slot.at[1, TOP], near.down),
-            (2, part.at[near.mine("far"), BOTTOM], slot.at[2, BOTTOM], near.up),
-            (3, part.at[near.mine("downside")], slot.at[3], near.down),
-            (4, part.at[near.mine("upside")], slot.at[4], near.up),
-            (5, part.at[near.mine("down")], slot.at[5], near.down),
-            (6, part.at[near.mine("up")], slot.at[6], near.up),
-            (7, part.at[near.mine("side")], slot.at[7], near.side),
+            (2, part.at[near.mine("far"), BOTTOM], slot.at[1, BOTTOM], near.up),
+            (3, part.at[near.mine("downside")], slot.at[2], near.down),
+            (4, part.at[near.mine("upside")], slot.at[3], near.up),
+            (5, part.at[near.mine("down")], slot.at[4], near.down),
+            (6, part.at[near.mine("up")], slot.at[5], near.up),
+            (7, part.at[near.mine("side")], slot.at[6], near.side),
         )
 
     def send(self, key):
@@ -604,13 +637,13 @@
         near, part, slot = self.near, self.part, self.slot
         self.arrive(3)
         self.arrive(4)
-        add_rows(part.at[near.mine("side")], [slot.at[3], slot.at[4]])
+        add_rows(part.at[near.mine("side")], [slot.at[2], slot.at[3]])
         self.send(7)
         self.arrive(1)
         add_rows(part.at[near.mine("down"), TOP], [slot.at[1, TOP]], 64)
         self.send(5)
         self.arrive(2)
-        add_rows(part.at[near.mine("up"), BOTTOM], [slot.at[2, BOTTOM]], 64)
+        add_rows(part.at[near.mine("up"), BOTTOM], [slot.at[1, BOTTOM]], 64)
         self.send(6)
 
     def fourth(self):
@@ -626,7 +659,7 @@
         chip = near.chips["own"]
         value = self.part[chip * 2 + near.core, rows].astype(jnp.float32)
         value = value + self.twin_part[chip, rows].astype(jnp.float32)
-        for key in (5, 6, 7):
+        for key in (4, 5, 6):
             value = value + self.slot[key, rows].astype(jnp.float32)
         return value
 
@@ -645,19 +678,29 @@
 
 
 def ffn_kernel(
-    input_ref, hidden_ref, teacher_ref, mask_ref, gate_up_ref, down_ref,
-    block_ref, grad_ref, back_ref, square_ref, weight_ref,
-    tokens, grads, both, act_t, both_t, part, twin_part, slot,
-    gather_send, gather_recv, scatter_send, scatter_recv,
+    input_ref, hidden_ref, teacher_ref, mask_ref, gate_up_ref, down_shard_ref,
+    block_ref, grad_ref, back_ref, square_ref, weight_ref, down_grad_ref,
+    tokens, grads, both, act_t, both_t, part, twin_part, slot, down_ref, down_part, down_slot, down_staged,
+    down_send, down_recv, leave_send, leave_recv, gather_send, gather_recv, scatter_send, scatter_recv,
     again_send, again_recv, return_send, return_recv,
 ):
     near = Neighbours()
+    data = lax.axis_index("dp")
     neighbours = [{"tensor": device} for device in (near.up, near.down, near.side, near.twin)]
+    neighbours = neighbours + [{"dp": device} for device in data_neighbours()]
     own = near.mine("own")
     tokens[own] = input_ref[...]
+    down_ref[pl.ds(pl.multiple_of(data * 256, 256), 256)] = down_shard_ref[...]
     greet(neighbours)
     gather = Gather(near, tokens, gather_send, gather_recv)
     gather.start()
+    down = DataGather(
+        down_shard_ref, lambda block: down_ref.at[pl.ds(pl.multiple_of(block * 256, 256), 256)],
+        down_send, down_recv,
+    )
+    down.start()
+    down.relay()
+    down.arrive()
     scatter = Scatter(near, part, twin_part, slot, scatter_send, scatter_recv)
 
     def rows_at(buffer, chip):
@@ -698,6 +741,7 @@
     squares = lax.fori_loop(0, 8, middle, jnp.zeros((16, 1), jnp.float32))
     square_ref[...] = jnp.broadcast_to(jnp.sum(squares, 0, keepdims=True), (8, 128))
     gather.finish()
+    down.finish()
     scatter.finish()
 
     again = Gather(near, grads, again_send, again_recv)
@@ -724,22 +768,35 @@
     lax.fori_loop(0, 8, backward, 0)
     back.first()
 
+    def lanes(block):
+        return pl.ds(pl.multiple_of(block * 256, 256), 256)
+
+    def down_weights(step, carry):
+        column = grads[:, :, lanes(step)].reshape(2048, 256)
+        down_part[:, lanes(step)] = low(nn(act_t[...], column))
+        return carry
+
+    lax.fori_loop(0, 8, down_weights, 0)
+    place = DataPlace()
+    leave = DataScatter(
+        lambda block: down_part.at[:, lanes(block)],
+        lambda other, rows: down_part[rows, lanes(place.block(0, other))],
+        down_slot, down_staged, leave_send, leave_recv,
+    )
+    leave.start()
+    back.second()
+
     def weights(step, carry):
-        @pl.when(step == 2)
-        def _():
-            back.second()
-
         @pl.when(step == 4)
         def _():
             back.third()
 
-        lanes = pl.ds(pl.multiple_of(step * 256, 256), 256)
-        for source, values, first, count in ((both_t, tokens, 0, 2 * HIDDEN), (act_t, grads, 2 * HIDDEN, HIDDEN)):
-            column = values[:, :, lanes].reshape(2048, 256)
-            weight_ref[pl.ds(first, count), lanes] = low(nn(source[...], column))
+        column = tokens[:, :, lanes(step)].reshape(2048, 256)
+        weight_ref[:, lanes(step)] = low(nn(both_t[...], column))
         return carry
 
     lax.fori_loop(0, 8, weights, 0)
+    leave.relay()
     back.fourth()
 
     def ending(index, carry):
@@ -748,15 +805,22 @@
         return carry
 
     lax.fori_loop(0, 8, ending, 0)
+    leave.result(down_grad_ref)
+    leave.finish()
     again.finish()
     back.finish()
 
 
-def run_ffn(ffn_in, hidden, teacher, mask, gate_up, down_t):
+def data_neighbours():
+    place = DataPlace()
+    return [place.block(shift, 0) for shift in range(1, 4)] + [place.block(0, 1)]
+
+
+def run_ffn(ffn_in, hidden, teacher, mask, gate_up, down_shard):
     rows, features = ffn_in.shape
     wide = jax.ShapeDtypeStruct((rows, features), jnp.float32)
     vmem = pl.BlockSpec(memory_space=pltpu.VMEM)
-    semaphores = []
+    semaphores = [pltpu.SemaphoreType.DMA((7,)) for _ in range(4)]
     for _ in range(2):
         for count in (Gather.copies, Gather.copies, Scatter.copies, Scatter.copies):
             semaphores.append(pltpu.SemaphoreType.DMA((count,)))
@@ -767,10 +831,11 @@
             wide,
             wide,
             jax.ShapeDtypeStruct((8, 128), jnp.float32),
-            jax.ShapeDtypeStruct((3 * HIDDEN, features), jnp.bfloat16),
+            jax.ShapeDtypeStruct((2 * HIDDEN, features), jnp.bfloat16),
+            jax.ShapeDtypeStruct((HIDDEN, 256), jnp.float32),
         ),
         in_specs=[vmem] * 6,
-        out_specs=[vmem] * 5,
+        out_specs=[vmem] * 6,
         scratch_shapes=[
             pltpu.VMEM((16, 128, 2048), jnp.bfloat16),
             pltpu.VMEM((16, 128, 2048), jnp.bfloat16),
@@ -779,7 +844,11 @@
             pltpu.VMEM((2 * HIDDEN, 2048), jnp.bfloat16),
             pltpu.VMEM((16, 128, 2048), jnp.bfloat16),
             pltpu.VMEM((8, 128, 2048), jnp.bfloat16),
-            pltpu.VMEM((8, 128, 2048), jnp.bfloat16),
+            pltpu.VMEM((7, 128, 2048), jnp.bfloat16),
+            pltpu.VMEM((2048, HIDDEN), jnp.bfloat16),
+            pltpu.VMEM((HIDDEN, 2048), jnp.bfloat16),
+            pltpu.VMEM((7, HIDDEN, 256), jnp.bfloat16),
+            pltpu.VMEM((HIDDEN, 256), jnp.bfloat16),
         ]
         + semaphores,
         compiler_params=pltpu.CompilerParams(
@@ -787,7 +856,499 @@
         ),
         cost_estimate=pl.CostEstimate(flops=160 << 30, bytes_accessed=16 << 20, transcendentals=0),
         name="feed_forward",
-    )(ffn_in, hidden, teacher, mask, gate_up, down_t)
+    )(ffn_in, hidden, teacher, mask, gate_up, down_shard)
+
+
+def everyone():
+    tensor, data = lax.axis_index("tensor"), lax.axis_index("dp")
+    devices = [{"tensor": (tensor + shift) % 16} for shift in range(1, 16)]
+    return devices + [{"dp": (data + shift) % 8} for shift in range(1, 8)]
+
+
+class Fan:
+    def __init__(self, axis, count, source, target, sends, receives):
+        self.axis, self.count, self.source, self.target = axis, count, source, target
+        self.sends, self.receives = sends, receives
+        self.index = lax.axis_index(axis)
+
+    def copy(self, shift):
+        peer = (self.index + shift) % self.count
+        return remote(
+            self.source(peer), self.target(self.index), self.sends.at[shift],
+            self.receives.at[shift], {self.axis: peer},
+        )
+
+    def start(self):
+        for shift in range(1, self.count):
+            self.copy(shift).start()
+
+    def arrive(self):
+        for shift in range(1, self.count):
+            piece = self.target((self.index + self.count - shift) % self.count)
+            peer = (self.index + shift) % self.count
+            remote(
+                piece, piece, self.sends.at[shift], self.receives.at[shift], {self.axis: peer}
+            ).wait_recv()
+
+    def finish(self):
+        for shift in range(1, self.count):
+            self.copy(shift).wait_send()
+
+
+class DataPlace:
+    def __init__(self):
+        index = lax.axis_index("dp")
+        self.x, self.z = index % 4, index // 4
+
+    def block(self, shift, other):
+        return ((self.z + other) % 2) * 4 + (self.x + shift) % 4
+
+
+class DataGather:
+    copies = 7
+
+    def __init__(self, source, target, sends, receives):
+        self.place = DataPlace()
+        self.source, self.target, self.sends, self.receives = source, target, sends, receives
+
+    def describe(self, key):
+        place = self.place
+        if key == 0:
+            return self.copy(key, self.source, place.block(0, 0), place.block(0, 1))
+        if key < 4:
+            return self.copy(key, self.source, place.block(0, 0), place.block(key, 0))
+        partner = place.block(0, 1)
+        return self.copy(key, self.target(partner), partner, place.block(key - 3, 0))
+
+    def copy(self, key, source, block, peer):
+        return remote(
+            source, self.target(block), self.sends.at[key], self.receives.at[key], {"dp": peer}
+        )
+
+    def start(self):
+        for key in range(4):
+            self.describe(key).start()
+
+    def wait(self, key, block):
+        piece = self.target(block)
+        self.copy(key, piece, block, self.place.block(0, 1)).wait_recv()
+
+    def relay(self):
+        self.wait(0, self.place.block(0, 1))
+        for key in range(4, 7):
+            self.describe(key).start()
+
+    def arrive(self):
+        for shift in range(1, 4):
+            self.wait(shift, self.place.block(4 - shift, 0))
+            self.wait(3 + shift, self.place.block(4 - shift, 1))
+
+    def finish(self):
+        for key in range(7):
+            self.describe(key).wait_send()
+
+
+class DataScatter:
+    copies = 7
+
+    def __init__(self, part, own, slot, staged, sends, receives):
+        self.place = DataPlace()
+        self.part, self.own, self.slot, self.staged = part, own, slot, staged
+        self.sends, self.receives = sends, receives
+
+    def describe(self, key):
+        place = self.place
+        if key == 6:
+            source, peer = self.staged, place.block(0, 1)
+        else:
+            shift, other = key // 2 + 1, key % 2
+            source, peer = self.part(place.block(shift, other)), place.block(shift, 0)
+        return remote(
+            source, self.slot.at[key], self.sends.at[key], self.receives.at[key], {"dp": peer}
+        )
+
+    def start(self):
+        for key in range(6):
+            self.describe(key).start()
+
+    def summed(self, other, rows, extra):
+        total = self.own(other, rows).astype(jnp.float32)
+        for key in range(other, 6, 2):
+            total = total + self.slot[key, rows].astype(jnp.float32)
+        if extra:
+            total = total + self.slot[6, rows].astype(jnp.float32)
+        return total
+
+    def relay(self):
+        for key in (1, 3, 5):
+            self.describe(key).wait_recv()
+
+        def piece(index, carry):
+            rows = pl.ds(pl.multiple_of(index * 16, 16), 16)
+            self.staged[rows] = low(self.summed(1, rows, False))
+            return carry
+
+        lax.fori_loop(0, self.staged.shape[0] // 16, piece, 0)
+        self.describe(6).start()
+
+    def result(self, output):
+        for key in (0, 2, 4, 6):
+            self.describe(key).wait_recv()
+
+        def piece(index, carry):
+            rows = pl.ds(pl.multiple_of(index * 16, 16), 16)
+            output[rows] = self.summed(0, rows, True)
+            return carry
+
+        lax.fori_loop(0, self.staged.shape[0] // 16, piece, 0)
+
+    def finish(self):
+        for key in range(7):
+            self.describe(key).wait_send()
+
+
+def tile_sum(first, second, axes, sems):
+    tensor, data = lax.axis_index("tensor"), lax.axis_index("dp")
+    one = Fan("tensor", 16, lambda peer: first.at[tensor], lambda index: first.at[index], sems[0], sems[1])
+    two = Fan("dp", 8, lambda peer: second.at[data], lambda index: second.at[index], sems[2], sems[3])
+    return one, two
+
+
+def entry_kernel(
+    normed_ref, mix_ref, small_ref, count_ref, pos_ref, gate_up_ref, out_ref,
+    gathered_ref, mix_full_ref, taps_ref, gain_ref, total_ref, gate_up_full_ref, out_full_ref,
+    proj_ref, spread_ref, heads_ref,
+    query_ref, key_ref, inv_ref, kc_ref, score_ref, step_ref, state_ref, update_ref, raw_ref,
+    tokens, small, counts, count_rows, free_ref, shift_ref,
+    gather_send, gather_recv, mix_send, mix_recv, wide_send, wide_recv, small_send, small_recv,
+    out_send, out_recv, all_send, all_recv, count_send, count_recv, row_send, row_recv,
+    head_send, head_recv, local,
+):
+    near = Neighbours()
+    tensor, data = lax.axis_index("tensor"), lax.axis_index("dp")
+    own = near.mine("own")
+    block_rows = pl.ds(pl.multiple_of(data * 256, 256), 256)
+
+    def rows_of_data(ref):
+        return lambda block: ref.at[pl.ds(pl.multiple_of(block * 256, 256), 256)]
+
+    def lanes_of_data(block):
+        return out_full_ref.at[tensor, :, pl.ds(pl.multiple_of(block * 256, 256), 256)]
+
+    wide_own = pltpu.make_async_copy(gate_up_ref, gate_up_full_ref.at[block_rows], local.at[0])
+    out_own = pltpu.make_async_copy(out_ref, lanes_of_data(data), local.at[1])
+    wide_own.start()
+    out_own.start()
+    tokens[own] = normed_ref[...]
+    mix_full_ref[block_rows] = mix_ref[...]
+    small[data] = small_ref[...]
+    counts[tensor] = count_ref[...]
+    greet(everyone())
+    gather = Gather(near, tokens, gather_send, gather_recv)
+    mix = DataGather(mix_ref, rows_of_data(mix_full_ref), mix_send, mix_recv)
+    wide = DataGather(gate_up_ref, rows_of_data(gate_up_full_ref), wide_send, wide_recv)
+    tiny = Fan("dp", 8, lambda peer: small.at[data], lambda index: small.at[index], small_send, small_recv)
+    outs = Fan("dp", 8, lambda peer: out_ref, lanes_of_data, out_send, out_recv)
+    one, two = tile_sum(counts, count_rows, None, (count_send, count_recv, row_send, row_recv))
+    tiny.start()
+    gather.start()
+    mix.start()
+    one.start()
+    outs.start()
+    wide.start()
+    one.arrive()
+    count_rows[data] = jnp.sum(counts[...], 0)
+    two.start()
+    mix.relay()
+    mix.arrive()
+
+    def project(step, carry):
+        gather.before(step)
+        chip = near.chip_at(step)
+        rows = pl.ds(pl.multiple_of(chip * 256, 256), 256)
+        values = jnp.concatenate([tokens[chip * 2], tokens[chip * 2 + 1]], 0)
+        proj_ref[rows, :] = nn(values, mix_full_ref[...])
+        return carry
+
+    lax.fori_loop(0, 8, project, 0)
+    keep = pltpu.make_async_copy(tokens, gathered_ref, local.at[2])
+    keep.start()
+    wide.relay()
+    out_own.wait()
+    outs.arrive()
+    out_gather = Gather(near, out_full_ref, all_send, all_recv)
+    out_gather.start()
+    tiny.arrive()
+    two.arrive()
+    total_ref[...] = jnp.sum(count_rows[...], 0)
+    table = jnp.sum(small[...].astype(jnp.float32), 0)
+    for tap in range(4):
+        for field in range(3):
+            taps_ref[tap : tap + 1, field * 128 : field * 128 + 128] = table[tap * 3 + field : tap * 3 + field + 1]
+    gain_ref[0:1, :] = table[12:13]
+    mixer_forward(
+        proj_ref, pos_ref, taps_ref, gain_ref,
+        heads_ref, query_ref, key_ref, inv_ref, kc_ref, score_ref, step_ref, state_ref, update_ref, raw_ref,
+        free_ref, shift_ref, out_gather.second, out_gather.third,
+    )
+
+    def head_rows(block):
+        return heads_ref.at[pl.ds(pl.multiple_of(block * 128, 128), 128)]
+
+    exchange = Fan("tensor", 16, head_rows, lambda index: spread_ref.at[index], head_send, head_recv)
+    exchange.start()
+    spread_ref[tensor] = heads_ref[pl.ds(pl.multiple_of(tensor * 128, 128), 128)]
+    out_gather.fourth()
+    out_gather.fifth()
+    exchange.arrive()
+    for name in NAMES:
+        out_gather.from_twin(name)
+    wide.arrive()
+    wide_own.wait()
+    keep.wait()
+    for part in (gather, mix, wide, tiny, outs, one, two, out_gather, exchange):
+        part.finish()
+
+
+def dma(*counts):
+    return [pltpu.SemaphoreType.DMA((count,)) for count in counts]
+
+
+def run_entry(normed, mix_shard, small, count, pos, gate_up, out_weight):
+    vmem, hbm = pl.BlockSpec(memory_space=pltpu.VMEM), pl.BlockSpec(memory_space=pl.ANY)
+    half, full = jnp.bfloat16, jnp.float32
+    shape = jax.ShapeDtypeStruct
+    return pl.pallas_call(
+        entry_kernel,
+        out_shape=(
+            shape((16, 128, 2048), half),
+            shape((2048, WIDE), half),
+            shape((8, 384), full),
+            shape((8, CHUNK), full),
+            shape((8, 128), full),
+            shape((2048, 2 * HIDDEN), half),
+            shape((16, 128, 2048), half),
+            shape((2048, WIDE), full),
+            shape((16, 128, CHUNK), half),
+            shape((2048, CHUNK), half),
+        )
+        + saved_shapes(),
+        in_specs=[vmem] * 5 + [hbm] * 2,
+        out_specs=[hbm, vmem, vmem, vmem, vmem, hbm, hbm] + [vmem] * 12,
+        scratch_shapes=[
+            pltpu.VMEM((16, 128, 2048), half),
+            pltpu.VMEM((8, 16, 128), half),
+            pltpu.VMEM((16, 8, 128), full),
+            pltpu.VMEM((8, 8, 128), full),
+            pltpu.VMEM((16, CHUNK, CHUNK), full),
+            pltpu.VMEM((16, CHUNK, CHUNK), full),
+        ]
+        + dma(17, 17, 7, 7, 7, 7, 8, 8, 8, 8, 17, 17, 16, 16, 8, 8, 16, 16, 3),
+        compiler_params=pltpu.CompilerParams(
+            collective_id=2, has_side_effects=True, vmem_limit_bytes=62 << 20
+        ),
+        cost_estimate=pl.CostEstimate(flops=60 << 30, bytes_accessed=16 << 20, transcendentals=0),
+        name="entry",
+    )(normed, mix_shard, small, count, pos, gate_up, out_weight)
+
+
+SMALL = 16
+
+
+def exit_kernel(
+    heads_grad_ref, attention_ref, ffn_part_ref, gathered_ref, proj_ref, pos_ref, taps_ref, gain_ref,
+    mix_ref, heads_ref, unit_ref, sums_ref,
+    query_ref, key_ref, inv_ref, kc_ref, score_ref, step_ref, state_ref, update_ref, raw_ref,
+    attn_ref, ffn_ref, weight_ref, total_ref,
+    grad, attention, proj_low, taps_grad, gain_grad,
+    back_ref, pull_ref, flow_ref, enter_ref, pre_ref,
+    part, twin_part, slot, ffn_own, ffn_slot, ffn_staged, parts, part_slot, part_staged, proj_t, tile,
+    sums, sum_rows,
+    head_send, head_recv, gather_send, gather_recv, ffn_send, ffn_recv, mix_send, mix_recv,
+    scatter_send, scatter_recv, sum_send, sum_recv, row_send, row_recv, local,
+):
+    near = Neighbours()
+    tensor, data = lax.axis_index("tensor"), lax.axis_index("dp")
+    own = near.mine("own")
+    place = DataPlace()
+
+    def lanes(block):
+        return pl.ds(pl.multiple_of(block * 256, 256), 256)
+
+    loads = [
+        pltpu.make_async_copy(ffn_part_ref.at[:, lanes(place.block(0, other))], ffn_own.at[other], local.at[other])
+        for other in range(2)
+    ]
+    for copy in loads:
+        copy.start()
+    attention[own] = attention_ref[...]
+    greet(everyone())
+
+    def head_rows(block):
+        return grad.at[pl.ds(pl.multiple_of(block * 128, 128), 128)]
+
+    exchange = Fan("tensor", 16, lambda peer: heads_grad_ref.at[peer], head_rows, head_send, head_recv)
+    exchange.start()
+    gather = Gather(near, attention, gather_send, gather_recv)
+    gather.start()
+    ffn = DataScatter(
+        lambda block: ffn_part_ref.at[:, lanes(block)], lambda other, rows: ffn_own[other, rows],
+        ffn_slot, ffn_staged, ffn_send, ffn_recv,
+    )
+    ffn.start()
+    grad[pl.ds(pl.multiple_of(tensor * 128, 128), 128)] = heads_grad_ref[tensor]
+    exchange.arrive()
+    mixer_backward(
+        grad, proj_ref, pos_ref, taps_ref, gain_ref,
+        query_ref, key_ref, inv_ref, kc_ref, score_ref, step_ref, state_ref, update_ref, raw_ref,
+        proj_low, taps_grad, gain_grad,
+        back_ref, pull_ref, flow_ref, enter_ref, pre_ref, gather.second, gather.third,
+    )
+    gather.fourth()
+    units = pltpu.make_async_copy(unit_ref, enter_ref, local.at[4])
+    units.start()
+    scatter = Scatter(near, part, twin_part, slot, scatter_send, scatter_recv)
+
+    def backward(step, carry):
+        chip = near.chip_at(step)
+        rows = pl.ds(pl.multiple_of(chip * 256, 256), 256)
+        values = proj_low[rows, :]
+        keep = lax.broadcasted_iota(jnp.int32, (256, WIDE), 1) <= 384
+        partial = low(nt(jnp.where(keep, values, jnp.zeros_like(values)), mix_ref[...]))
+        proj_t[:, rows] = values.T[:400]
+        part[chip * 2] = partial[:128]
+        part[chip * 2 + 1] = partial[128:]
+        scatter.to_twin(chip)
+        return carry
+
+    lax.fori_loop(0, 8, backward, 0)
+    gather.fifth()
+    for name in NAMES:
+        gather.from_twin(name)
+    scatter.first()
+
+    def fetch(step):
+        return pltpu.make_async_copy(gathered_ref.at[:, :, lanes(step)], tile.at[step % 2], local.at[2 + step % 2])
+
+    fetch(0).start()
+    table = jnp.concatenate([taps_grad[...], gain_grad[...]], 1)
+
+    def weights(step, carry):
+        @pl.when(step < 7)
+        def _():
+            fetch(step + 1).start()
+
+        @pl.when(step == 3)
+        def _():
+            scatter.second()
+
+        fetch(step).wait()
+        column = tile[step % 2].reshape(2048, 256)
+        product = nn(proj_t[...], column)
+        parts[0:400, lanes(step)] = low(product)
+        parts[400:528, lanes(step)] = low(tn(heads_ref[...], attention[:, :, lanes(step)].reshape(2048, 256)))
+        return carry
+
+    lax.fori_loop(0, 8, weights, 0)
+    pick_row = lax.broadcasted_iota(jnp.int32, (CHUNK, 2048), 0)
+    pick_lane = lax.broadcasted_iota(jnp.int32, (CHUNK, 2048), 1)
+    wanted = (pick_lane // 256) * 16 + pick_lane % 256
+    select = ((pick_row == wanted) & (pick_lane % 256 < 16)).astype(jnp.bfloat16)
+    for tap in range(4):
+        for field in range(3):
+            row = tap * 3 + field
+            pull_ref[0, row : row + 1, :] = taps_grad[tap : tap + 1, field * 128 : field * 128 + 128]
+    pull_ref[0, 12:13, :] = gain_grad[0:1, :]
+    small = nn(low(pull_ref[0, 0:16, :]), select)
+    small_row = lax.broadcasted_iota(jnp.int32, (16, 2048), 0)
+    moved = jnp.concatenate([small[15:16], small[0:15]], 0)
+    beta_row = parts[384:400, :].astype(jnp.float32)
+    parts[384:400, :] = low(jnp.where(small_row == 0, beta_row, moved))
+    mix = DataScatter(
+        lambda block: parts.at[:, lanes(block)],
+        lambda other, rows: parts[rows, lanes(place.block(0, other))],
+        part_slot, part_staged, mix_send, mix_recv,
+    )
+    mix.start()
+    scatter.third()
+    for copy in loads:
+        copy.wait()
+    ffn.relay()
+    scatter.fourth()
+    units.wait()
+
+    def ending(index, total):
+        rows = pl.ds(pl.multiple_of(index * 16, 16), 16)
+        value = scatter.total(rows)
+        attn_ref[rows] = value
+        unit = jnp.concatenate([enter_ref[piece, rows] for piece in range(16)], 1)
+        return total + value * unit
+
+    total = lax.fori_loop(0, 8, ending, jnp.zeros((16, 2048), jnp.float32))
+    total = jnp.sum(total, 0, keepdims=True)
+    sums[tensor, 8:24] = sums_ref[8:24]
+    for piece in range(8):
+        sums[tensor, piece : piece + 1] = total[:, piece * 256 : piece * 256 + 256]
+    one, two = tile_sum(sums, sum_rows, None, (sum_send, sum_recv, row_send, row_recv))
+    one.start()
+    mix.relay()
+    one.arrive()
+    sum_rows[data] = jnp.sum(sums[...], 0)
+    two.start()
+    ffn.result(ffn_ref)
+    two.arrive()
+    total_ref[...] = jnp.sum(sum_rows[...], 0)
+    mix.result(weight_ref)
+    for item in (exchange, gather, ffn, scatter, mix, one, two):
+        item.finish()
+
+
+def run_exit(heads_grad, attention, ffn_part, gathered, proj, pos, taps, gain, mix, heads, unit, sums, saved):
+    vmem, hbm = pl.BlockSpec(memory_space=pltpu.VMEM), pl.BlockSpec(memory_space=pl.ANY)
+    half, full = jnp.bfloat16, jnp.float32
+    shape = jax.ShapeDtypeStruct
+    return pl.pallas_call(
+        exit_kernel,
+        out_shape=(
+            shape((128, 2048), full),
+            shape((2 * HIDDEN, 256), full),
+            shape((528, 256), full),
+            shape((24, 256), full),
+        ),
+        in_specs=[vmem] * 2 + [hbm] * 2 + [vmem] * 6 + [hbm] + [vmem] * 10,
+        out_specs=[vmem] * 4,
+        scratch_shapes=[
+            pltpu.VMEM((2048, CHUNK), half),
+            pltpu.VMEM((16, 128, 2048), half),
+            pltpu.VMEM((2048, WIDE), half),
+            pltpu.VMEM((8, 384), full),
+            pltpu.VMEM((8, CHUNK), full),
+            pltpu.VMEM((16, CHUNK, CHUNK), half),
+            pltpu.VMEM((16, CHUNK, CHUNK), full),
+            pltpu.VMEM((16, CHUNK, CHUNK), half),
+            pltpu.VMEM((16, CHUNK, CHUNK), full),
+            pltpu.VMEM((2048, 384), full),
+            pltpu.VMEM((16, 128, 2048), half),
+            pltpu.VMEM((8, 128, 2048), half),
+            pltpu.VMEM((7, 128, 2048), half),
+            pltpu.VMEM((2, 2 * HIDDEN, 256), half),
+            pltpu.VMEM((7, 2 * HIDDEN, 256), half),
+            pltpu.VMEM((2 * HIDDEN, 256), half),
+            pltpu.VMEM((528, 2048), half),
+            pltpu.VMEM((7, 528, 256), half),
+            pltpu.VMEM((528, 256), half),
+            pltpu.VMEM((400, 2048), half),
+            pltpu.VMEM((2, 16, 128, 256), half),
+            pltpu.VMEM((16, 24, 256), full),
+            pltpu.VMEM((8, 24, 256), full),
+        ]
+        + dma(16, 16, 17, 17, 7, 7, 7, 7, 16, 16, 16, 16, 8, 8, 5),
+        compiler_params=pltpu.CompilerParams(
+            collective_id=3, has_side_effects=True, vmem_limit_bytes=63 << 20
+        ),
+        cost_estimate=pl.CostEstimate(flops=60 << 30, bytes_accessed=16 << 20, transcendentals=0),
+        name="exit",
+    )(heads_grad, attention, ffn_part, gathered, proj, pos, taps, gain, mix, heads, unit, sums, *saved)
 
 
 def token_places(segment):
@@ -812,50 +1373,39 @@
     hidden_units = gate_weight.shape[1]
     rows = 128
     features = inputs.shape[2]
-    valid = f32(lax.psum(jnp.sum(padding), ("dp", "tensor")))
-    scale = 16 * 1024 / valid
-
-    small = jnp.concatenate([conv_taps.reshape(12, 16), head_gain.reshape(1, 16)], 0).reshape(1, 208)
-    small = jnp.pad(small, ((0, 7), (0, WIDE - 208)))
+
+    small = jnp.concatenate([conv_taps.reshape(12, 16), head_gain.reshape(1, 16)], 0)
+    lane = jnp.arange(CHUNK)[None, :] // 16 == lax.axis_index("dp")
+    small = jnp.where(lane, jnp.tile(jnp.pad(small, ((0, 3), (0, 0))), (1, 8)), 0)
     mix_shard = jnp.concatenate(
         [qkv_weight.reshape(256, 384), jnp.broadcast_to(beta_weight, (256, CHUNK))], 1
     )
-    mix_all = lax.all_gather(jnp.concatenate([mix_shard, small], 0), "dp", axis=0)
-    mix_full = mix_all[:, :256].reshape(2048, WIDE)
-    small_all = f32(jnp.transpose(mix_all[:, 256, :208].reshape(8, 13, 16), (1, 0, 2)).reshape(13, CHUNK))
-    taps = jnp.pad(small_all[:12].reshape(4, 384), ((0, 4), (0, 0)))
-    gain = jnp.pad(small_all[12:], ((0, 7), (0, 0)))
+    gate_up_shard = jnp.concatenate([pad_lanes(gate_weight, HIDDEN), pad_lanes(up_weight, HIDDEN)], 1)
+    down_shard = pad_lanes(jnp.transpose(down_weight), HIDDEN)
+    count = jnp.broadcast_to(f32(jnp.sum(padding)), (8, 128))
 
     tokens = f32(inputs.reshape(rows, features))
     attn_scale = lax.rsqrt(jnp.mean(tokens * tokens, -1, keepdims=True) + 1e-06)
     attn_unit = tokens * attn_scale
     normed = (attn_unit * attn_gain).astype(jnp.bfloat16)
-    gathered = lax.all_gather(normed, "tensor", axis=0, tiled=True)
-
-    ffn_shard = jnp.concatenate(
-        [pad_lanes(gate_weight, 384), pad_lanes(up_weight, 384), pad_lanes(jnp.transpose(down_weight), 384)], 1
-    )
-    ffn_full = lax.all_gather(ffn_shard, "dp", axis=0, tiled=True)
-    gate_up, down_t = ffn_full[:, :768], ffn_full[:, 768:]
-    out_all = lax.all_gather(lax.all_gather(jnp.transpose(out_weight), "dp", axis=0, tiled=True), "tensor", axis=1, tiled=True)
-
-    proj = nn(gathered, mix_full)
     pos = token_places(segment_ids)
-    heads, *saved = run_forward(proj, pos, taps, gain)
-    spread = lax.all_to_all(heads.reshape(16, rows, CHUNK), "tensor", 0, 0, tiled=True)
+    (
+        gathered, mix_full, taps, gain, total, gate_up, out_full, proj, spread, heads, *saved
+    ) = run_entry(normed, mix_shard, small, count, pos, gate_up_shard, out_weight)
+    out_full = out_full.reshape(features, features)
+    valid = total[0, 0]
+    scale = 16 * 1024 / valid
     heads_rows = jnp.transpose(spread, (1, 0, 2)).reshape(rows, features)
-    hidden = tokens + nt(heads_rows, out_all)
+    hidden = tokens + nn(heads_rows, out_full)
 
     mlp_scale = lax.rsqrt(jnp.mean(hidden * hidden, -1, keepdims=True) + 1e-06)
     mlp_unit = hidden * mlp_scale
     ffn_in = (mlp_unit * mlp_gain).astype(jnp.bfloat16)
     mask = f32(padding.reshape(rows, 1))
     masks = jnp.broadcast_to(jnp.stack([mask, scale * mask]), (2, rows, CHUNK))
-    output, block_grad, mlp_grad, square_tile, ffn_part = run_ffn(
-        ffn_in, hidden, teacher.reshape(rows, features), masks, gate_up, down_t
-    )
-    squares = square_tile[0, 0]
-    ffn_grads = f32(lax.psum_scatter(ffn_part, "dp", scatter_dimension=1, tiled=True))
+    output, block_grad, mlp_grad, square_tile, ffn_part, down_grad = run_ffn(
+        ffn_in, hidden, teacher.reshape(rows, features), masks, gate_up, down_shard
+    )
 
     mlp_sum = jnp.sum(mlp_grad * mlp_unit, 0)
     mlp_inner = mlp_grad * mlp_gain
@@ -863,51 +1413,36 @@
         mlp_inner - mlp_unit * jnp.mean(mlp_inner * mlp_unit, -1, keepdims=True)
     )
     attention_low = hidden_grad.astype(jnp.bfloat16)
-    heads_grad_rows = nn(attention_low, out_all).astype(jnp.bfloat16)
-    heads_grad = lax.all_to_all(
-        jnp.transpose(heads_grad_rows.reshape(rows, 16, CHUNK), (1, 0, 2)), "tensor", 0, 0, tiled=True
-    ).reshape(2048, CHUNK)
-    attention_all = lax.all_gather(attention_low, "tensor", axis=0, tiled=True)
-    out_part = tn(attention_all, heads).astype(jnp.bfloat16)
-
-    proj_low, taps_part, gain_part = run_backward(f32(heads_grad), proj, pos, taps, gain, saved)
-    attn_grad = f32(
-        lax.psum_scatter(
-            nt(proj_low, jnp.where(jnp.arange(WIDE) <= 384, mix_full, 0)).astype(jnp.bfloat16),
-            "tensor", scatter_dimension=0, tiled=True,
-        )
-    )
-    mix_part = tn(gathered, proj_low)[:, :385]
-    small_part = jnp.concatenate([taps_part[:4].reshape(12, CHUNK), gain_part[:1]], 0)
-    small_part = jnp.transpose(small_part.reshape(13, 8, 16), (1, 0, 2)).reshape(8, 208)
-    small_part = jnp.pad(small_part, ((0, 0), (0, 48))).reshape(2048, 1)
-    mix_part = jnp.concatenate([mix_part, small_part, jnp.zeros((2048, 126), jnp.float32)], 1)
-    mix_part = jnp.concatenate([mix_part.astype(jnp.bfloat16), out_part], 1)
-    mix_grads = f32(lax.psum_scatter(mix_part, "dp", scatter_dimension=0, tiled=True))
-
-    attn_sum = jnp.sum(attn_grad * attn_unit, 0)
+    heads_grad_rows = nt(attention_low, out_full).astype(jnp.bfloat16)
+    heads_grad = jnp.transpose(heads_grad_rows.reshape(rows, 16, CHUNK), (1, 0, 2))
+    sums = jnp.concatenate(
+        [jnp.zeros((8, 256)), mlp_sum.reshape(8, 256), jnp.broadcast_to(square_tile[0:1, 0:1], (8, 256))], 0
+    )
+    units = jnp.transpose(attn_unit.reshape(rows, 16, CHUNK), (1, 0, 2))
+    attn_grad, ffn_grads, mix_grads, totals = run_exit(
+        heads_grad, attention_low, ffn_part, gathered, proj, pos, taps, gain, mix_full, heads, units, sums, saved
+    )
     attn_inner = attn_grad * attn_gain
     input_grad = hidden_grad + attn_scale * (
         attn_inner - attn_unit * jnp.mean(attn_inner * attn_unit, -1, keepdims=True)
     )
-    attn_total, mlp_total, square_total = lax.psum((attn_sum, mlp_sum, squares), ("dp", "tensor"))
-    loss = square_total / (valid * features)
-    small_grad = mix_grads[:208, 385].reshape(13, 16)
+    loss = totals[16, 0] / (valid * features)
+    small_grad = mix_grads[385:398, :16]
     shape = (2, 64, features)
     return (
         output.reshape(shape),
         loss,
         input_grad.reshape(shape),
-        attn_total,
-        mix_grads[:, :384].reshape(256, 3, CHUNK),
-        mix_grads[:, 384:385],
+        totals[:8].reshape(features),
+        jnp.transpose(mix_grads[:384]).reshape(256, 3, CHUNK),
+        jnp.transpose(mix_grads[384:385]),
         small_grad[:12].reshape(4, 3, 1, 16),
         small_grad[12:].reshape(1, 16),
-        jnp.transpose(mix_grads[:, 512:]),
-        mlp_total,
+        mix_grads[400:],
+        totals[8:16].reshape(features),
         jnp.transpose(ffn_grads[:hidden_units]),
-        jnp.transpose(ffn_grads[384 : 384 + hidden_units]),
-        ffn_grads[768 : 768 + hidden_units],
+        jnp.transpose(ffn_grads[HIDDEN : HIDDEN + hidden_units]),
+        down_grad[:hidden_units],
     )
 
 

time: 794 us -> 498 us (0.63)
  waiting for transfers between devices: 244 us -> 0 us
  Pallas kernels: 246 us -> 431 us
  blocking collectives: 181 us -> 0 us
  matrix products: 42.2 us -> 11.6 us
  between operations: 17.1 us -> 4.69 us
  starting transfers between devices: 9.14 us -> 0 us
    reduce_scatter x3 -> x0, waiting for transfers between devices: 165 us -> none  [the longest x1 92.5 us: body(): lax.psum_scatter(nt(proj_low, jnp.where(jnp.arange(WIDE) <= 384, mix_full...]
    pallas_call x2, Pallas kernels: 75.4 us -> 236 us  [the longest x1 125 us: run_entry(): pl.pallas_call(entry_kernel, out_shape=(shape((16, 128, 2048), half), sha...]
    psum x2 -> x0, blocking collectives: 143 us -> none  [the longest x1 74.8 us: body(): lax.psum((attn_sum, mlp_sum, squares), ('dp', 'tensor'))]
    all_gather x5 -> x0, waiting for transfers between devices: 64.1 us -> none  [the longest x1 49.3 us: body(): gathered = lax.all_gather(normed, 'tensor', axis=0, tiled=True)]
    all_gather x1 -> x0, blocking collectives: 38.4 us -> none  [body(): lax.all_gather(jnp.transpose(out_weight), 'dp', axis=0, tiled=True)]
    pallas_call x1, Pallas kernels: 170 us -> 194 us  [run_ffn(): pl.pallas_call(ffn_kernel, out_shape=(jax.ShapeDtypeStruct((rows, feature...]
    all_to_all x2 -> x0, waiting for transfers between devices: 13.9 us -> none  [the longest x1 13.9 us: body(): lax.all_to_all(jnp.transpose(heads_grad_rows.reshape(rows, 16, CHUNK), (1...]
    dot_general x2 -> x0, matrix products: 13.3 us -> none  [tn(): lax.dot_general(a, b, (((0,), (0,)), ((), ())), preferred_element_type=jn...]
  transfers between devices with their start and end apart: 10 -> 0, of which waited for: 6 -> 0; matrix products, arithmetic and copies ran while one was open for 9% -> 0% of each run, Pallas kernels for 10% -> 0%
where the time goes in v3:
time: 498 us; the launch traced here: 496 us
  Pallas kernels  431 us (87%)
  local copies, waits for them, and re-layouts  26.3 us (5%)
  other arithmetic  22.7 us (5%)
  matrix products  11.6 us (2%)
    pallas_call x1, Pallas kernels, run_ffn(): pl.pallas_call(ffn_kernel, out_shape=(jax.ShapeDtypeStruct((rows, feature...  194 us
    pallas_call x1, Pallas kernels, run_entry(): pl.pallas_call(entry_kernel, out_shape=(shape((16, 128, 2048), half), sha...  125 us
    pallas_call x1, Pallas kernels, run_exit(): pl.pallas_call(exit_kernel, out_shape=(shape((128, 2048), full), shape((2...  111 us

profile of v3, /device:TPU:0, one launch (start us, length us, event | category | flops | bytes accessed | tf_op | source)
XLA Modules:
  0.0 495.9 jit_solution(7307394875460755197)
XLA Ops:
  0.6 1.2 multiply_reduce_fusion.4
  2.0 2.0 multiply_convert_fusion.1.normed_ref
  4.0 1.9 convert_reduce_fusion
  6.5 1.4 fusion.13
  9.2 1.1 copy.60
  10.3 1.1 copy.61
  12.2 1.1 copy.56
  17.0 125.0 %entry.1 = (bf16[16,128,2048]{2,1,0:T(8,128)(2,1)}, bf16[2048,512]{1,0:T(8,128)(2,1)}, f32[8,384]{1,0:T(8,128)}, f32[8,128]{1,0:T(8,128)}, f32[8,128]{1,0:T(8,12...) custom-call(bf16[128,2048]{1,0:T(8,128)(2,1)} %multiply_convert_fusi, ...), custom_call_target="tpu_custom_call" | custom-call | flops 64424509440 | bytes 16777216 | tf_op jit(solution)/shard_map/entry/pallas_call | solution.py:1121
  142.2 5.4 %multiply_reduce_fusion.3 = (f32[128]{0:T(128)S(1)}, f32[128,2048]{1,0:T(8,128)S(1)}) fusion(f32[128,2048]{1,0:T(8,128)S(1)} %bitcast.65, bf16[16,128,2048]{2,1,0:T(8,128)(2,1)} %get-tuple-element.43, bf16[16,128,128]{2,1,0:T(8,128)(2,1)} %get-tuple-element.42), kind=kOutput, calls=%fused_computation.13 | convolution fusion | flops 1074528128 | bytes 11010560 | tf_op jit(solution)/shard_map/dot_general | solution.py:17
  149.5 1.2 slice.42
  153.1 194.2 %feed_forward.1 = (bf16[128,2048]{1,0:T(8,128)(2,1)}, f32[128,2048]{1,0:T(8,128)}, f32[128,2048]{1,0:T(8,128)}, f32[8,128]{1,0:T(8,128)}, bf16[768,2048]{1,0:T(8,128)(2,1)}, /*index=5*/f32[384,256]{1,0:T(8,128)}) custom-call(bf16[128,2048]{1,0:T(8,128)(2,1)} %multiply_convert_fusion.input_ref, f32[128,2048]{1,0:T(8,128)} %copy-done, ...), custom_call_target="tpu_custom_call" | custom-call | flops 171798691840 | bytes 16777216 | tf_op jit(solution)/shard_map/feed_forward/pallas_call | solution.py:827
  347.4 1.9 multiply_reduce_fusion.1
  349.3 1.3 slice.43
  352.0 3.1 fusion.12
  355.9 6.3 %convolution_convert_fusion = bf16[128,2048]{1,0:T(8,128)(2,1)S(1)} fusion(bf16[128,2048]{1,0:T(8,128)(2,1)S(1)} %get-tuple-element.125.attention_ref, bf16[2048,2048]{1,0:T(8,128)(2,1)} %bitcast.64), kind=kOutput, calls=%fused_computation.3 | convolution fusion | flops 1074003968 | bytes 9437184 | tf_op jit(solution)/shard_map/dot_general | solution.py:21
  363.7 1.3 fusion.1.unit_ref
  365.1 111.3 %exit.1 = (f32[128,2048]{1,0:T(8,128)}, f32[768,256]{1,0:T(8,128)}, f32[528,256]{1,0:T(8,128)}, f32[24,256]{1,0:T(8,128)}) custom-call(bf16[16,128,128]{2,1,0:T(8,128)(2,1)} %bitcast.74, bf16[128,2048]{1,0:T(8,128)(2,1)} %copy-done.5, bf16[768,2048]{1,0:T(8,128)(2,1)} %get-tuple-element.49.ffn_part_ref, ...), custom_call_target="tpu_custom_call" | custom-call | flops 64424509440 | bytes 16777216 | tf_op jit(solution)/shard_map/exit/pallas_call | solution.py:1310
  476.4 1.6 multiply_reduce_fusion
  478.0 2.9 multiply_add_fusion
  480.9 1.0 slice.46
  482.8 2.0 slice_bitcast_fusion
  484.8 1.6 slice.50
  490.8 1.3 slice_bitcast_fusion.4
  492.0 1.2 slice.49
  (81 shorter events, 18.9 us)
Async XLA Ops:
  2.0 6.6 %copy-start.13 = (f32[128]{0:T(128)}, f32[128]{0:T(128)S(1)}, u32[]{:S(2)}) copy-start(f32[128]{0:T(128)S(1)} %rsqrt.20) | copy-start | bytes 1540
  17.0 125.0 %copy-start.1 = (bf16[2,64,2048]{2,1,0:T(8,128)(2,1)S(1)}, bf16[2,64,2048]{2,1,0:T(8,128)(2,1)}, u32[]{:S(2)}) copy-start(bf16[2,64,2048]{2,1,0:T(8,128)(2,1)} %param.14) | copy-start | bytes 1572868
  142.1 6.5 %copy-start.10 = (f32[2048]{0:T(1024)S(1)}, f32[2048]{0:T(1024)}, u32[]{:S(2)}) copy-start(f32[2048]{0:T(1024)} %param.24) | copy-start | bytes 24580
  142.2 7.3 %copy-start.3 = (f32[2,64,2048]{2,1,0:T(8,128)}, f32[2,64,2048]{2,1,0:T(8,128)S(1)}, u32[]{:S(2)}) copy-start(f32[2,64,2048]{2,1,0:T(8,128)S(1)} %convert_element_type.84) | copy-start | bytes 3145732
  142.2 10.0 %copy-start.8 = (bf16[352,256]{1,0:T(8,128)(2,1)S(1)}, bf16[352,256]{1,0:T(8,128)(2,1)}, u32[]{:S(2)}) copy-start(bf16[352,256]{1,0:T(8,128)(2,1)} %param.27) | copy-start | bytes 540676
  147.6 1.0 copy-start
  148.6 1.0 copy-start.15
  153.1 194.2 %copy-start.11 = (f32[2048]{0:T(1024)S(1)}, f32[2048]{0:T(1024)}, u32[]{:S(2)}) copy-start(f32[2048]{0:T(1024)} %param.24) | copy-start | bytes 24580
  153.1 194.2 %copy-start.16 = (f32[128]{0:T(128)S(1)}, f32[128]{0:T(128)}, u32[]{:S(2)}) copy-start(f32[128]{0:T(128)} %copy-done.15) | copy-start | bytes 1540
  349.3 14.3 %copy-start.4 = (f32[2,64,2048]{2,1,0:T(8,128)S(1)}, f32[2,64,2048]{2,1,0:T(8,128)}, u32[]{:S(2)}) copy-start(f32[2,64,2048]{2,1,0:T(8,128)} %copy-done.3) | copy-start | bytes 3145732
  352.0 11.7 %copy-start.14 = (f32[128]{0:T(128)S(1)}, f32[128]{0:T(128)}, u32[]{:S(2)}) copy-start(f32[128]{0:T(128)} %copy-done.13) | copy-start | bytes 1540
  355.1 0.8 copy-start.5
  365.1 111.3 %copy-start.2 = (bf16[2,64,2048]{2,1,0:T(8,128)(2,1)S(1)}, bf16[2,64,2048]{2,1,0:T(8,128)(2,1)}, u32[]{:S(2)}) copy-start(bf16[2,64,2048]{2,1,0:T(8,128)(2,1)} %param.14) | copy-start | bytes 1572868
  365.1 111.4 %copy-start.9 = (f32[2048]{0:T(1024)S(1)}, f32[2048]{0:T(1024)}, u32[]{:S(2)}) copy-start(f32[2048]{0:T(1024)} %param.18) | copy-start | bytes 24580
  476.4 10.0 %copy-start.12 = (f32[24,256]{1,0:T(8,128)S(1)}, f32[24,256]{1,0:T(8,128)}, u32[]{:S(2)}) copy-start(f32[24,256]{1,0:T(8,128)} %get-tuple-element.66) | copy-start | bytes 73732
  476.4 16.8 %copy-start.7 = (f32[384,256]{1,0:T(8,128)S(1)}, f32[384,256]{1,0:T(8,128)}, u32[]{:S(2)}) copy-start(f32[384,256]{1,0:T(8,128)} %get-tuple-element.70) | copy-start | bytes 1179652
  476.4 17.6 %copy-start.6 = (bf16[128,2048]{1,0:T(8,128)(2,1)S(1)}, bf16[128,2048]{1,0:T(8,128)(2,1)}, u32[]{:S(2)}) copy-start(bf16[128,2048]{1,0:T(8,128)(2,1)} %get-tuple-element.46) | copy-start | bytes 1572868

commit v4 on v3

--- a/solution.py
+++ b/solution.py
@@ -8,8 +8,6 @@
 MESH = pl.DeviceIdType.MESH
 CHUNK = 128
 WIDE = 512
-GROUPED = 4
-PAIRED = 2
 PARAMS = pltpu.CompilerParams(vmem_limit_bytes=56 << 20)
 
 
@@ -46,19 +44,19 @@
     return row, column
 
 
-def rows_of(index, sequence):
+def chunk_rows(index, sequence):
     first = pl.multiple_of(index * 256 + sequence * 64, 64)
     second = pl.multiple_of(index * 256 + 128 + sequence * 64, 64)
     return first, second
 
 
 def load(ref, index, sequence, lanes=slice(None)):
-    first, second = rows_of(index, sequence)
+    first, second = chunk_rows(index, sequence)
     return jnp.concatenate([ref[pl.ds(first, 64), lanes], ref[pl.ds(second, 64), lanes]], 0)
 
 
 def store(ref, index, sequence, value, lanes=slice(None)):
-    first, second = rows_of(index, sequence)
+    first, second = chunk_rows(index, sequence)
     ref[pl.ds(first, 64), lanes] = value[:64]
     ref[pl.ds(second, 64), lanes] = value[64:]
 
@@ -119,13 +117,14 @@
 def mixer_forward(
     proj_ref, pos_ref, taps_ref, gain_ref,
     heads_ref, query_ref, key_ref, inv_ref, kc_ref, score_ref, step_ref, state_ref, update_ref, raw_ref,
-    free_ref, shift_ref, after_prepare, after_advance,
+    free_ref, shift_ref, which, between,
 ):
     row, column = grid_masks()
     depth = row - column
 
-    def prepare(double, carry):
-        streams = [(double * GROUPED + item // 2, item % 2) for item in range(2 * GROUPED)]
+    streams = [(index, which) for index in range(8)]
+
+    def prepare():
         lines, queries, keys_all, values_all, betas, withins, carrieds, mixings = ([] for _ in range(8))
         for index, sequence in streams:
             line, place = columns_of(pos_ref, index, sequence)
@@ -166,28 +165,17 @@
             score_ref[block] = low(jnp.where(withins[item], scores[item], 0.0))
             step_ref[block] = low(through - ends_all[item][:, :128])
             shift_ref[block] = ends_all[item][:, 128:]
-        return carry
-
-    lax.fori_loop(0, 8 // GROUPED, prepare, 0)
-
-    def advance(index, states):
-        new = []
-        for sequence in range(2):
-            block = index * 2 + sequence
-            state_low = low(states[sequence])
-            state_ref[block] = state_low
-            new.append(nn(step_ref[block], state_low) + shift_ref[block])
-        return tuple(new)
-
-    zero = jnp.zeros((CHUNK, CHUNK), jnp.float32)
-    after_prepare()
-    states = (zero, zero)
+
+    prepare()
+    between()
+    state = jnp.zeros((CHUNK, CHUNK), jnp.float32)
     for index in range(8):
-        states = advance(index, states)
-    after_advance()
-
-    def finish(double, carry):
-        streams = [(double * GROUPED + item // 2, item % 2) for item in range(2 * GROUPED)]
+        block = index * 2 + which
+        state_low = low(state)
+        state_ref[block] = state_low
+        state = nn(step_ref[block], state_low) + shift_ref[block]
+
+    def finish():
         blocks = [index * 2 + sequence for index, sequence in streams]
         states = [state_ref[block] for block in blocks]
         recalls = [nn(kc_ref[block], state) for block, state in zip(blocks, states)]
@@ -205,24 +193,21 @@
             update_ref[blocks[item]] = low(updates[item])
             raw_ref[blocks[item]] = output
             store(heads_ref, index, sequence, low(output * scale * gain_ref[0:1, :]))
-        return carry
-
-    lax.fori_loop(0, 8 // GROUPED, finish, 0)
+
+    finish()
 
 
 def mixer_backward(
     grad_ref, proj_ref, pos_ref, taps_ref, gain_ref,
     query_ref, key_ref, inv_ref, kc_ref, score_ref, step_ref, state_ref, update_ref, raw_ref,
     out_ref, taps_grad_ref, gain_grad_ref,
-    back_ref, pull_ref, flow_ref, enter_ref, pre_ref, after_prepare, after_collect,
+    back_ref, pull_ref, flow_ref, enter_ref, pre_ref, which, between, after,
 ):
     row, column = grid_masks()
     depth = row - column
-    taps_grad_ref[...] = jnp.zeros_like(taps_grad_ref)
-    gain_grad_ref[...] = jnp.zeros_like(gain_grad_ref)
-
-    def prepare(double, carry):
-        streams = [(double * GROUPED + item // 2, item % 2) for item in range(2 * GROUPED)]
+
+    def prepare():
+        streams = [(index, which) for index in range(8)]
         blocks = [index * 2 + sequence for index, sequence in streams]
         back_lows = []
         for (index, sequence), block in zip(streams, blocks):
@@ -251,28 +236,18 @@
             enter_ref[block] = enter
             back_ref[block] = back_low
             pull_ref[block] = pull
-        return carry
-
-    lax.fori_loop(0, 8 // GROUPED, prepare, 0)
-
-    def retreat(step, flows):
-        index = 7 - step
-        new = []
-        for sequence in range(2):
-            block = index * 2 + sequence
-            flow_low = low(flows[sequence])
-            flow_ref[block] = flow_low
-            new.append(tn(step_ref[block], flow_low) + enter_ref[block])
-        return tuple(new)
-
-    zero = jnp.zeros((CHUNK, CHUNK), jnp.float32)
-    after_prepare()
-    flows = (zero, zero)
-    for step in range(8):
-        flows = retreat(step, flows)
+
+    prepare()
+    between()
+    flow = jnp.zeros((CHUNK, CHUNK), jnp.float32)
+    for index in reversed(range(8)):
+        block = index * 2 + which
+        flow_low = low(flow)
+        flow_ref[block] = flow_low
+        flow = tn(step_ref[block], flow_low) + enter_ref[block]
 
     def collect(double, carry):
-        streams = [(double * PAIRED + item // 2, item % 2) for item in range(2 * PAIRED)]
+        streams = [(double * 4 + item, which) for item in range(4)]
         blocks = [index * 2 + sequence for index, sequence in streams]
         lines, places, betas, carrieds, closings = ([] for _ in range(5))
         for index, sequence in streams:
@@ -354,19 +329,20 @@
                 taps_grad_ref[offset : offset + 1, :] += jnp.sum(
                     pre_grad * moved[offset], 0, keepdims=True
                 )
-            store(pre_ref, index, sequence, pre_grad)
+            pre_ref[pl.ds(pl.multiple_of(index * CHUNK, CHUNK), CHUNK), :] = pre_grad
             logit_grad = jnp.where(column == 0, beta_grad * beta * (1.0 - beta), 0.0)
             store(out_ref, index, sequence, low(logit_grad), slice(384, 512))
         return carry
 
-    lax.fori_loop(0, 8 // PAIRED, collect, 0)
-    after_collect()
-
-    def spread(index, carry):
-        for sequence in range(2):
-            after = pl.multiple_of(jnp.minimum(index * 256 + 256, 1792) + sequence * 64, 64)
+    lax.fori_loop(0, 2, collect, 0)
+    after()
+
+    def spread(pair_index, carry):
+        for item in range(2):
+            index, sequence = pair_index * 2 + item, which
+            after = pl.multiple_of(jnp.minimum(index * CHUNK + CHUNK, 896), CHUNK)
             live = jnp.where(index == 7, 0.0, 1.0)
-            current = load(pre_ref, index, sequence)
+            current = pre_ref[pl.ds(pl.multiple_of(index * CHUNK, CHUNK), CHUNK), :]
             window = jnp.concatenate([current, pre_ref[pl.ds(after, 8), :] * live], 0)
             _, place = columns_of(pos_ref, index, sequence)
             _, follow = columns_of(pos_ref, jnp.minimum(index + 1, 7), sequence)
@@ -378,7 +354,7 @@
             store(out_ref, index, sequence, low(total), slice(0, 384))
         return carry
 
-    lax.fori_loop(0, 8, spread, 0)
+    lax.fori_loop(0, 4, spread, 0)
 
 
 def saved_shapes():
@@ -421,10 +397,10 @@
     def twins(self, name):
         return self.chips[name] * 2 + 1 - self.core
 
-    def chip_at(self, step):
-        quarter = step // 2
+    def quarter_at(self, step):
+        quarter = step % 4
         shift = quarter + quarter // 2 - 2 * (quarter // 3)
-        return ((self.y + shift) % 4) * 2 + (self.z + step % 2) % 2
+        return (self.y + shift) % 4
 
 
 def greet(devices):
@@ -441,122 +417,100 @@
     )
 
 
-TOP, BOTTOM, WHOLE = pl.ds(0, 64), pl.ds(64, 64), pl.ds(0, 128)
 NAMES = ("own", "side", "down", "up", "downside", "upside", "far", "farside")
+ORDER = (("own", "side"), ("up", "upside"), ("down", "downside"), ("far", "farside"))
+
+
+class Rows:
+    def __init__(self, first, count):
+        self.first, self.count = first, count
+        self.whole = pl.ds(first, count)
+        self.top = pl.ds(first, count // 2)
+        self.bottom = pl.ds(first + count // 2, count // 2)
+
+
+ALL, HALVES = Rows(0, 128), (Rows(0, 64), Rows(64, 64))
 
 
 class Gather:
     copies = 17
 
-    def __init__(self, near, buffer, sends, receives):
+    def __init__(self, near, buffer, sends, receives, rows=ALL):
         self.near, self.buffer, self.sends, self.receives = near, buffer, sends, receives
-
-    def send(self, key, block, rows, device):
-        piece = self.buffer.at[block, rows]
-        copy = remote(piece, piece, self.sends.at[key], self.receives.at[key], {"tensor": device})
-        copy.start()
-
-    def arrive(self, key, block, rows=WHOLE):
-        piece = self.buffer.at[block, rows]
-        remote(
-            piece, piece, self.sends.at[key], self.receives.at[key], {"tensor": self.near.twin}
-        ).wait_recv()
+        self.rows = rows
+
+    def piece(self, key, name):
+        rows = self.rows
+        part = {5: rows.top, 6: rows.bottom, 7: rows.top, 8: rows.bottom}.get(key, rows.whole)
+        return self.buffer.at[self.near.mine(name), part]
+
+    def copy(self, key, piece, device):
+        return remote(piece, piece, self.sends.at[key], self.receives.at[key], {"tensor": device})
+
+    def send(self, key, name, device):
+        self.copy(key, self.piece(key, name), device).start()
+
+    def arrive(self, key, name):
+        self.copy(key, self.piece(key, name), self.near.twin).wait_recv()
 
     def to_twin(self, name):
-        self.send(9 + NAMES.index(name), self.near.mine(name), WHOLE, self.near.twin)
-
-    def from_twin(self, name):
-        self.arrive(9 + NAMES.index(name), self.near.twins(name))
+        self.send(9 + NAMES.index(name), name, self.near.twin)
+
+    def from_twin(self, *names):
+        for name in names:
+            piece = self.buffer.at[self.near.twins(name), self.rows.whole]
+            self.copy(9 + NAMES.index(name), piece, self.near.twin).wait_recv()
 
     def start(self):
         near = self.near
-        own = near.mine("own")
-        self.send(1, own, WHOLE, near.up)
-        self.send(2, own, WHOLE, near.down)
-        self.send(0, own, WHOLE, near.side)
+        self.send(1, "own", near.up)
+        self.send(2, "own", near.down)
+        self.send(0, "own", near.side)
         self.to_twin("own")
 
+    def from_down(self):
+        self.arrive(1, "down")
+        self.send(5, "down", self.near.up)
+        self.to_twin("down")
+
+    def from_up(self):
+        self.arrive(2, "up")
+        self.send(6, "up", self.near.down)
+        self.to_twin("up")
+
+    def from_side(self):
+        self.arrive(0, "side")
+        self.send(3, "side", self.near.up)
+        self.send(4, "side", self.near.down)
+        self.to_twin("side")
+
     def second(self):
-        near = self.near
-        self.arrive(1, near.mine("down"))
-        self.send(5, near.mine("down"), TOP, near.up)
-        self.arrive(2, near.mine("up"))
-        self.send(6, near.mine("up"), BOTTOM, near.down)
-        self.arrive(0, near.mine("side"))
-        self.send(3, near.mine("side"), WHOLE, near.up)
-        self.send(4, near.mine("side"), WHOLE, near.down)
-        self.to_twin("side")
-        self.to_twin("up")
-        self.to_twin("down")
+        self.from_down()
+        self.from_up()
+        self.from_side()
 
     def third(self):
-        near = self.near
-        far = near.mine("far")
-        self.arrive(5, far, TOP)
-        self.send(7, far, TOP, near.side)
-        self.arrive(6, far, BOTTOM)
-        self.send(8, far, BOTTOM, near.side)
+        self.arrive(5, "far")
+        self.send(7, "far", self.near.side)
+        self.arrive(6, "far")
+        self.send(8, "far", self.near.side)
         self.to_twin("far")
 
     def fourth(self):
-        near = self.near
-        self.arrive(4, near.mine("upside"))
+        self.arrive(4, "upside")
         self.to_twin("upside")
-        self.arrive(3, near.mine("downside"))
+        self.arrive(3, "downside")
         self.to_twin("downside")
 
     def fifth(self):
-        far = self.near.mine("farside")
-        self.arrive(7, far, TOP)
-        self.arrive(8, far, BOTTOM)
+        self.arrive(7, "farside")
+        self.arrive(8, "farside")
         self.to_twin("farside")
 
     def finish(self):
-        near = self.near
         names = ("own", "own", "own", "side", "side", "down", "up", "far", "far") + NAMES
         for key, name in enumerate(names):
-            rows = {5: TOP, 6: BOTTOM, 7: TOP, 8: BOTTOM}.get(key, WHOLE)
-            piece = self.buffer.at[near.mine(name), rows]
-            remote(
-                piece, piece, self.sends.at[key], self.receives.at[key], {"tensor": near.twin}
-            ).wait_send()
-
-    def before(self, step):
-        @pl.when(step == 0)
-        def _():
-            self.from_twin("own")
-
-        @pl.when(step == 1)
-        def _():
-            self.second()
-            self.from_twin("side")
-
-        @pl.when(step == 2)
-        def _():
-            self.from_twin("up")
-
-        @pl.when(step == 3)
-        def _():
-            self.third()
-            self.fourth()
-            self.from_twin("upside")
-
-        @pl.when(step == 4)
-        def _():
-            self.from_twin("down")
-
-        @pl.when(step == 5)
-        def _():
-            self.from_twin("downside")
-
-        @pl.when(step == 6)
-        def _():
-            self.from_twin("far")
-
-        @pl.when(step == 7)
-        def _():
-            self.fifth()
-            self.from_twin("farside")
+            self.copy(key, self.piece(key, name), self.near.twin).wait_send()
 
 
 def add_rows(target, sources, count=128):
@@ -572,102 +526,128 @@
 
 
 class Scatter:
-    slots = 8
     copies = 16
 
-    def __init__(self, near, part, twin_part, slot, sends, receives):
+    def __init__(self, near, part, twin_part, slot, sends, receives, rows=ALL):
         self.near, self.part, self.twin_part, self.slot = near, part, twin_part, slot
-        self.sends, self.receives = sends, receives
+        self.sends, self.receives, self.rows = sends, receives, rows
 
     def describe(self, key, source, target, device):
         return remote(source, target, self.sends.at[key], self.receives.at[key], {"tensor": device})
 
     def twin_copy(self, chip):
+        whole = self.rows.whole
         return self.describe(
-            8 + chip, self.part.at[chip * 2 + 1 - self.near.core], self.twin_part.at[chip], self.near.twin
+            8 + chip, self.part.at[chip * 2 + 1 - self.near.core, whole],
+            self.twin_part.at[chip, whole], self.near.twin,
         )
 
     def to_twin(self, chip):
         self.twin_copy(chip).start()
+
+    def mine(self, name, rows=None):
+        return self.part.at[self.near.mine(name), self.rows.whole if rows is None else rows]
 
     def chip_sum(self, name):
         chip = self.near.chips[name]
         self.twin_copy(chip).wait_recv()
-        add_rows(self.part.at[chip * 2 + self.near.core], [self.twin_part.at[chip]])
-
-    def outgoing(self):
-        near, part, slot = self.near, self.part, self.slot
-        return (
-            (0, part.at[near.mine("farside")], slot.at[0], near.side),
-            (1, part.at[near.mine("far"), TOP], slot.at[1, TOP], near.down),
-            (2, part.at[near.mine("far"), BOTTOM], slot.at[1, BOTTOM], near.up),
-            (3, part.at[near.mine("downside")], slot.at[2], near.down),
-            (4, part.at[near.mine("upside")], slot.at[3], near.up),
-            (5, part.at[near.mine("down")], slot.at[4], near.down),
-            (6, part.at[near.mine("up")], slot.at[5], near.up),
-            (7, part.at[near.mine("side")], slot.at[6], near.side),
-        )
+        add_rows(self.mine(name), [self.twin_part.at[chip, self.rows.whole]], self.rows.count)
+
+    def outgoing(self, key):
+        near, slot, rows = self.near, self.slot, self.rows
+        name, place, part, device = (
+            ("farside", 0, rows.whole, near.side),
+            ("far", 1, rows.top, near.down),
+            ("far", 1, rows.bottom, near.up),
+            ("downside", 2, rows.whole, near.down),
+            ("upside", 3, rows.whole, near.up),
+            ("down", 4, rows.whole, near.down),
+            ("up", 5, rows.whole, near.up),
+            ("side", 6, rows.whole, near.side),
+        )[key]
+        return self.describe(key, self.mine(name, part), slot.at[place, part], device)
 
     def send(self, key):
-        self.describe(*self.outgoing()[key]).start()
+        self.outgoing(key).start()
 
     def arrive(self, key):
-        self.describe(*self.outgoing()[key]).wait_recv()
+        self.outgoing(key).wait_recv()
+
+    def sums(self, *names):
+        for name in names:
+            self.chip_sum(name)
+            key = {"farside": 0, "downside": 3, "upside": 4}.get(name)
+            if key is not None:
+                self.send(key)
 
     def first(self):
-        self.chip_sum("farside")
-        self.send(0)
-        self.chip_sum("downside")
-        self.send(3)
-        self.chip_sum("upside")
-        self.send(4)
-        self.chip_sum("far")
-        self.chip_sum("down")
-        self.chip_sum("up")
-        self.chip_sum("side")
+        self.sums("farside", "downside", "upside", "far", "down", "up", "side")
 
     def second(self):
-        near, part, slot = self.near, self.part, self.slot
         self.arrive(0)
-        add_rows(part.at[near.mine("far")], [slot.at[0]])
+        add_rows(self.mine("far"), [self.slot.at[0, self.rows.whole]], self.rows.count)
         self.send(1)
         self.send(2)
 
-    def third(self):
-        near, part, slot = self.near, self.part, self.slot
+    def to_side(self):
+        slot, rows = self.slot, self.rows
         self.arrive(3)
         self.arrive(4)
-        add_rows(part.at[near.mine("side")], [slot.at[2], slot.at[3]])
+        add_rows(self.mine("side"), [slot.at[2, rows.whole], slot.at[3, rows.whole]], rows.count)
         self.send(7)
+
+    def to_down(self):
+        rows = self.rows
         self.arrive(1)
-        add_rows(part.at[near.mine("down"), TOP], [slot.at[1, TOP]], 64)
+        add_rows(self.mine("down", rows.top), [self.slot.at[1, rows.top]], rows.count // 2)
         self.send(5)
+
+    def to_up(self):
+        rows = self.rows
         self.arrive(2)
-        add_rows(part.at[near.mine("up"), BOTTOM], [slot.at[1, BOTTOM]], 64)
+        add_rows(self.mine("up", rows.bottom), [self.slot.at[1, rows.bottom]], rows.count // 2)
         self.send(6)
 
+    def third(self):
+        self.to_side()
+        self.to_down()
+        self.to_up()
+
     def fourth(self):
-        near = self.near
-        chip = near.chips["own"]
-        self.twin_copy(chip).wait_recv()
+        self.twin_copy(self.near.chips["own"]).wait_recv()
         for key in (7, 5, 6):
             self.arrive(key)
-        return self.part.at[chip * 2 + near.core], self.twin_part.at[chip]
 
     def total(self, rows):
-        near = self.near
-        chip = near.chips["own"]
-        value = self.part[chip * 2 + near.core, rows].astype(jnp.float32)
+        chip = self.near.chips["own"]
+        value = self.part[chip * 2 + self.near.core, rows].astype(jnp.float32)
         value = value + self.twin_part[chip, rows].astype(jnp.float32)
-        for key in (4, 5, 6):
-            value = value + self.slot[key, rows].astype(jnp.float32)
+        for place in (4, 5, 6):
+            value = value + self.slot[place, rows].astype(jnp.float32)
         return value
 
     def finish(self):
         for chip in range(8):
             self.twin_copy(chip).wait_send()
-        for copy in self.outgoing():
-            self.describe(*copy).wait_send()
+        for key in range(8):
+            self.outgoing(key).wait_send()
+
+
+def at_steps(step, table):
+    for moment, actions in table.items():
+
+        @pl.when(step == moment)
+        def _(actions=actions):
+            for action in actions:
+                action()
+
+
+def pair(items, names):
+    return lambda: items.from_twin(*names)
+
+
+def summing(items, *names):
+    return lambda: items.sums(*names)
 
 
 HIDDEN = 384
@@ -675,14 +655,44 @@
 
 def sigmoid(value):
     return 1.0 / (1.0 + jnp.exp(-value))
+
+
+def rows_of(half, quarter):
+    return pl.ds(pl.multiple_of(half * 1024 + quarter * 256, 256), 256)
+
+
+def half_of(half):
+    return pl.ds(pl.multiple_of(half * 64, 64), 64)
+
+
+def quarter_rows(buffer, half, quarter):
+    return buffer[pl.ds(quarter * 4, 4), half_of(half)].reshape(256, buffer.shape[2])
+
+
+def lanes(block):
+    return pl.ds(pl.multiple_of(block * 256, 256), 256)
+
+
+def token_column(buffer, block):
+    first = buffer[:, 0:64, lanes(block)].reshape(1024, 256)
+    return jnp.concatenate([first, buffer[:, 64:128, lanes(block)].reshape(1024, 256)], 0)
+
+
+def scatter_quarter(scatters, half, quarter, partial, part):
+    part[pl.ds(quarter * 4, 4), half_of(half)] = partial.reshape(4, 64, partial.shape[1])
+    for index, scatter in enumerate(scatters):
+
+        @pl.when(half == index)
+        def _(scatter=scatter):
+            scatter.to_twin(quarter * 2)
+            scatter.to_twin(quarter * 2 + 1)
 
 
 def ffn_kernel(
     input_ref, hidden_ref, teacher_ref, mask_ref, gate_up_ref, down_shard_ref,
     block_ref, grad_ref, back_ref, square_ref, weight_ref, down_grad_ref,
     tokens, grads, both, act_t, both_t, part, twin_part, slot, down_ref, down_part, down_slot, down_staged,
-    down_send, down_recv, leave_send, leave_recv, gather_send, gather_recv, scatter_send, scatter_recv,
-    again_send, again_recv, return_send, return_recv,
+    down_send, down_recv, leave_send, leave_recv, *sems,
 ):
     near = Neighbours()
     data = lax.axis_index("dp")
@@ -690,90 +700,114 @@
     neighbours = neighbours + [{"dp": device} for device in data_neighbours()]
     own = near.mine("own")
     tokens[own] = input_ref[...]
-    down_ref[pl.ds(pl.multiple_of(data * 256, 256), 256)] = down_shard_ref[...]
+    down_ref[lanes(data)] = down_shard_ref[...]
     greet(neighbours)
-    gather = Gather(near, tokens, gather_send, gather_recv)
-    gather.start()
-    down = DataGather(
-        down_shard_ref, lambda block: down_ref.at[pl.ds(pl.multiple_of(block * 256, 256), 256)],
-        down_send, down_recv,
+    a, g = (
+        [Gather(near, buffer, sems[k + 2 * h], sems[k + 2 * h + 1], HALVES[h]) for h in range(2)]
+        for buffer, k in ((tokens, 0), (grads, 4))
     )
+    r, b = (
+        [Scatter(near, part, twin_part, slot, sems[k + 2 * h], sems[k + 2 * h + 1], HALVES[h]) for h in range(2)]
+        for k in (8, 12)
+    )
+    a[0].start()
+    down = DataGather(down_shard_ref, lambda block: down_ref.at[lanes(block)], down_send, down_recv)
     down.start()
-    down.relay()
-    down.arrive()
-    scatter = Scatter(near, part, twin_part, slot, scatter_send, scatter_recv)
-
-    def rows_at(buffer, chip):
-        return jnp.concatenate([buffer[chip * 2], buffer[chip * 2 + 1]], 0)
 
     def forward(step, carry):
-        gather.before(step)
-        chip = near.chip_at(step)
-        rows = pl.ds(pl.multiple_of(chip * 256, 256), 256)
-        product = nn(rows_at(tokens, chip), gate_up_ref[...])
+        at_steps(step, {
+            0: [a[0].second, a[1].start, down.relay, a[0].third, a[1].from_side, a[0].fourth, down.arrive, pair(a[0], ORDER[0])],
+            1: [pair(a[0], ORDER[1])],
+            2: [a[0].fifth, summing(r[0], "side"), pair(a[0], ORDER[2])],
+            3: [summing(r[0], "up", "upside"), a[1].from_down, a[1].from_up, pair(a[0], ORDER[3])],
+            4: [summing(r[0], "downside", "down"), a[1].fourth, pair(a[1], ORDER[0])],
+            5: [summing(r[0], "farside", "far"), pair(a[1], ORDER[1])],
+            6: [summing(r[1], "side"), a[1].third, r[0].to_side, pair(a[1], ORDER[2])],
+            7: [
+                summing(r[1], "upside"), r[0].second, summing(r[1], "up", "down", "downside"), r[0].to_down,
+                a[1].fifth, pair(a[1], ORDER[3]),
+            ],
+        })
+        half, quarter = step // 4, near.quarter_at(step)
+        rows = rows_of(half, quarter)
+        product = nn(quarter_rows(tokens, half, quarter), gate_up_ref[...])
         both[rows, :] = product
         gate, up = product[:, :HIDDEN], product[:, HIDDEN:]
         act = low(gate * sigmoid(gate) * up)
         act_t[:, rows] = act.T
-        partial = low(nt(act, down_ref[...]))
-        part[chip * 2] = partial[:128]
-        part[chip * 2 + 1] = partial[128:]
-        scatter.to_twin(chip)
+        scatter_quarter(r, half, quarter, low(nt(act, down_ref[...])), part)
         return carry
 
     lax.fori_loop(0, 8, forward, 0)
-    scatter.first()
-    scatter.second()
-    scatter.third()
-    scatter.fourth()
-
-    def middle(index, squares):
-        rows = pl.ds(pl.multiple_of(index * 16, 16), 16)
-        output = hidden_ref[rows] + scatter.total(rows)
-        block_ref[rows] = low(output)
-        diff = output - teacher_ref[rows].astype(jnp.float32)
-        weight = mask_ref[0, rows, 0:1]
-        grad = mask_ref[1, rows, 0:1] * diff
-        grad_ref[rows] = grad
-        grads[own, rows] = low(grad)
-        return squares + weight * jnp.sum(diff * diff, -1, keepdims=True)
-
-    squares = lax.fori_loop(0, 8, middle, jnp.zeros((16, 1), jnp.float32))
-    square_ref[...] = jnp.broadcast_to(jnp.sum(squares, 0, keepdims=True), (8, 128))
-    gather.finish()
-    down.finish()
-    scatter.finish()
-
-    again = Gather(near, grads, again_send, again_recv)
-    again.start()
-    back = Scatter(near, part, twin_part, slot, return_send, return_recv)
+    square_ref[...] = jnp.zeros_like(square_ref)
+
+    def middle(half):
+        def piece(index, carry):
+            rows = pl.ds(pl.multiple_of(half * 64 + index * 16, 16), 16)
+            output = hidden_ref[rows] + r[half].total(rows)
+            block_ref[rows] = low(output)
+            diff = output - teacher_ref[rows].astype(jnp.float32)
+            weight = mask_ref[0, rows, 0:1]
+            grad = mask_ref[1, rows, 0:1] * diff
+            grad_ref[rows] = grad
+            grads[own, rows] = low(grad)
+            squares = jnp.sum(weight * jnp.sum(diff * diff, -1, keepdims=True), 0, keepdims=True)
+            square_ref[...] += jnp.broadcast_to(squares, (8, 128))
+            return carry
+
+        lax.fori_loop(0, 4, piece, 0)
+
+    r[0].to_up()
+    r[1].to_side()
+    r[1].sums("far", "farside")
+    r[0].fourth()
+    middle(0)
+    g[0].start()
+    r[1].second()
+    g[0].from_down()
+    g[0].from_up()
+    r[1].to_down()
+    r[1].to_up()
+    g[0].from_side()
+    g[0].third()
+    r[0].finish()
+
+    def turn():
+        r[1].fourth()
+        middle(1)
+        r[1].finish()
 
     def backward(step, carry):
-        again.before(step)
-        chip = near.chip_at(step)
-        rows = pl.ds(pl.multiple_of(chip * 256, 256), 256)
-        act_grad = nn(rows_at(grads, chip), down_ref[...])
+        at_steps(step, {
+            0: [pair(g[0], ORDER[0])],
+            1: [turn, summing(b[0], "side"), g[1].start, g[0].fifth, g[0].fourth, pair(g[0], ORDER[1])],
+            2: [g[1].second, pair(g[0], ORDER[2])],
+            3: [summing(b[0], "upside", "up"), pair(g[0], ORDER[3])],
+            4: [summing(b[0], "downside", "down"), g[1].third, pair(g[1], ORDER[0])],
+            5: [summing(b[0], "farside", "far"), g[1].fourth, summing(b[1], "side"), pair(g[1], ORDER[1])],
+            6: [b[0].to_side, g[1].fifth, pair(g[1], ORDER[2])],
+            7: [b[0].second, summing(b[1], "upside", "up"), pair(g[1], ORDER[3])],
+        })
+        half, quarter = step // 4, near.quarter_at(step)
+        rows = rows_of(half, quarter)
+        act_grad = nn(quarter_rows(grads, half, quarter), down_ref[...])
         gate, up = both[rows, :HIDDEN], both[rows, HIDDEN:]
         sigma = sigmoid(gate)
         gate_low = low(act_grad * up * sigma * (1.0 + gate * (1.0 - sigma)))
         up_low = low(act_grad * gate * sigma)
         both_low = jnp.concatenate([gate_low, up_low], 1)
         both_t[:, rows] = both_low.T
-        partial = low(nt(both_low, gate_up_ref[...]))
-        part[chip * 2] = partial[:128]
-        part[chip * 2 + 1] = partial[128:]
-        back.to_twin(chip)
+        scatter_quarter(b, half, quarter, low(nt(both_low, gate_up_ref[...])), part)
         return carry
 
     lax.fori_loop(0, 8, backward, 0)
-    back.first()
-
-    def lanes(block):
-        return pl.ds(pl.multiple_of(block * 256, 256), 256)
+    b[1].sums("downside", "down")
+    b[0].to_down()
+    b[0].to_up()
 
     def down_weights(step, carry):
-        column = grads[:, :, lanes(step)].reshape(2048, 256)
-        down_part[:, lanes(step)] = low(nn(act_t[...], column))
+        at_steps(step, {2: [summing(b[1], "far", "farside")]})
+        down_part[:, lanes(step)] = low(nn(act_t[...], token_column(grads, step)))
         return carry
 
     lax.fori_loop(0, 8, down_weights, 0)
@@ -784,31 +818,31 @@
         down_slot, down_staged, leave_send, leave_recv,
     )
     leave.start()
-    back.second()
+
+    def ending(half):
+        b[half].fourth()
+
+        def piece(index, carry):
+            rows = pl.ds(pl.multiple_of(half * 64 + index * 16, 16), 16)
+            back_ref[rows] = b[half].total(rows)
+            return carry
+
+        lax.fori_loop(0, 4, piece, 0)
 
     def weights(step, carry):
-        @pl.when(step == 4)
-        def _():
-            back.third()
-
-        column = tokens[:, :, lanes(step)].reshape(2048, 256)
-        weight_ref[:, lanes(step)] = low(nn(both_t[...], column))
+        at_steps(step, {3: [b[1].to_side], 7: [b[1].second]})
+        weight_ref[:, lanes(step)] = low(nn(both_t[...], token_column(tokens, step)))
         return carry
 
     lax.fori_loop(0, 8, weights, 0)
+    ending(0)
+    b[1].to_down()
+    b[1].to_up()
     leave.relay()
-    back.fourth()
-
-    def ending(index, carry):
-        rows = pl.ds(pl.multiple_of(index * 16, 16), 16)
-        back_ref[rows] = back.total(rows)
-        return carry
-
-    lax.fori_loop(0, 8, ending, 0)
+    ending(1)
     leave.result(down_grad_ref)
-    leave.finish()
-    again.finish()
-    back.finish()
+    for item in (down, leave, a[0], a[1], g[0], g[1], b[0], b[1]):
+        item.finish()
 
 
 def data_neighbours():
@@ -820,10 +854,8 @@
     rows, features = ffn_in.shape
     wide = jax.ShapeDtypeStruct((rows, features), jnp.float32)
     vmem = pl.BlockSpec(memory_space=pltpu.VMEM)
-    semaphores = [pltpu.SemaphoreType.DMA((7,)) for _ in range(4)]
-    for _ in range(2):
-        for count in (Gather.copies, Gather.copies, Scatter.copies, Scatter.copies):
-            semaphores.append(pltpu.SemaphoreType.DMA((count,)))
+    counts = [7] * 4 + [Gather.copies] * 8 + [Scatter.copies] * 8
+    semaphores = [pltpu.SemaphoreType.DMA((count,)) for count in counts]
     return pl.pallas_call(
         ffn_kernel,
         out_shape=(
@@ -1020,9 +1052,8 @@
     proj_ref, spread_ref, heads_ref,
     query_ref, key_ref, inv_ref, kc_ref, score_ref, step_ref, state_ref, update_ref, raw_ref,
     tokens, small, counts, count_rows, free_ref, shift_ref,
-    gather_send, gather_recv, mix_send, mix_recv, wide_send, wide_recv, small_send, small_recv,
-    out_send, out_recv, all_send, all_recv, count_send, count_recv, row_send, row_recv,
-    head_send, head_recv, local,
+    mix_send, mix_recv, wide_send, wide_recv, small_send, small_recv,
+    out_send, out_recv, all_send, all_recv, count_send, count_recv, row_send, row_recv, local, *sems,
 ):
     near = Neighbours()
     tensor, data = lax.axis_index("tensor"), lax.axis_index("dp")
@@ -1044,70 +1075,108 @@
     small[data] = small_ref[...]
     counts[tensor] = count_ref[...]
     greet(everyone())
-    gather = Gather(near, tokens, gather_send, gather_recv)
+    a = [Gather(near, tokens, sems[2 * h], sems[2 * h + 1], HALVES[h]) for h in range(2)]
     mix = DataGather(mix_ref, rows_of_data(mix_full_ref), mix_send, mix_recv)
     wide = DataGather(gate_up_ref, rows_of_data(gate_up_full_ref), wide_send, wide_recv)
     tiny = Fan("dp", 8, lambda peer: small.at[data], lambda index: small.at[index], small_send, small_recv)
     outs = Fan("dp", 8, lambda peer: out_ref, lanes_of_data, out_send, out_recv)
     one, two = tile_sum(counts, count_rows, None, (count_send, count_recv, row_send, row_recv))
+    everything = Gather(near, out_full_ref, all_send, all_recv)
+    a[0].start()
+    outs.start()
+    one.start()
     tiny.start()
-    gather.start()
     mix.start()
-    one.start()
-    outs.start()
+
+    def counted():
+        one.arrive()
+        count_rows[data] = jnp.sum(counts[...], 0)
+        two.start()
+
+    def outer():
+        out_own.wait()
+        outs.arrive()
+        everything.start()
+
+    def ready():
+        tiny.arrive()
+        two.arrive()
+        total_ref[...] = jnp.sum(count_rows[...], 0)
+        table = jnp.sum(small[...].astype(jnp.float32), 0)
+        for tap in range(4):
+            for field in range(3):
+                row = tap * 3 + field
+                taps_ref[tap : tap + 1, field * 128 : field * 128 + 128] = table[row : row + 1]
+        gain_ref[0:1, :] = table[12:13]
+
+    def head_rows(half):
+        def place(block):
+            return heads_ref.at[pl.ds(pl.multiple_of(block * 128 + half * 64, 64), 64)]
+
+        return place
+
+    def target_rows(half):
+        return lambda index: spread_ref.at[index, HALVES[half].whole]
+
+    exchanges = [
+        Fan("tensor", 16, head_rows(h), target_rows(h), sems[4 + 2 * h], sems[5 + 2 * h]) for h in range(2)
+    ]
+    keep = pltpu.make_async_copy(tokens, gathered_ref, local.at[2])
+    a[0].second()
+    a[1].start()
+    counted()
+    mix.relay()
+    a[0].third()
+    a[0].fourth()
+    outer()
+    a[1].second()
+    a[0].fifth()
+    mix.arrive()
     wide.start()
-    one.arrive()
-    count_rows[data] = jnp.sum(counts[...], 0)
-    two.start()
-    mix.relay()
-    mix.arrive()
-
-    def project(step, carry):
-        gather.before(step)
-        chip = near.chip_at(step)
-        rows = pl.ds(pl.multiple_of(chip * 256, 256), 256)
-        values = jnp.concatenate([tokens[chip * 2], tokens[chip * 2 + 1]], 0)
-        proj_ref[rows, :] = nn(values, mix_full_ref[...])
+
+    def per_sequence(sequence, carry):
+        def project(step, inner):
+            at_steps(sequence * 4 + step, {
+                0: [pair(a[0], ORDER[0])],
+                1: [pair(a[0], ORDER[1])],
+                2: [pair(a[0], ORDER[2])],
+                3: [a[1].third, a[1].fourth, pair(a[0], ORDER[3])],
+                4: [pair(a[1], ORDER[0])],
+                5: [pair(a[1], ORDER[1])],
+                6: [pair(a[1], ORDER[2])],
+                7: [pair(a[1], ORDER[3]), keep.start],
+            })
+            quarter = near.quarter_at(step)
+            product = nn(quarter_rows(tokens, sequence, quarter), mix_full_ref[...])
+            for item in range(4):
+                rows = pl.ds(pl.multiple_of((quarter * 4 + item) * 128 + sequence * 64, 64), 64)
+                proj_ref[rows, :] = product[item * 64 : item * 64 + 64]
+            return inner
+
+        lax.fori_loop(0, 4, project, 0)
+        at_steps(sequence, {0: [ready]})
+        mixer_forward(
+            proj_ref, pos_ref, taps_ref, gain_ref,
+            heads_ref, query_ref, key_ref, inv_ref, kc_ref, score_ref, step_ref, state_ref, update_ref, raw_ref,
+            free_ref, shift_ref, sequence,
+            lambda: at_steps(sequence, {0: [a[1].fifth, everything.second, wide.relay], 1: [everything.fourth]}),
+        )
+        at_steps(sequence, {
+            0: [exchanges[0].start, everything.third],
+            1: [exchanges[1].start, everything.fifth],
+        })
         return carry
 
-    lax.fori_loop(0, 8, project, 0)
-    keep = pltpu.make_async_copy(tokens, gathered_ref, local.at[2])
-    keep.start()
-    wide.relay()
-    out_own.wait()
-    outs.arrive()
-    out_gather = Gather(near, out_full_ref, all_send, all_recv)
-    out_gather.start()
-    tiny.arrive()
-    two.arrive()
-    total_ref[...] = jnp.sum(count_rows[...], 0)
-    table = jnp.sum(small[...].astype(jnp.float32), 0)
-    for tap in range(4):
-        for field in range(3):
-            taps_ref[tap : tap + 1, field * 128 : field * 128 + 128] = table[tap * 3 + field : tap * 3 + field + 1]
-    gain_ref[0:1, :] = table[12:13]
-    mixer_forward(
-        proj_ref, pos_ref, taps_ref, gain_ref,
-        heads_ref, query_ref, key_ref, inv_ref, kc_ref, score_ref, step_ref, state_ref, update_ref, raw_ref,
-        free_ref, shift_ref, out_gather.second, out_gather.third,
-    )
-
-    def head_rows(block):
-        return heads_ref.at[pl.ds(pl.multiple_of(block * 128, 128), 128)]
-
-    exchange = Fan("tensor", 16, head_rows, lambda index: spread_ref.at[index], head_send, head_recv)
-    exchange.start()
+    lax.fori_loop(0, 2, per_sequence, 0)
     spread_ref[tensor] = heads_ref[pl.ds(pl.multiple_of(tensor * 128, 128), 128)]
-    out_gather.fourth()
-    out_gather.fifth()
-    exchange.arrive()
-    for name in NAMES:
-        out_gather.from_twin(name)
+    everything.from_twin(*NAMES)
     wide.arrive()
     wide_own.wait()
     keep.wait()
-    for part in (gather, mix, wide, tiny, outs, one, two, out_gather, exchange):
-        part.finish()
+    for exchange in exchanges:
+        exchange.arrive()
+    for item in (a[0], a[1], mix, wide, tiny, outs, one, two, everything, exchanges[0], exchanges[1]):
+        item.finish()
 
 
 def dma(*counts):
@@ -1143,7 +1212,7 @@
             pltpu.VMEM((16, CHUNK, CHUNK), full),
             pltpu.VMEM((16, CHUNK, CHUNK), full),
         ]
-        + dma(17, 17, 7, 7, 7, 7, 8, 8, 8, 8, 17, 17, 16, 16, 8, 8, 16, 16, 3),
+        + dma(7, 7, 7, 7, 8, 8, 8, 8, 17, 17, 16, 16, 8, 8, 3, 17, 17, 17, 17, 16, 16, 16, 16),
         compiler_params=pltpu.CompilerParams(
             collective_id=2, has_side_effects=True, vmem_limit_bytes=62 << 20
         ),
@@ -1165,15 +1234,12 @@
     part, twin_part, slot, ffn_own, ffn_slot, ffn_staged, parts, part_slot, part_staged, proj_t, tile,
     sums, sum_rows,
     head_send, head_recv, gather_send, gather_recv, ffn_send, ffn_recv, mix_send, mix_recv,
-    scatter_send, scatter_recv, sum_send, sum_recv, row_send, row_recv, local,
+    sum_send, sum_recv, row_send, row_recv, local, *sems,
 ):
     near = Neighbours()
     tensor, data = lax.axis_index("tensor"), lax.axis_index("dp")
     own = near.mine("own")
     place = DataPlace()
-
-    def lanes(block):
-        return pl.ds(pl.multiple_of(block * 256, 256), 256)
 
     loads = [
         pltpu.make_async_copy(ffn_part_ref.at[:, lanes(place.block(0, other))], ffn_own.at[other], local.at[other])
@@ -1198,34 +1264,42 @@
     ffn.start()
     grad[pl.ds(pl.multiple_of(tensor * 128, 128), 128)] = heads_grad_ref[tensor]
     exchange.arrive()
-    mixer_backward(
-        grad, proj_ref, pos_ref, taps_ref, gain_ref,
-        query_ref, key_ref, inv_ref, kc_ref, score_ref, step_ref, state_ref, update_ref, raw_ref,
-        proj_low, taps_grad, gain_grad,
-        back_ref, pull_ref, flow_ref, enter_ref, pre_ref, gather.second, gather.third,
-    )
-    gather.fourth()
+    taps_grad[...] = jnp.zeros_like(taps_grad)
+    gain_grad[...] = jnp.zeros_like(gain_grad)
+    scatters = [
+        Scatter(near, part, twin_part, slot, sems[2 * h], sems[2 * h + 1], HALVES[h]) for h in range(2)
+    ]
+
+    def per_sequence(sequence, carry):
+        mixer_backward(
+            grad, proj_ref, pos_ref, taps_ref, gain_ref,
+            query_ref, key_ref, inv_ref, kc_ref, score_ref, step_ref, state_ref, update_ref, raw_ref,
+            proj_low, taps_grad, gain_grad,
+            back_ref, pull_ref, flow_ref, enter_ref, pre_ref, sequence,
+            lambda: at_steps(sequence, {}),
+            lambda: at_steps(sequence, {0: [gather.second], 1: [gather.third, scatters[0].second]}),
+        )
+
+        def backward(step, inner):
+            quarter = near.quarter_at(step)
+            pieces = []
+            for item in range(4):
+                rows = pl.ds(pl.multiple_of((quarter * 4 + item) * 128 + sequence * 64, 64), 64)
+                pieces.append(proj_low[rows, :])
+            values = jnp.concatenate(pieces, 0)
+            keep = lax.broadcasted_iota(jnp.int32, (256, WIDE), 1) <= 384
+            proj_t[:, rows_of(sequence, quarter)] = values.T[:400]
+            partial = low(nt(jnp.where(keep, values, jnp.zeros_like(values)), mix_ref[...]))
+            scatter_quarter(scatters, sequence, quarter, partial, part)
+            return inner
+
+        lax.fori_loop(0, 4, backward, 0)
+        at_steps(sequence, {0: [scatters[0].first], 1: [gather.fourth, scatters[1].first]})
+        return carry
+
+    lax.fori_loop(0, 2, per_sequence, 0)
     units = pltpu.make_async_copy(unit_ref, enter_ref, local.at[4])
     units.start()
-    scatter = Scatter(near, part, twin_part, slot, scatter_send, scatter_recv)
-
-    def backward(step, carry):
-        chip = near.chip_at(step)
-        rows = pl.ds(pl.multiple_of(chip * 256, 256), 256)
-        values = proj_low[rows, :]
-        keep = lax.broadcasted_iota(jnp.int32, (256, WIDE), 1) <= 384
-        partial = low(nt(jnp.where(keep, values, jnp.zeros_like(values)), mix_ref[...]))
-        proj_t[:, rows] = values.T[:400]
-        part[chip * 2] = partial[:128]
-        part[chip * 2 + 1] = partial[128:]
-        scatter.to_twin(chip)
-        return carry
-
-    lax.fori_loop(0, 8, backward, 0)
-    gather.fifth()
-    for name in NAMES:
-        gather.from_twin(name)
-    scatter.first()
 
     def fetch(step):
         return pltpu.make_async_copy(gathered_ref.at[:, :, lanes(step)], tile.at[step % 2], local.at[2 + step % 2])
@@ -1238,18 +1312,22 @@
         def _():
             fetch(step + 1).start()
 
-        @pl.when(step == 3)
-        def _():
-            scatter.second()
-
         fetch(step).wait()
-        column = tile[step % 2].reshape(2048, 256)
+        first = tile[step % 2, :, 0:64].reshape(1024, 256)
+        column = jnp.concatenate([first, tile[step % 2, :, 64:128].reshape(1024, 256)], 0)
         product = nn(proj_t[...], column)
         parts[0:400, lanes(step)] = low(product)
+        at_steps(step, {3: [scatters[0].third], 5: [gather.fifth], 7: [scatters[1].second]})
+        return carry
+
+    lax.fori_loop(0, 8, weights, 0)
+    gather.from_twin(*NAMES)
+
+    def out_weights(step, carry):
         parts[400:528, lanes(step)] = low(tn(heads_ref[...], attention[:, :, lanes(step)].reshape(2048, 256)))
         return carry
 
-    lax.fori_loop(0, 8, weights, 0)
+    lax.fori_loop(0, 8, out_weights, 0)
     pick_row = lax.broadcasted_iota(jnp.int32, (CHUNK, 2048), 0)
     pick_lane = lax.broadcasted_iota(jnp.int32, (CHUNK, 2048), 1)
     wanted = (pick_lane // 256) * 16 + pick_lane % 256
@@ -1270,28 +1348,31 @@
         part_slot, part_staged, mix_send, mix_recv,
     )
     mix.start()
-    scatter.third()
     for copy in loads:
         copy.wait()
+    units.wait()
+    scatters[1].third()
     ffn.relay()
-    scatter.fourth()
-    units.wait()
-
-    def ending(index, total):
-        rows = pl.ds(pl.multiple_of(index * 16, 16), 16)
-        value = scatter.total(rows)
-        attn_ref[rows] = value
-        unit = jnp.concatenate([enter_ref[piece, rows] for piece in range(16)], 1)
-        return total + value * unit
-
-    total = lax.fori_loop(0, 8, ending, jnp.zeros((16, 2048), jnp.float32))
+
+    def ending(half):
+        def piece(index, total):
+            rows = pl.ds(pl.multiple_of(half * 64 + index * 16, 16), 16)
+            value = scatters[half].total(rows)
+            attn_ref[rows] = value
+            return total + value * jnp.concatenate([enter_ref[block, rows] for block in range(16)], 1)
+
+        scatters[half].fourth()
+        return lax.fori_loop(0, 4, piece, jnp.zeros((16, 2048), jnp.float32))
+
+    total = ending(0)
+    mix.relay()
+    total = total + ending(1)
     total = jnp.sum(total, 0, keepdims=True)
     sums[tensor, 8:24] = sums_ref[8:24]
     for piece in range(8):
         sums[tensor, piece : piece + 1] = total[:, piece * 256 : piece * 256 + 256]
     one, two = tile_sum(sums, sum_rows, None, (sum_send, sum_recv, row_send, row_recv))
     one.start()
-    mix.relay()
     one.arrive()
     sum_rows[data] = jnp.sum(sums[...], 0)
     two.start()
@@ -1299,7 +1380,7 @@
     two.arrive()
     total_ref[...] = jnp.sum(sum_rows[...], 0)
     mix.result(weight_ref)
-    for item in (exchange, gather, ffn, scatter, mix, one, two):
+    for item in (exchange, gather, ffn, scatters[0], scatters[1], mix, one, two):
         item.finish()
 
 
@@ -1327,7 +1408,7 @@
             pltpu.VMEM((16, CHUNK, CHUNK), full),
             pltpu.VMEM((16, CHUNK, CHUNK), half),
             pltpu.VMEM((16, CHUNK, CHUNK), full),
-            pltpu.VMEM((2048, 384), full),
+            pltpu.VMEM((1024, 384), full),
             pltpu.VMEM((16, 128, 2048), half),
             pltpu.VMEM((8, 128, 2048), half),
             pltpu.VMEM((7, 128, 2048), half),
@@ -1342,7 +1423,7 @@
             pltpu.VMEM((16, 24, 256), full),
             pltpu.VMEM((8, 24, 256), full),
         ]
-        + dma(16, 16, 17, 17, 7, 7, 7, 7, 16, 16, 16, 16, 8, 8, 5),
+        + dma(16, 16, 17, 17, 7, 7, 7, 7, 16, 16, 8, 8, 5, 16, 16, 16, 16),
         compiler_params=pltpu.CompilerParams(
             collective_id=3, has_side_effects=True, vmem_limit_bytes=63 << 20
         ),

time: 498 us -> 429 us (0.86)
  Pallas kernels: 431 us -> 362 us
    pallas_call x1, Pallas kernels: 194 us -> 153 us  [run_ffn(): pl.pallas_call(ffn_kernel, out_shape=(jax.ShapeDtypeStruct((rows, feature...]
    pallas_call x1, Pallas kernels: 125 us -> 98.6 us  [run_entry(): pl.pallas_call(entry_kernel, out_shape=(shape((16, 128, 2048), half), sha...]
where the time goes in v4:
time: 429 us; the launch traced here: 428 us
  Pallas kernels  362 us (84%)
  local copies, waits for them, and re-layouts  26.3 us (6%)
  other arithmetic  22.7 us (5%)
  matrix products  11.6 us (3%)
  between operations  4.69 us (1%)
    pallas_call x1, Pallas kernels, run_ffn(): pl.pallas_call(ffn_kernel, out_shape=(jax.ShapeDtypeStruct((rows, feature...  153 us
    pallas_call x1, Pallas kernels, run_exit(): pl.pallas_call(exit_kernel, out_shape=(shape((128, 2048), full), shape((2...  111 us
    pallas_call x1, Pallas kernels, run_entry(): pl.pallas_call(entry_kernel, out_shape=(shape((16, 128, 2048), half), sha...  98.6 us
    unnamed x45, local copies, waits for them, and re-layouts  9.02 us

profile of v4, /device:TPU:0, one launch (start us, length us, event | category | flops | bytes accessed | tf_op | source)
XLA Modules:
  0.0 427.6 jit_solution(1817396500958932752)
XLA Ops:
  0.6 1.2 multiply_reduce_fusion.4
  2.0 2.0 multiply_convert_fusion.1.normed_ref
  4.0 1.9 convert_reduce_fusion
  6.5 1.4 fusion.13
  9.2 1.1 copy.60
  10.3 1.1 copy.61
  12.2 1.1 copy.56
  17.0 98.6 %entry.1 = (bf16[16,128,2048]{2,1,0:T(8,128)(2,1)}, bf16[2048,512]{1,0:T(8,128)(2,1)}, f32[8,384]{1,0:T(8,128)}, f32[8,128]{1,0:T(8,128)}, f32[8,128]{1,0:T(8,12...) custom-call(bf16[128,2048]{1,0:T(8,128)(2,1)} %multiply_convert_fusi, ...), custom_call_target="tpu_custom_call" | custom-call | flops 64424509440 | bytes 16777216 | tf_op jit(solution)/shard_map/entry/pallas_call | solution.py:1190
  115.8 5.4 %multiply_reduce_fusion.3 = (f32[128]{0:T(128)S(1)}, f32[128,2048]{1,0:T(8,128)S(1)}) fusion(f32[128,2048]{1,0:T(8,128)S(1)} %bitcast.65, bf16[16,128,2048]{2,1,0:T(8,128)(2,1)} %get-tuple-element.43, bf16[16,128,128]{2,1,0:T(8,128)(2,1)} %get-tuple-element.42), kind=kOutput, calls=%fused_computation.13 | convolution fusion | flops 1074528128 | bytes 11010560 | tf_op jit(solution)/shard_map/dot_general | solution.py:15
  123.1 1.2 slice.42
  126.7 152.6 %feed_forward.1 = (bf16[128,2048]{1,0:T(8,128)(2,1)}, f32[128,2048]{1,0:T(8,128)}, f32[128,2048]{1,0:T(8,128)}, f32[8,128]{1,0:T(8,128)}, bf16[768,2048]{1,0:T(8,128)(2,1)}, /*index=5*/f32[384,256]{1,0:T(8,128)}) custom-call(bf16[128,2048]{1,0:T(8,128)(2,1)} %multiply_convert_fusion.input_ref, f32[128,2048]{1,0:T(8,128)} %copy-done, ...), custom_call_target="tpu_custom_call" | custom-call | flops 171798691840 | bytes 16777216 | tf_op jit(solution)/shard_map/feed_forward/pallas_call | solution.py:859
  279.3 1.9 multiply_reduce_fusion.1
  281.2 1.3 slice.43
  283.9 3.1 fusion.12
  287.9 6.3 %convolution_convert_fusion = bf16[128,2048]{1,0:T(8,128)(2,1)S(1)} fusion(bf16[128,2048]{1,0:T(8,128)(2,1)S(1)} %get-tuple-element.125.attention_ref, bf16[2048,2048]{1,0:T(8,128)(2,1)} %bitcast.64), kind=kOutput, calls=%fused_computation.3 | convolution fusion | flops 1074003968 | bytes 9437184 | tf_op jit(solution)/shard_map/dot_general | solution.py:19
  295.7 1.3 fusion.1.unit_ref
  297.0 111.0 %exit.1 = (f32[128,2048]{1,0:T(8,128)}, f32[768,256]{1,0:T(8,128)}, f32[528,256]{1,0:T(8,128)}, f32[24,256]{1,0:T(8,128)}) custom-call(bf16[16,128,128]{2,1,0:T(8,128)(2,1)} %bitcast.74, bf16[128,2048]{1,0:T(8,128)(2,1)} %copy-done.5, bf16[768,2048]{1,0:T(8,128)(2,1)} %get-tuple-element.49.ffn_part_ref, ...), custom_call_target="tpu_custom_call" | custom-call | flops 64424509440 | bytes 16777216 | tf_op jit(solution)/shard_map/exit/pallas_call | solution.py:1391
  408.1 1.6 multiply_reduce_fusion
  409.7 2.9 multiply_add_fusion
  412.6 1.0 slice.46
  414.5 2.0 slice_bitcast_fusion
  416.5 1.6 slice.50
  422.4 1.3 slice_bitcast_fusion.4
  423.7 1.2 slice.49
  (81 shorter events, 18.9 us)
Async XLA Ops:
  2.0 6.6 %copy-start.13 = (f32[128]{0:T(128)}, f32[128]{0:T(128)S(1)}, u32[]{:S(2)}) copy-start(f32[128]{0:T(128)S(1)} %rsqrt.20) | copy-start | bytes 1540
  17.0 98.6 %copy-start.1 = (bf16[2,64,2048]{2,1,0:T(8,128)(2,1)S(1)}, bf16[2,64,2048]{2,1,0:T(8,128)(2,1)}, u32[]{:S(2)}) copy-start(bf16[2,64,2048]{2,1,0:T(8,128)(2,1)} %param.14) | copy-start | bytes 1572868
  115.7 6.5 %copy-start.10 = (f32[2048]{0:T(1024)S(1)}, f32[2048]{0:T(1024)}, u32[]{:S(2)}) copy-start(f32[2048]{0:T(1024)} %param.24) | copy-start | bytes 24580
  115.8 7.3 %copy-start.3 = (f32[2,64,2048]{2,1,0:T(8,128)}, f32[2,64,2048]{2,1,0:T(8,128)S(1)}, u32[]{:S(2)}) copy-start(f32[2,64,2048]{2,1,0:T(8,128)S(1)} %convert_element_type.84) | copy-start | bytes 3145732
  115.8 10.0 %copy-start.8 = (bf16[352,256]{1,0:T(8,128)(2,1)S(1)}, bf16[352,256]{1,0:T(8,128)(2,1)}, u32[]{:S(2)}) copy-start(bf16[352,256]{1,0:T(8,128)(2,1)} %param.27) | copy-start | bytes 540676
  121.2 1.0 copy-start
  122.1 1.0 copy-start.15
  126.7 152.6 %copy-start.11 = (f32[2048]{0:T(1024)S(1)}, f32[2048]{0:T(1024)}, u32[]{:S(2)}) copy-start(f32[2048]{0:T(1024)} %param.24) | copy-start | bytes 24580
  126.7 152.6 %copy-start.16 = (f32[128]{0:T(128)S(1)}, f32[128]{0:T(128)}, u32[]{:S(2)}) copy-start(f32[128]{0:T(128)} %copy-done.15) | copy-start | bytes 1540
  281.2 14.3 %copy-start.4 = (f32[2,64,2048]{2,1,0:T(8,128)S(1)}, f32[2,64,2048]{2,1,0:T(8,128)}, u32[]{:S(2)}) copy-start(f32[2,64,2048]{2,1,0:T(8,128)} %copy-done.3) | copy-start | bytes 3145732
  283.9 11.7 %copy-start.14 = (f32[128]{0:T(128)S(1)}, f32[128]{0:T(128)}, u32[]{:S(2)}) copy-start(f32[128]{0:T(128)} %copy-done.13) | copy-start | bytes 1540
  287.1 0.8 copy-start.5
  297.0 111.1 %copy-start.2 = (bf16[2,64,2048]{2,1,0:T(8,128)(2,1)S(1)}, bf16[2,64,2048]{2,1,0:T(8,128)(2,1)}, u32[]{:S(2)}) copy-start(bf16[2,64,2048]{2,1,0:T(8,128)(2,1)} %param.14) | copy-start | bytes 1572868
  297.0 111.1 %copy-start.9 = (f32[2048]{0:T(1024)S(1)}, f32[2048]{0:T(1024)}, u32[]{:S(2)}) copy-start(f32[2048]{0:T(1024)} %param.18) | copy-start | bytes 24580
  408.0 10.0 %copy-start.12 = (f32[24,256]{1,0:T(8,128)S(1)}, f32[24,256]{1,0:T(8,128)}, u32[]{:S(2)}) copy-start(f32[24,256]{1,0:T(8,128)} %get-tuple-element.66) | copy-start | bytes 73732
  408.0 16.8 %copy-start.7 = (f32[384,256]{1,0:T(8,128)S(1)}, f32[384,256]{1,0:T(8,128)}, u32[]{:S(2)}) copy-start(f32[384,256]{1,0:T(8,128)} %get-tuple-element.70) | copy-start | bytes 1179652
  408.0 17.6 %copy-start.6 = (bf16[128,2048]{1,0:T(8,128)(2,1)S(1)}, bf16[128,2048]{1,0:T(8,128)(2,1)}, u32[]{:S(2)}) copy-start(bf16[128,2048]{1,0:T(8,128)(2,1)} %get-tuple-element.46) | copy-start | bytes 1572868

commit v5 on v4

--- a/solution.py
+++ b/solution.py
@@ -633,6 +633,32 @@
             self.outgoing(key).wait_send()
 
 
+def strips(count, body, start=0):
+    def piece(index, carry):
+        return body(pl.ds(pl.multiple_of(start + index * 16, 16), 16), carry)
+
+    return lambda carry: lax.fori_loop(0, count // 16, piece, carry)
+
+
+def normalise(values):
+    scale = lax.rsqrt(jnp.mean(values * values, -1, keepdims=True) + 1e-06)
+    return values * scale, scale
+
+
+def norm_into(source, gain_ref, target):
+    def strip(rows, carry):
+        unit, _ = normalise(source[rows].astype(jnp.float32))
+        target[rows] = low(unit * gain_ref[0:1, :])
+        return carry
+
+    strips(128, strip)(0)
+
+
+def norm_back(values, unit, scale, gain_ref):
+    inner = values * gain_ref[0:1, :]
+    return scale * (inner - unit * jnp.mean(inner * unit, -1, keepdims=True))
+
+
 def at_steps(step, table):
     for moment, actions in table.items():
 
@@ -651,6 +677,7 @@
 
 
 HIDDEN = 384
+FF_UNITS = 352
 
 
 def sigmoid(value):
@@ -689,9 +716,10 @@
 
 
 def ffn_kernel(
-    input_ref, hidden_ref, teacher_ref, mask_ref, gate_up_ref, down_shard_ref,
-    block_ref, grad_ref, back_ref, square_ref, weight_ref, down_grad_ref,
+    hidden_ref, mlp_gain_ref, teacher_ref, mask_ref, gate_up_src, down_shard_ref,
+    block_ref, back_ref, back_low_ref, sums_ref, weight_ref, down_grad_ref,
     tokens, grads, both, act_t, both_t, part, twin_part, slot, down_ref, down_part, down_slot, down_staged,
+    grad_ref, square_ref, gain_sum, gate_up_ref, local,
     down_send, down_recv, leave_send, leave_recv, *sems,
 ):
     near = Neighbours()
@@ -699,8 +727,21 @@
     neighbours = [{"tensor": device} for device in (near.up, near.down, near.side, near.twin)]
     neighbours = neighbours + [{"dp": device} for device in data_neighbours()]
     own = near.mine("own")
-    tokens[own] = input_ref[...]
-    down_ref[lanes(data)] = down_shard_ref[...]
+    norm_into(hidden_ref, mlp_gain_ref, tokens.at[own])
+    fills = [
+        pltpu.make_async_copy(
+            gate_up_src.at[index * FF_UNITS : index * FF_UNITS + FF_UNITS],
+            gate_up_ref.at[index * HIDDEN : index * HIDDEN + FF_UNITS], local.at[index],
+        )
+        for index in range(2)
+    ]
+    for fill in fills:
+        fill.start()
+    blank = jnp.zeros((HIDDEN - FF_UNITS, 2048), jnp.bfloat16)
+    gate_up_ref[FF_UNITS:HIDDEN] = blank
+    gate_up_ref[HIDDEN + FF_UNITS : 2 * HIDDEN] = blank
+    down_ref[FF_UNITS:HIDDEN] = blank
+    down_ref[0:FF_UNITS, lanes(data)] = down_shard_ref[...]
     greet(neighbours)
     a, g = (
         [Gather(near, buffer, sems[k + 2 * h], sems[k + 2 * h + 1], HALVES[h]) for h in range(2)]
@@ -711,8 +752,10 @@
         for k in (8, 12)
     )
     a[0].start()
-    down = DataGather(down_shard_ref, lambda block: down_ref.at[lanes(block)], down_send, down_recv)
+    down = DataGather(down_shard_ref, lambda block: down_ref.at[0:FF_UNITS, lanes(block)], down_send, down_recv)
     down.start()
+    for fill in fills:
+        fill.wait()
 
     def forward(step, carry):
         at_steps(step, {
@@ -730,16 +773,17 @@
         })
         half, quarter = step // 4, near.quarter_at(step)
         rows = rows_of(half, quarter)
-        product = nn(quarter_rows(tokens, half, quarter), gate_up_ref[...])
+        product = nt(quarter_rows(tokens, half, quarter), gate_up_ref[...])
         both[rows, :] = product
         gate, up = product[:, :HIDDEN], product[:, HIDDEN:]
         act = low(gate * sigmoid(gate) * up)
         act_t[:, rows] = act.T
-        scatter_quarter(r, half, quarter, low(nt(act, down_ref[...])), part)
+        scatter_quarter(r, half, quarter, low(nn(act, down_ref[...])), part)
         return carry
 
     lax.fori_loop(0, 8, forward, 0)
     square_ref[...] = jnp.zeros_like(square_ref)
+    gain_sum[...] = jnp.zeros_like(gain_sum)
 
     def middle(half):
         def piece(index, carry):
@@ -790,14 +834,14 @@
         })
         half, quarter = step // 4, near.quarter_at(step)
         rows = rows_of(half, quarter)
-        act_grad = nn(quarter_rows(grads, half, quarter), down_ref[...])
+        act_grad = nt(quarter_rows(grads, half, quarter), down_ref[...])
         gate, up = both[rows, :HIDDEN], both[rows, HIDDEN:]
         sigma = sigmoid(gate)
         gate_low = low(act_grad * up * sigma * (1.0 + gate * (1.0 - sigma)))
         up_low = low(act_grad * gate * sigma)
         both_low = jnp.concatenate([gate_low, up_low], 1)
         both_t[:, rows] = both_low.T
-        scatter_quarter(b, half, quarter, low(nt(both_low, gate_up_ref[...])), part)
+        scatter_quarter(b, half, quarter, low(nn(both_low, gate_up_ref[...])), part)
         return carry
 
     lax.fori_loop(0, 8, backward, 0)
@@ -824,7 +868,12 @@
 
         def piece(index, carry):
             rows = pl.ds(pl.multiple_of(half * 64 + index * 16, 16), 16)
-            back_ref[rows] = b[half].total(rows)
+            value = b[half].total(rows)
+            unit, scale = normalise(hidden_ref[rows])
+            gain_sum[...] += value * unit
+            grad = grad_ref[rows] + norm_back(value, unit, scale, mlp_gain_ref)
+            back_ref[rows] = grad
+            back_low_ref[rows] = low(grad)
             return carry
 
         lax.fori_loop(0, 4, piece, 0)
@@ -840,6 +889,11 @@
     b[1].to_up()
     leave.relay()
     ending(1)
+    total = jnp.sum(gain_sum[...], 0, keepdims=True)
+    sums_ref[0:8, :] = jnp.zeros((8, 256), jnp.float32)
+    for piece in range(8):
+        sums_ref[8 + piece : 9 + piece, :] = total[:, piece * 256 : piece * 256 + 256]
+    sums_ref[16:24, :] = jnp.concatenate([square_ref[...], square_ref[...]], 1)
     leave.result(down_grad_ref)
     for item in (down, leave, a[0], a[1], g[0], g[1], b[0], b[1]):
         item.finish()
@@ -850,8 +904,8 @@
     return [place.block(shift, 0) for shift in range(1, 4)] + [place.block(0, 1)]
 
 
-def run_ffn(ffn_in, hidden, teacher, mask, gate_up, down_shard):
-    rows, features = ffn_in.shape
+def run_ffn(hidden, gain, teacher, mask, gate_up, down_shard):
+    rows, features = hidden.shape
     wide = jax.ShapeDtypeStruct((rows, features), jnp.float32)
     vmem = pl.BlockSpec(memory_space=pltpu.VMEM)
     counts = [7] * 4 + [Gather.copies] * 8 + [Scatter.copies] * 8
@@ -861,12 +915,12 @@
         out_shape=(
             jax.ShapeDtypeStruct((rows, features), jnp.bfloat16),
             wide,
-            wide,
-            jax.ShapeDtypeStruct((8, 128), jnp.float32),
+            jax.ShapeDtypeStruct((rows, features), jnp.bfloat16),
+            jax.ShapeDtypeStruct((24, 256), jnp.float32),
             jax.ShapeDtypeStruct((2 * HIDDEN, features), jnp.bfloat16),
             jax.ShapeDtypeStruct((HIDDEN, 256), jnp.float32),
         ),
-        in_specs=[vmem] * 6,
+        in_specs=[vmem] * 4 + [pl.BlockSpec(memory_space=pl.ANY), vmem],
         out_specs=[vmem] * 6,
         scratch_shapes=[
             pltpu.VMEM((16, 128, 2048), jnp.bfloat16),
@@ -877,10 +931,15 @@
             pltpu.VMEM((16, 128, 2048), jnp.bfloat16),
             pltpu.VMEM((8, 128, 2048), jnp.bfloat16),
             pltpu.VMEM((7, 128, 2048), jnp.bfloat16),
-            pltpu.VMEM((2048, HIDDEN), jnp.bfloat16),
+            pltpu.VMEM((HIDDEN, 2048), jnp.bfloat16),
             pltpu.VMEM((HIDDEN, 2048), jnp.bfloat16),
             pltpu.VMEM((7, HIDDEN, 256), jnp.bfloat16),
             pltpu.VMEM((HIDDEN, 256), jnp.bfloat16),
+            pltpu.VMEM((128, 2048), jnp.float32),
+            pltpu.VMEM((8, 128), jnp.float32),
+            pltpu.VMEM((16, 2048), jnp.float32),
+            pltpu.VMEM((2 * HIDDEN, 2048), jnp.bfloat16),
+            pltpu.SemaphoreType.DMA((2,)),
         ]
         + semaphores,
         compiler_params=pltpu.CompilerParams(
@@ -888,7 +947,7 @@
         ),
         cost_estimate=pl.CostEstimate(flops=160 << 30, bytes_accessed=16 << 20, transcendentals=0),
         name="feed_forward",
-    )(ffn_in, hidden, teacher, mask, gate_up, down_shard)
+    )(hidden, gain, teacher, mask, gate_up, down_shard)
 
 
 def everyone():
@@ -1047,10 +1106,11 @@
 
 
 def entry_kernel(
-    normed_ref, mix_ref, small_ref, count_ref, pos_ref, gate_up_ref, out_ref,
-    gathered_ref, mix_full_ref, taps_ref, gain_ref, total_ref, gate_up_full_ref, out_full_ref,
-    proj_ref, spread_ref, heads_ref,
-    query_ref, key_ref, inv_ref, kc_ref, score_ref, step_ref, state_ref, update_ref, raw_ref,
+    input_ref, attn_gain_ref, mix_ref, small_ref, count_ref, pos_ref, gate_ref, up_ref, out_ref,
+    gathered_ref, taps_ref, gain_ref, total_ref, gate_up_full_ref, out_full_ref, spread_ref,
+    far0, far1, far2, far3, far4, far5, far6, far7, far8, far9, far10, far11,
+    proj_ref, mix_full_ref, heads_ref,
+    query_ref, key_ref, inv_ref, kc_ref, score_ref, step_ref, state_ref, update_ref, raw_ref, save_sems, mix_parts,
     tokens, small, counts, count_rows, free_ref, shift_ref,
     mix_send, mix_recv, wide_send, wide_recv, small_send, small_recv,
     out_send, out_recv, all_send, all_recv, count_send, count_recv, row_send, row_recv, local, *sems,
@@ -1060,33 +1120,42 @@
     own = near.mine("own")
     block_rows = pl.ds(pl.multiple_of(data * 256, 256), 256)
 
-    def rows_of_data(ref):
-        return lambda block: ref.at[pl.ds(pl.multiple_of(block * 256, 256), 256)]
+    def mix_rows(block):
+        return mix_parts.at[:, pl.ds(pl.multiple_of(block * 256, 256), 256)]
+
+    def gate_lanes(block):
+        return gate_up_full_ref.at[0:FF_UNITS, pl.ds(pl.multiple_of(block * 256, 256), 256)]
+
+    def up_lanes(block):
+        return gate_up_full_ref.at[FF_UNITS : 2 * FF_UNITS, pl.ds(pl.multiple_of(block * 256, 256), 256)]
 
     def lanes_of_data(block):
         return out_full_ref.at[tensor, :, pl.ds(pl.multiple_of(block * 256, 256), 256)]
 
-    wide_own = pltpu.make_async_copy(gate_up_ref, gate_up_full_ref.at[block_rows], local.at[0])
+    gate_own = pltpu.make_async_copy(gate_ref, gate_lanes(data), local.at[0])
+    up_own = pltpu.make_async_copy(up_ref, up_lanes(data), local.at[3])
     out_own = pltpu.make_async_copy(out_ref, lanes_of_data(data), local.at[1])
-    wide_own.start()
+    gate_own.start()
+    up_own.start()
     out_own.start()
-    tokens[own] = normed_ref[...]
-    mix_full_ref[block_rows] = mix_ref[...]
+    norm_into(input_ref, attn_gain_ref, tokens.at[own])
+    mix_parts[:, block_rows] = mix_ref[...]
     small[data] = small_ref[...]
     counts[tensor] = count_ref[...]
     greet(everyone())
     a = [Gather(near, tokens, sems[2 * h], sems[2 * h + 1], HALVES[h]) for h in range(2)]
-    mix = DataGather(mix_ref, rows_of_data(mix_full_ref), mix_send, mix_recv)
-    wide = DataGather(gate_up_ref, rows_of_data(gate_up_full_ref), wide_send, wide_recv)
+    mix = DataGather(mix_ref, mix_rows, mix_send, mix_recv)
+    wide = DataGather(gate_ref, gate_lanes, wide_send, wide_recv)
+    wide_up = DataGather(up_ref, up_lanes, sems[8], sems[9])
     tiny = Fan("dp", 8, lambda peer: small.at[data], lambda index: small.at[index], small_send, small_recv)
     outs = Fan("dp", 8, lambda peer: out_ref, lanes_of_data, out_send, out_recv)
     one, two = tile_sum(counts, count_rows, None, (count_send, count_recv, row_send, row_recv))
     everything = Gather(near, out_full_ref, all_send, all_recv)
     a[0].start()
     outs.start()
-    one.start()
     tiny.start()
     mix.start()
+    one.start()
 
     def counted():
         one.arrive()
@@ -1102,7 +1171,12 @@
         tiny.arrive()
         two.arrive()
         total_ref[...] = jnp.sum(count_rows[...], 0)
-        table = jnp.sum(small[...].astype(jnp.float32), 0)
+        table = jnp.sum(small[:, 0:16].astype(jnp.float32), 0)
+        for block in range(8):
+            for part in range(2):
+                line = small[block, 16:32].astype(jnp.float32)[part : part + 1]
+                first = block * 256 + part * 128
+                mix_full_ref[first : first + 128, 384:512] = low(jnp.broadcast_to(line, (128, 128)).T)
         for tap in range(4):
             for field in range(3):
                 row = tap * 3 + field
@@ -1122,17 +1196,31 @@
         Fan("tensor", 16, head_rows(h), target_rows(h), sems[4 + 2 * h], sems[5 + 2 * h]) for h in range(2)
     ]
     keep = pltpu.make_async_copy(tokens, gathered_ref, local.at[2])
+    saves = [
+        pltpu.make_async_copy(source, target, save_sems.at[index])
+        for index, (source, target) in enumerate(zip(
+            (
+                proj_ref, mix_full_ref, heads_ref, query_ref, key_ref, inv_ref, kc_ref, score_ref, step_ref,
+                state_ref, update_ref, raw_ref,
+            ),
+            (far0, far1, far2, far3, far4, far5, far6, far7, far8, far9, far10, far11),
+        ))
+    ]
     a[0].second()
     a[1].start()
+    outer()
     counted()
     mix.relay()
     a[0].third()
     a[0].fourth()
-    outer()
+    ready()
     a[1].second()
     a[0].fifth()
     mix.arrive()
     wide.start()
+    wide_up.start()
+    for field in range(3):
+        mix_full_ref[:, field * 128 : field * 128 + 128] = mix_parts[field]
 
     def per_sequence(sequence, carry):
         def project(step, inner):
@@ -1140,11 +1228,11 @@
                 0: [pair(a[0], ORDER[0])],
                 1: [pair(a[0], ORDER[1])],
                 2: [pair(a[0], ORDER[2])],
-                3: [a[1].third, a[1].fourth, pair(a[0], ORDER[3])],
+                3: [a[1].third, pair(a[0], ORDER[3])],
                 4: [pair(a[1], ORDER[0])],
                 5: [pair(a[1], ORDER[1])],
                 6: [pair(a[1], ORDER[2])],
-                7: [pair(a[1], ORDER[3]), keep.start],
+                7: [pair(a[1], ORDER[3]), keep.start, saves[1].start],
             })
             quarter = near.quarter_at(step)
             product = nn(quarter_rows(tokens, sequence, quarter), mix_full_ref[...])
@@ -1154,28 +1242,34 @@
             return inner
 
         lax.fori_loop(0, 4, project, 0)
-        at_steps(sequence, {0: [ready]})
         mixer_forward(
             proj_ref, pos_ref, taps_ref, gain_ref,
             heads_ref, query_ref, key_ref, inv_ref, kc_ref, score_ref, step_ref, state_ref, update_ref, raw_ref,
             free_ref, shift_ref, sequence,
-            lambda: at_steps(sequence, {0: [a[1].fifth, everything.second, wide.relay], 1: [everything.fourth]}),
+            lambda: at_steps(sequence, {0: [a[1].fourth, everything.second, wide.relay, wide_up.relay], 1: [everything.third, saves[0].start]}),
         )
         at_steps(sequence, {
-            0: [exchanges[0].start, everything.third],
-            1: [exchanges[1].start, everything.fifth],
+            0: [exchanges[0].start, a[1].fifth],
+            1: [exchanges[1].start, everything.fourth],
         })
         return carry
 
     lax.fori_loop(0, 2, per_sequence, 0)
     spread_ref[tensor] = heads_ref[pl.ds(pl.multiple_of(tensor * 128, 128), 128)]
+    for save in (saves[2:]):
+        save.start()
+    everything.fifth()
     everything.from_twin(*NAMES)
     wide.arrive()
-    wide_own.wait()
+    wide_up.arrive()
+    for save in saves:
+        save.wait()
+    gate_own.wait()
+    up_own.wait()
     keep.wait()
     for exchange in exchanges:
         exchange.arrive()
-    for item in (a[0], a[1], mix, wide, tiny, outs, one, two, everything, exchanges[0], exchanges[1]):
+    for item in (a[0], a[1], mix, wide, wide_up, tiny, outs, one, two, everything, exchanges[0], exchanges[1]):
         item.finish()
 
 
@@ -1183,7 +1277,17 @@
     return [pltpu.SemaphoreType.DMA((count,)) for count in counts]
 
 
-def run_entry(normed, mix_shard, small, count, pos, gate_up, out_weight):
+def kept_shapes():
+    shape = jax.ShapeDtypeStruct
+    rows = shape((2048, CHUNK), jnp.bfloat16)
+    return (shape((2048, WIDE), jnp.float32), shape((2048, WIDE), jnp.bfloat16), rows) + saved_shapes()
+
+
+def kept_buffers():
+    return [pltpu.VMEM(item.shape, item.dtype) for item in kept_shapes()]
+
+
+def run_entry(tokens, attn_gain, mix_shard, small, count, pos, gate_t, up_t, out_weight):
     vmem, hbm = pl.BlockSpec(memory_space=pltpu.VMEM), pl.BlockSpec(memory_space=pl.ANY)
     half, full = jnp.bfloat16, jnp.float32
     shape = jax.ShapeDtypeStruct
@@ -1191,50 +1295,51 @@
         entry_kernel,
         out_shape=(
             shape((16, 128, 2048), half),
-            shape((2048, WIDE), half),
             shape((8, 384), full),
             shape((8, CHUNK), full),
             shape((8, 128), full),
-            shape((2048, 2 * HIDDEN), half),
+            shape((2 * FF_UNITS, 2048), half),
             shape((16, 128, 2048), half),
-            shape((2048, WIDE), full),
             shape((16, 128, CHUNK), half),
-            shape((2048, CHUNK), half),
         )
-        + saved_shapes(),
-        in_specs=[vmem] * 5 + [hbm] * 2,
-        out_specs=[hbm, vmem, vmem, vmem, vmem, hbm, hbm] + [vmem] * 12,
-        scratch_shapes=[
+        + kept_shapes(),
+        in_specs=[vmem] * 6 + [hbm] * 3,
+        out_specs=[hbm, vmem, vmem, vmem, hbm, hbm, vmem] + [hbm] * 12,
+        scratch_shapes=kept_buffers()
+        + dma(12)
+        + [
+            pltpu.VMEM((3, 2048, CHUNK), half),
             pltpu.VMEM((16, 128, 2048), half),
-            pltpu.VMEM((8, 16, 128), half),
+            pltpu.VMEM((8, 32, 128), half),
             pltpu.VMEM((16, 8, 128), full),
             pltpu.VMEM((8, 8, 128), full),
             pltpu.VMEM((16, CHUNK, CHUNK), full),
             pltpu.VMEM((16, CHUNK, CHUNK), full),
         ]
-        + dma(7, 7, 7, 7, 8, 8, 8, 8, 17, 17, 16, 16, 8, 8, 3, 17, 17, 17, 17, 16, 16, 16, 16),
+        + dma(7, 7, 7, 7, 8, 8, 8, 8, 17, 17, 16, 16, 8, 8, 4, 17, 17, 17, 17, 16, 16, 16, 16, 7, 7),
         compiler_params=pltpu.CompilerParams(
             collective_id=2, has_side_effects=True, vmem_limit_bytes=62 << 20
         ),
         cost_estimate=pl.CostEstimate(flops=60 << 30, bytes_accessed=16 << 20, transcendentals=0),
         name="entry",
-    )(normed, mix_shard, small, count, pos, gate_up, out_weight)
+    )(tokens, attn_gain, mix_shard, small, count, pos, gate_t, up_t, out_weight)
 
 
 SMALL = 16
 
 
 def exit_kernel(
-    heads_grad_ref, attention_ref, ffn_part_ref, gathered_ref, proj_ref, pos_ref, taps_ref, gain_ref,
-    mix_ref, heads_ref, unit_ref, sums_ref,
-    query_ref, key_ref, inv_ref, kc_ref, score_ref, step_ref, state_ref, update_ref, raw_ref,
-    attn_ref, ffn_ref, weight_ref, total_ref,
+    out_full_ref, attention_ref, ffn_part_ref, gathered_ref, hidden_grad_ref, pos_ref, taps_ref, gain_ref, input_ref, attn_gain_ref, sums_ref,
+    far0, far1, far2, far3, far4, far5, far6, far7, far8, far9, far10, far11,
+    input_grad_ref, ffn_ref, qkv_grad_ref, small_grad_ref, out_grad_ref, total_ref,
+    proj_ref, mix_ref, heads_ref,
+    query_ref, key_ref, inv_ref, kc_ref, score_ref, step_ref, state_ref, update_ref, raw_ref, load_sems, weight_ref,
     grad, attention, proj_low, taps_grad, gain_grad,
     back_ref, pull_ref, flow_ref, enter_ref, pre_ref,
-    part, twin_part, slot, ffn_own, ffn_slot, ffn_staged, parts, part_slot, part_staged, proj_t, tile,
-    sums, sum_rows,
+    part, twin_part, slot, ffn_own, ffn_slot, ffn_staged, parts, part_slot, part_staged, outs, out_slot, out_staged,
+    proj_t, tile, sums, sum_rows,
     head_send, head_recv, gather_send, gather_recv, ffn_send, ffn_recv, mix_send, mix_recv,
-    sum_send, sum_recv, row_send, row_recv, local, *sems,
+    outs_send, outs_recv, sum_send, sum_recv, row_send, row_recv, local, *sems,
 ):
     near = Neighbours()
     tensor, data = lax.axis_index("tensor"), lax.axis_index("dp")
@@ -1247,13 +1352,35 @@
     ]
     for copy in loads:
         copy.start()
+    fill = pltpu.make_async_copy(out_full_ref, part, local.at[5])
+    fill.start()
+    sources = (far0, far1, far2, far3, far4, far5, far6, far7, far8, far9, far10, far11)
+    places = (
+        proj_ref, mix_ref, heads_ref, query_ref, key_ref, inv_ref, kc_ref, score_ref, step_ref, state_ref,
+        update_ref, raw_ref,
+    )
+    saves = [
+        pltpu.make_async_copy(source, target, load_sems.at[index])
+        for index, (source, target) in enumerate(zip(sources, places))
+    ]
+    for copy in saves:
+        copy.start()
+    base = pltpu.make_async_copy(hidden_grad_ref, input_grad_ref, local.at[4])
+    base.start()
     attention[own] = attention_ref[...]
     greet(everyone())
+    fill.wait()
+
+    def head_grads(head, carry):
+        flow_ref[head] = low(nt(attention_ref[...], part[head]))
+        return carry
+
+    lax.fori_loop(0, 16, head_grads, 0)
 
     def head_rows(block):
         return grad.at[pl.ds(pl.multiple_of(block * 128, 128), 128)]
 
-    exchange = Fan("tensor", 16, lambda peer: heads_grad_ref.at[peer], head_rows, head_send, head_recv)
+    exchange = Fan("tensor", 16, lambda peer: flow_ref.at[peer], head_rows, head_send, head_recv)
     exchange.start()
     gather = Gather(near, attention, gather_send, gather_recv)
     gather.start()
@@ -1262,8 +1389,11 @@
         ffn_slot, ffn_staged, ffn_send, ffn_recv,
     )
     ffn.start()
-    grad[pl.ds(pl.multiple_of(tensor * 128, 128), 128)] = heads_grad_ref[tensor]
+    grad[pl.ds(pl.multiple_of(tensor * 128, 128), 128)] = flow_ref[tensor]
     exchange.arrive()
+    exchange.finish()
+    for copy in saves:
+        copy.wait()
     taps_grad[...] = jnp.zeros_like(taps_grad)
     gain_grad[...] = jnp.zeros_like(gain_grad)
     scatters = [
@@ -1280,31 +1410,40 @@
             lambda: at_steps(sequence, {0: [gather.second], 1: [gather.third, scatters[0].second]}),
         )
 
+        def flip(step, inner):
+            quarter = near.quarter_at(step)
+            proj_t[:, rows_of(sequence, quarter)] = quarter_values(sequence, quarter).T[:400]
+            return inner
+
+        lax.fori_loop(0, 4, flip, 0)
+        at_steps(sequence, {0: [lambda: partials(0), scatters[0].first]})
+        return carry
+
+    def quarter_values(sequence, quarter):
+        pieces = []
+        for item in range(4):
+            rows = pl.ds(pl.multiple_of((quarter * 4 + item) * 128 + sequence * 64, 64), 64)
+            pieces.append(proj_low[rows, :])
+        return jnp.concatenate(pieces, 0)
+
+    def partials(sequence):
         def backward(step, inner):
             quarter = near.quarter_at(step)
-            pieces = []
-            for item in range(4):
-                rows = pl.ds(pl.multiple_of((quarter * 4 + item) * 128 + sequence * 64, 64), 64)
-                pieces.append(proj_low[rows, :])
-            values = jnp.concatenate(pieces, 0)
+            values = quarter_values(sequence, quarter)
             keep = lax.broadcasted_iota(jnp.int32, (256, WIDE), 1) <= 384
-            proj_t[:, rows_of(sequence, quarter)] = values.T[:400]
             partial = low(nt(jnp.where(keep, values, jnp.zeros_like(values)), mix_ref[...]))
             scatter_quarter(scatters, sequence, quarter, partial, part)
             return inner
 
         lax.fori_loop(0, 4, backward, 0)
-        at_steps(sequence, {0: [scatters[0].first], 1: [gather.fourth, scatters[1].first]})
-        return carry
 
     lax.fori_loop(0, 2, per_sequence, 0)
-    units = pltpu.make_async_copy(unit_ref, enter_ref, local.at[4])
-    units.start()
 
     def fetch(step):
         return pltpu.make_async_copy(gathered_ref.at[:, :, lanes(step)], tile.at[step % 2], local.at[2 + step % 2])
 
     fetch(0).start()
+    partials(1)
     table = jnp.concatenate([taps_grad[...], gain_grad[...]], 1)
 
     def weights(step, carry):
@@ -1317,17 +1456,10 @@
         column = jnp.concatenate([first, tile[step % 2, :, 64:128].reshape(1024, 256)], 0)
         product = nn(proj_t[...], column)
         parts[0:400, lanes(step)] = low(product)
-        at_steps(step, {3: [scatters[0].third], 5: [gather.fifth], 7: [scatters[1].second]})
+        at_steps(step, {1: [scatters[1].first], 3: [gather.fourth], 5: [scatters[0].third]})
         return carry
 
     lax.fori_loop(0, 8, weights, 0)
-    gather.from_twin(*NAMES)
-
-    def out_weights(step, carry):
-        parts[400:528, lanes(step)] = low(tn(heads_ref[...], attention[:, :, lanes(step)].reshape(2048, 256)))
-        return carry
-
-    lax.fori_loop(0, 8, out_weights, 0)
     pick_row = lax.broadcasted_iota(jnp.int32, (CHUNK, 2048), 0)
     pick_lane = lax.broadcasted_iota(jnp.int32, (CHUNK, 2048), 1)
     wanted = (pick_lane // 256) * 16 + pick_lane % 256
@@ -1348,24 +1480,40 @@
         part_slot, part_staged, mix_send, mix_recv,
     )
     mix.start()
+    scatters[1].second()
+    gather.fifth()
+    gather.from_twin(*NAMES)
+
+    def out_weights(step, carry):
+        outs[:, lanes(step)] = low(tn(heads_ref[...], attention[:, :, lanes(step)].reshape(2048, 256)))
+        return carry
+
+    lax.fori_loop(0, 8, out_weights, 0)
+    out_scatter = DataScatter(
+        lambda block: outs.at[:, lanes(block)],
+        lambda other, rows: outs[rows, lanes(place.block(0, other))],
+        out_slot, out_staged, outs_send, outs_recv,
+    )
+    out_scatter.start()
     for copy in loads:
         copy.wait()
-    units.wait()
+    ffn.relay()
+    base.wait()
+
+    def ending(half):
+        def strip(rows, total):
+            value = scatters[half].total(rows)
+            unit, scale = normalise(input_ref[rows].astype(jnp.float32))
+            input_grad_ref[rows] += norm_back(value, unit, scale, attn_gain_ref)
+            return total + value * unit
+
+        scatters[half].fourth()
+        return strips(64, strip, half * 64)(jnp.zeros((16, 2048), jnp.float32))
+
+    total = ending(0)
     scatters[1].third()
-    ffn.relay()
-
-    def ending(half):
-        def piece(index, total):
-            rows = pl.ds(pl.multiple_of(half * 64 + index * 16, 16), 16)
-            value = scatters[half].total(rows)
-            attn_ref[rows] = value
-            return total + value * jnp.concatenate([enter_ref[block, rows] for block in range(16)], 1)
-
-        scatters[half].fourth()
-        return lax.fori_loop(0, 4, piece, jnp.zeros((16, 2048), jnp.float32))
-
-    total = ending(0)
     mix.relay()
+    out_scatter.relay()
     total = total + ending(1)
     total = jnp.sum(total, 0, keepdims=True)
     sums[tensor, 8:24] = sums_ref[8:24]
@@ -1380,11 +1528,17 @@
     two.arrive()
     total_ref[...] = jnp.sum(sum_rows[...], 0)
     mix.result(weight_ref)
-    for item in (exchange, gather, ffn, scatters[0], scatters[1], mix, one, two):
+    for field in range(3):
+        qkv_grad_ref[field] = weight_ref[field * 128 : field * 128 + 128, :].T
+    small_grad_ref[...] = weight_ref[384:400, :]
+    out_scatter.result(out_grad_ref)
+    for item in (gather, ffn, scatters[0], scatters[1], mix, out_scatter, one, two):
         item.finish()
 
 
-def run_exit(heads_grad, attention, ffn_part, gathered, proj, pos, taps, gain, mix, heads, unit, sums, saved):
+def run_exit(
+    out_full, attention, ffn_part, gathered, hidden_grad, proj, pos, taps, gain, mix, heads, tokens, attn_gain, sums, saved
+):
     vmem, hbm = pl.BlockSpec(memory_space=pltpu.VMEM), pl.BlockSpec(memory_space=pl.ANY)
     half, full = jnp.bfloat16, jnp.float32
     shape = jax.ShapeDtypeStruct
@@ -1393,12 +1547,17 @@
         out_shape=(
             shape((128, 2048), full),
             shape((2 * HIDDEN, 256), full),
-            shape((528, 256), full),
+            shape((3, 256, CHUNK), full),
+            shape((16, 256), full),
+            shape((CHUNK, 256), full),
             shape((24, 256), full),
         ),
-        in_specs=[vmem] * 2 + [hbm] * 2 + [vmem] * 6 + [hbm] + [vmem] * 10,
-        out_specs=[vmem] * 4,
-        scratch_shapes=[
+        in_specs=[hbm, vmem] + [hbm] * 3 + [vmem] * 6 + [hbm] * 12,
+        out_specs=[vmem] * 6,
+        scratch_shapes=kept_buffers()
+        + dma(12)
+        + [
+            pltpu.VMEM((400, 256), full),
             pltpu.VMEM((2048, CHUNK), half),
             pltpu.VMEM((16, 128, 2048), half),
             pltpu.VMEM((2048, WIDE), half),
@@ -1415,21 +1574,27 @@
             pltpu.VMEM((2, 2 * HIDDEN, 256), half),
             pltpu.VMEM((7, 2 * HIDDEN, 256), half),
             pltpu.VMEM((2 * HIDDEN, 256), half),
-            pltpu.VMEM((528, 2048), half),
-            pltpu.VMEM((7, 528, 256), half),
-            pltpu.VMEM((528, 256), half),
+            pltpu.VMEM((400, 2048), half),
+            pltpu.VMEM((7, 400, 256), half),
+            pltpu.VMEM((400, 256), half),
+            pltpu.VMEM((CHUNK, 2048), half),
+            pltpu.VMEM((7, CHUNK, 256), half),
+            pltpu.VMEM((CHUNK, 256), half),
             pltpu.VMEM((400, 2048), half),
             pltpu.VMEM((2, 16, 128, 256), half),
             pltpu.VMEM((16, 24, 256), full),
             pltpu.VMEM((8, 24, 256), full),
         ]
-        + dma(16, 16, 17, 17, 7, 7, 7, 7, 16, 16, 8, 8, 5, 16, 16, 16, 16),
+        + dma(16, 16, 17, 17, 7, 7, 7, 7, 7, 7, 16, 16, 8, 8, 6, 16, 16, 16, 16),
         compiler_params=pltpu.CompilerParams(
             collective_id=3, has_side_effects=True, vmem_limit_bytes=63 << 20
         ),
         cost_estimate=pl.CostEstimate(flops=60 << 30, bytes_accessed=16 << 20, transcendentals=0),
         name="exit",
-    )(heads_grad, attention, ffn_part, gathered, proj, pos, taps, gain, mix, heads, unit, sums, *saved)
+    )(
+        out_full, attention, ffn_part, gathered, hidden_grad, pos, taps, gain, tokens, attn_gain, sums, proj, mix, heads,
+        *saved,
+    )
 
 
 def token_places(segment):
@@ -1437,10 +1602,6 @@
     before = jnp.sum((segment[:, None, :] < segment[:, :, None]).astype(jnp.int32), -1)
     place = jnp.arange(length, dtype=jnp.int32)[None, :] - before
     return jnp.transpose(place.reshape(2, 8, CHUNK), (1, 0, 2)).reshape(16, CHUNK).astype(jnp.float32)
-
-
-def pad_lanes(array, width):
-    return jnp.pad(array, ((0, 0), (0, width - array.shape[1])))
 
 
 def f32(value):
@@ -1458,68 +1619,45 @@
     small = jnp.concatenate([conv_taps.reshape(12, 16), head_gain.reshape(1, 16)], 0)
     lane = jnp.arange(CHUNK)[None, :] // 16 == lax.axis_index("dp")
     small = jnp.where(lane, jnp.tile(jnp.pad(small, ((0, 3), (0, 0))), (1, 8)), 0)
-    mix_shard = jnp.concatenate(
-        [qkv_weight.reshape(256, 384), jnp.broadcast_to(beta_weight, (256, CHUNK))], 1
-    )
-    gate_up_shard = jnp.concatenate([pad_lanes(gate_weight, HIDDEN), pad_lanes(up_weight, HIDDEN)], 1)
-    down_shard = pad_lanes(jnp.transpose(down_weight), HIDDEN)
+    small = jnp.concatenate([small, jnp.pad(beta_weight.reshape(2, CHUNK), ((0, 14), (0, 0)))], 0)
+    mix_shard = jnp.transpose(qkv_weight, (1, 0, 2))
+    gate_t, up_t = jnp.transpose(gate_weight), jnp.transpose(up_weight)
     count = jnp.broadcast_to(f32(jnp.sum(padding)), (8, 128))
 
-    tokens = f32(inputs.reshape(rows, features))
-    attn_scale = lax.rsqrt(jnp.mean(tokens * tokens, -1, keepdims=True) + 1e-06)
-    attn_unit = tokens * attn_scale
-    normed = (attn_unit * attn_gain).astype(jnp.bfloat16)
+    tokens = inputs.reshape(rows, features)
+    attn_gain_row = attn_gain.reshape(1, features)
+    mlp_gain_row = mlp_gain.reshape(1, features)
     pos = token_places(segment_ids)
     (
-        gathered, mix_full, taps, gain, total, gate_up, out_full, proj, spread, heads, *saved
-    ) = run_entry(normed, mix_shard, small, count, pos, gate_up_shard, out_weight)
-    out_full = out_full.reshape(features, features)
+        gathered, taps, gain, total, gate_up, out_full, spread, proj, mix_full, heads, *saved
+    ) = run_entry(tokens, attn_gain_row, mix_shard, small, count, pos, gate_t, up_t, out_weight)
     valid = total[0, 0]
     scale = 16 * 1024 / valid
     heads_rows = jnp.transpose(spread, (1, 0, 2)).reshape(rows, features)
-    hidden = tokens + nn(heads_rows, out_full)
-
-    mlp_scale = lax.rsqrt(jnp.mean(hidden * hidden, -1, keepdims=True) + 1e-06)
-    mlp_unit = hidden * mlp_scale
-    ffn_in = (mlp_unit * mlp_gain).astype(jnp.bfloat16)
+    hidden = f32(tokens) + nn(heads_rows, out_full.reshape(features, features))
+
     mask = f32(padding.reshape(rows, 1))
     masks = jnp.broadcast_to(jnp.stack([mask, scale * mask]), (2, rows, CHUNK))
-    output, block_grad, mlp_grad, square_tile, ffn_part, down_grad = run_ffn(
-        ffn_in, hidden, teacher.reshape(rows, features), masks, gate_up, down_shard
+    output, hidden_grad, attention_low, sums, ffn_part, down_grad = run_ffn(
+        hidden, mlp_gain_row, teacher.reshape(rows, features), masks, gate_up, down_weight
     )
-
-    mlp_sum = jnp.sum(mlp_grad * mlp_unit, 0)
-    mlp_inner = mlp_grad * mlp_gain
-    hidden_grad = block_grad + mlp_scale * (
-        mlp_inner - mlp_unit * jnp.mean(mlp_inner * mlp_unit, -1, keepdims=True)
-    )
-    attention_low = hidden_grad.astype(jnp.bfloat16)
-    heads_grad_rows = nt(attention_low, out_full).astype(jnp.bfloat16)
-    heads_grad = jnp.transpose(heads_grad_rows.reshape(rows, 16, CHUNK), (1, 0, 2))
-    sums = jnp.concatenate(
-        [jnp.zeros((8, 256)), mlp_sum.reshape(8, 256), jnp.broadcast_to(square_tile[0:1, 0:1], (8, 256))], 0
-    )
-    units = jnp.transpose(attn_unit.reshape(rows, 16, CHUNK), (1, 0, 2))
-    attn_grad, ffn_grads, mix_grads, totals = run_exit(
-        heads_grad, attention_low, ffn_part, gathered, proj, pos, taps, gain, mix_full, heads, units, sums, saved
-    )
-    attn_inner = attn_grad * attn_gain
-    input_grad = hidden_grad + attn_scale * (
-        attn_inner - attn_unit * jnp.mean(attn_inner * attn_unit, -1, keepdims=True)
+    input_grad, ffn_grads, qkv_grad, small_grads, out_grad, totals = run_exit(
+        out_full, attention_low, ffn_part, gathered, hidden_grad, proj, pos, taps, gain, mix_full, heads, tokens,
+        attn_gain_row, sums, saved,
     )
     loss = totals[16, 0] / (valid * features)
-    small_grad = mix_grads[385:398, :16]
+    small_grad = small_grads[1:14, :16]
     shape = (2, 64, features)
     return (
         output.reshape(shape),
         loss,
         input_grad.reshape(shape),
         totals[:8].reshape(features),
-        jnp.transpose(mix_grads[:384]).reshape(256, 3, CHUNK),
-        jnp.transpose(mix_grads[384:385]),
+        jnp.transpose(qkv_grad, (1, 0, 2)),
+        jnp.transpose(small_grads[0:1]),
         small_grad[:12].reshape(4, 3, 1, 16),
         small_grad[12:].reshape(1, 16),
-        mix_grads[400:],
+        out_grad,
         totals[8:16].reshape(features),
         jnp.transpose(ffn_grads[:hidden_units]),
         jnp.transpose(ffn_grads[HIDDEN : HIDDEN + hidden_units]),

time: 429 us -> 392 us (0.914)
  other arithmetic: 22.7 us -> 5.32 us
  Pallas kernels: 362 us -> 355 us
  local copies, waits for them, and re-layouts: 26.3 us -> 20.1 us
  matrix products: 11.6 us -> 5.8 us
    dot_general x1 -> x0, matrix products: 6.29 us -> none  [nt(): lax.dot_general(a, b, (((1,), (1,)), ((), ())), preferred_element_type=jn...]
    convert_element_type x3 -> x0, other arithmetic: 6.13 us -> none  [the longest x1 3.14 us: body(): attention_low = hidden_grad.astype(jnp.bfloat16)]
    pallas_call x1, Pallas kernels: 111 us -> 106 us  [run_exit(): pl.pallas_call(exit_kernel, out_shape=(shape((128, 2048), full), shape((2...]
    reduce_sum x3 -> x0, other arithmetic: 4.72 us -> none  [the longest x1 1.88 us: body(): mlp_sum = jnp.sum(mlp_grad * mlp_unit, 0)]
    unnamed x45 -> x14, local copies, waits for them, and re-layouts: 9.02 us -> 9.04 us
where the time goes in v5:
time: 392 us; the launch traced here: 391 us
  Pallas kernels  355 us (91%)
  local copies, waits for them, and re-layouts  20.1 us (5%)
  matrix products  5.8 us (1%)
  other arithmetic  5.32 us (1%)
  between operations  4.52 us (1%)
    pallas_call x1, Pallas kernels, run_ffn(): pl.pallas_call(ffn_kernel, out_shape=(jax.ShapeDtypeStruct((rows, feature...  154 us
    pallas_call x1, Pallas kernels, run_exit(): pl.pallas_call(exit_kernel, out_shape=(shape((128, 2048), full), shape((2...  106 us
    pallas_call x1, Pallas kernels, run_entry(): pl.pallas_call(entry_kernel, out_shape=(shape((16, 128, 2048), half), sha...  94.9 us
    unnamed x14, local copies, waits for them, and re-layouts  9.04 us

profile of v5, /device:TPU:0, one launch (start us, length us, event | category | flops | bytes accessed | tf_op | source)
XLA Modules:
  0.0 390.6 jit_solution(7402781069101656004)
XLA Ops:
  0.7 0.7 reduce
  1.4 1.4 fusion.10
  4.1 0.7 copy.33
  4.8 0.7 fusion.8
  5.5 1.9 convert_reduce_fusion
  8.1 0.6 fusion.3.small_ref
  8.7 94.9 %entry.1 = (bf16[16,128,2048]{2,1,0:T(8,128)(2,1)}, f32[8,384]{1,0:T(8,128)}, f32[8,128]{1,0:T(8,128)}, f32[8,128]{1,0:T(8,128)}, bf16[704,2048]{1,0:T(8,128)(2,...) custom-call(bf16[128,2048]{1,0:T(8,128)(2,1)} %bitcast.47, ...), custom_call_target="tpu_custom_call" | custom-call | flops 64424509440 | bytes 16777216 | tf_op jit(solution)/shard_map/entry/pallas_call | solution.py:1294
  103.6 1.2 slice.33
  106.2 0.8 broadcast_in_dim.30.mask_ref
  107.0 5.8 %fusion.hidden_ref = f32[128,2048]{1,0:T(8,128)} fusion(bf16[16,128,2048]{2,1,0:T(8,128)(2,1)} %get-tuple-element.45.out_full_ref, bf16[128,2048]{1,0:T(8,128)(2,1)S(1)} %bitcast.49, bf16[16,128,128]{2,1,0:T(8,128)(2,1)} %get-tuple-element.44), kind=kOutput, calls=%fused_computation.2 | convolution fusion | flops 1074266112 | bytes 10485760 | tf_op jit(solution)/shard_map/dot_general | solution.py:15
  112.8 154.1 %feed_forward.1 = (bf16[128,2048]{1,0:T(8,128)(2,1)}, f32[128,2048]{1,0:T(8,128)}, bf16[128,2048]{1,0:T(8,128)(2,1)}, f32[24,256]{1,0:T(8,128)}, bf16[768,2048]{1,0:T(8,128)(2,1)}, /*index=5*/f32[384,256]{1,0:T(8,128)}) custom-call(f32[128,2048]{1,0:T(8,128)} %fusion.hidden_ref, f32[1,2048]{1,0:T(1,128)} %bitcast.63, bf16[128,2048]{1,0:T(8,128)(2,1)} %bitcast.59, ...), custom_call_target="tpu_custom_call" | custom-call | flops 171798691840 | bytes 16777216 | tf_op jit(solution)/shard_map/feed_forward/pallas_call | solution.py:913
  266.9 105.9 %exit.1 = (f32[128,2048]{1,0:T(8,128)}, f32[768,256]{1,0:T(8,128)}, f32[3,256,128]{2,1,0:T(8,128)}, f32[16,256]{1,0:T(8,128)}, f32[128,256]{1,0:T(8,128)}, /*index=5*/f32[24,256]{1,0:T(8,128)}) custom-call(bf16[16,128,2048]{2,1,0:T(8,128)(2,1)} %get-tuple-element.45.out_full_ref, bf16[128,2048]{1,0:T(8,128)(2,1)} %get-tuple-element.49.attention_ref, ...), custom_call_target="tpu_custom_call" | custom-call | flops 64424509440 | bytes 16777216 | tf_op jit(solution)/shard_map/exit/pallas_call | solution.py:1545
  372.8 1.2 slice.34
  374.6 1.2 slice.38
  375.8 1.3 slice_bitcast_fusion.4
  377.1 0.7 slice.37
  377.8 0.6 reshape.160
  378.4 0.7 slice_bitcast_fusion.2
  380.3 0.8 slice.42
  381.0 2.0 slice_bitcast_fusion
  383.0 0.8 copy.44
  383.8 2.3 copy.45
  386.1 1.8 copy.46
  387.9 1.6 copy.47
  (20 shorter events, 2.7 us)
Async XLA Ops:
  8.7 98.2 %copy-start = (bf16[2,64,2048]{2,1,0:T(8,128)(2,1)S(1)}, bf16[2,64,2048]{2,1,0:T(8,128)(2,1)}, u32[]{:S(2)}) copy-start(bf16[2,64,2048]{2,1,0:T(8,128)(2,1)} %param.14) | copy-start | bytes 1572868
  266.9 113.4 %copy-start.2 = (f32[384,256]{1,0:T(8,128)S(1)}, f32[384,256]{1,0:T(8,128)}, u32[]{:S(2)}) copy-start(f32[384,256]{1,0:T(8,128)} %get-tuple-element.74) | copy-start | bytes 1179652
  266.9 116.2 %copy-start.1 = (bf16[128,2048]{1,0:T(8,128)(2,1)S(1)}, bf16[128,2048]{1,0:T(8,128)(2,1)}, u32[]{:S(2)}) copy-start(bf16[128,2048]{1,0:T(8,128)(2,1)} %get-tuple-element.48) | copy-start | bytes 1572868

commit v6 on v5

--- a/solution.py
+++ b/solution.py
@@ -82,7 +82,7 @@
 
 
 def activate(total):
-    sigma = jax.nn.sigmoid(total)
+    sigma = sigmoid(total)
     act = total * sigma
     query, keys, values = act[:, :128], act[:, 128:256], act[:, 256:]
     query_scale = lax.rsqrt(jnp.sum(query * query, -1, keepdims=True) + 1e-06)
@@ -134,7 +134,7 @@
             queries.append(low(query * 128 ** (-0.5)))
             keys_all.append(keys)
             values_all.append(low(values))
-            betas.append(jax.nn.sigmoid(load(proj_ref, index, sequence, slice(384, 512))))
+            betas.append(sigmoid(load(proj_ref, index, sequence, slice(384, 512))))
             withins.append((depth >= 0) & (depth.astype(jnp.float32) <= place))
             carrieds.append(place > row.astype(jnp.float32))
         grams = [fine(nt, split(keys), split(keys * beta)) for keys, beta in zip(keys_all, betas)]
@@ -182,7 +182,7 @@
         reads = [nn(load(query_ref, *stream), state) for stream, state in zip(streams, states)]
         updates = [free_ref[block] - recall for block, recall in zip(blocks, recalls)]
         weighted = [
-            low(jax.nn.sigmoid(load(proj_ref, *stream, slice(384, 512))) * update)
+            low(sigmoid(load(proj_ref, *stream, slice(384, 512))) * update)
             for stream, update in zip(streams, updates)
         ]
         mixed = [nn(score_ref[block], weight) for block, weight in zip(blocks, weighted)]
@@ -224,7 +224,7 @@
         for (index, sequence), back_low, pull in zip(streams, back_lows, pulls):
             _, place = columns_of(pos_ref, index, sequence)
             carried = place > row.astype(jnp.float32)
-            beta = jax.nn.sigmoid(load(proj_ref, index, sequence, slice(384, 512)))
+            beta = sigmoid(load(proj_ref, index, sequence, slice(384, 512)))
             rights.append(
                 jnp.concatenate([jnp.where(carried, back_low, 0.0), low(-beta * pull)], 0)
             )
@@ -254,7 +254,7 @@
             line, place = columns_of(pos_ref, index, sequence)
             lines.append(line)
             places.append(place)
-            betas.append(jax.nn.sigmoid(load(proj_ref, index, sequence, slice(384, 512))))
+            betas.append(sigmoid(load(proj_ref, index, sequence, slice(384, 512))))
             carrieds.append(place > row.astype(jnp.float32))
             closings.append((127 - row).astype(jnp.float32) <= line[:, 127:128])
         queries = [load(query_ref, *stream) for stream in streams]
@@ -1169,8 +1169,6 @@
 
     def ready():
         tiny.arrive()
-        two.arrive()
-        total_ref[...] = jnp.sum(count_rows[...], 0)
         table = jnp.sum(small[:, 0:16].astype(jnp.float32), 0)
         for block in range(8):
             for part in range(2):
@@ -1208,13 +1206,13 @@
     ]
     a[0].second()
     a[1].start()
-    outer()
-    counted()
     mix.relay()
     a[0].third()
+    counted()
     a[0].fourth()
     ready()
     a[1].second()
+    outer()
     a[0].fifth()
     mix.arrive()
     wide.start()
@@ -1228,7 +1226,7 @@
                 0: [pair(a[0], ORDER[0])],
                 1: [pair(a[0], ORDER[1])],
                 2: [pair(a[0], ORDER[2])],
-                3: [a[1].third, pair(a[0], ORDER[3])],
+                3: [a[1].third, everything.second, pair(a[0], ORDER[3])],
                 4: [pair(a[1], ORDER[0])],
                 5: [pair(a[1], ORDER[1])],
                 6: [pair(a[1], ORDER[2])],
@@ -1246,11 +1244,11 @@
             proj_ref, pos_ref, taps_ref, gain_ref,
             heads_ref, query_ref, key_ref, inv_ref, kc_ref, score_ref, step_ref, state_ref, update_ref, raw_ref,
             free_ref, shift_ref, sequence,
-            lambda: at_steps(sequence, {0: [a[1].fourth, everything.second, wide.relay, wide_up.relay], 1: [everything.third, saves[0].start]}),
+            lambda: at_steps(sequence, {0: [a[1].fourth, wide.relay, wide_up.relay], 1: [everything.fourth, saves[0].start]}),
         )
         at_steps(sequence, {
-            0: [exchanges[0].start, a[1].fifth],
-            1: [exchanges[1].start, everything.fourth],
+            0: [exchanges[0].start, everything.third, a[1].fifth],
+            1: [exchanges[1].start],
         })
         return carry
 
@@ -1259,6 +1257,8 @@
     for save in (saves[2:]):
         save.start()
     everything.fifth()
+    two.arrive()
+    total_ref[...] = jnp.sum(count_rows[...], 0)
     everything.from_twin(*NAMES)
     wide.arrive()
     wide_up.arrive()
@@ -1369,26 +1369,26 @@
     base.start()
     attention[own] = attention_ref[...]
     greet(everyone())
-    fill.wait()
-
-    def head_grads(head, carry):
-        flow_ref[head] = low(nt(attention_ref[...], part[head]))
-        return carry
-
-    lax.fori_loop(0, 16, head_grads, 0)
-
-    def head_rows(block):
-        return grad.at[pl.ds(pl.multiple_of(block * 128, 128), 128)]
-
-    exchange = Fan("tensor", 16, lambda peer: flow_ref.at[peer], head_rows, head_send, head_recv)
-    exchange.start()
-    gather = Gather(near, attention, gather_send, gather_recv)
-    gather.start()
     ffn = DataScatter(
         lambda block: ffn_part_ref.at[:, lanes(block)], lambda other, rows: ffn_own[other, rows],
         ffn_slot, ffn_staged, ffn_send, ffn_recv,
     )
     ffn.start()
+    gather = Gather(near, attention, gather_send, gather_recv)
+    gather.start()
+    fill.wait()
+
+    def head_grads(head, carry):
+        flow_ref[head] = low(nt(attention_ref[...], part[head]))
+        return carry
+
+    lax.fori_loop(0, 16, head_grads, 0)
+
+    def head_rows(block):
+        return grad.at[pl.ds(pl.multiple_of(block * 128, 128), 128)]
+
+    exchange = Fan("tensor", 16, lambda peer: flow_ref.at[peer], head_rows, head_send, head_recv)
+    exchange.start()
     grad[pl.ds(pl.multiple_of(tensor * 128, 128), 128)] = flow_ref[tensor]
     exchange.arrive()
     exchange.finish()

time: 392 us -> 381 us (0.972)
  Pallas kernels: 355 us -> 344 us
    pallas_call x1, Pallas kernels: 94.9 us -> 84.5 us  [run_entry(): pl.pallas_call(entry_kernel, out_shape=(shape((16, 128, 2048), half), sha...]
where the time goes in v6:
time: 381 us; the launch traced here: 380 us
  Pallas kernels  344 us (90%)
  local copies, waits for them, and re-layouts  20.1 us (5%)
  matrix products  5.8 us (2%)
  other arithmetic  5.32 us (1%)
  between operations  4.52 us (1%)
    pallas_call x1, Pallas kernels, run_ffn(): pl.pallas_call(ffn_kernel, out_shape=(jax.ShapeDtypeStruct((rows, feature...  156 us
    pallas_call x1, Pallas kernels, run_exit(): pl.pallas_call(exit_kernel, out_shape=(shape((128, 2048), full), shape((2...  104 us
    pallas_call x1, Pallas kernels, run_entry(): pl.pallas_call(entry_kernel, out_shape=(shape((16, 128, 2048), half), sha...  84.5 us
    unnamed x14, local copies, waits for them, and re-layouts  9.04 us

profile of v6, /device:TPU:0, one launch (start us, length us, event | category | flops | bytes accessed | tf_op | source)
XLA Modules:
  0.0 379.8 jit_solution(16561580254115922134)
XLA Ops:
  0.7 0.7 reduce
  1.4 1.4 fusion.10
  4.1 0.7 copy.33
  4.8 0.7 fusion.8
  5.5 1.9 convert_reduce_fusion
  8.1 0.6 fusion.3.small_ref
  8.7 84.5 %entry.1 = (bf16[16,128,2048]{2,1,0:T(8,128)(2,1)}, f32[8,384]{1,0:T(8,128)}, f32[8,128]{1,0:T(8,128)}, f32[8,128]{1,0:T(8,128)}, bf16[704,2048]{1,0:T(8,128)(2,...) custom-call(bf16[128,2048]{1,0:T(8,128)(2,1)} %bitcast.47, ...), custom_call_target="tpu_custom_call" | custom-call | flops 64424509440 | bytes 16777216 | tf_op jit(solution)/shard_map/entry/pallas_call | solution.py:1294
  93.3 1.2 slice.33
  95.8 0.8 broadcast_in_dim.30.mask_ref
  96.6 5.8 %fusion.hidden_ref = f32[128,2048]{1,0:T(8,128)} fusion(bf16[16,128,2048]{2,1,0:T(8,128)(2,1)} %get-tuple-element.45.out_full_ref, bf16[128,2048]{1,0:T(8,128)(2,1)S(1)} %bitcast.49, bf16[16,128,128]{2,1,0:T(8,128)(2,1)} %get-tuple-element.44), kind=kOutput, calls=%fused_computation.2 | convolution fusion | flops 1074266112 | bytes 10485760 | tf_op jit(solution)/shard_map/dot_general | solution.py:15
  102.4 155.6 %feed_forward.1 = (bf16[128,2048]{1,0:T(8,128)(2,1)}, f32[128,2048]{1,0:T(8,128)}, bf16[128,2048]{1,0:T(8,128)(2,1)}, f32[24,256]{1,0:T(8,128)}, bf16[768,2048]{1,0:T(8,128)(2,1)}, /*index=5*/f32[384,256]{1,0:T(8,128)}) custom-call(f32[128,2048]{1,0:T(8,128)} %fusion.hidden_ref, f32[1,2048]{1,0:T(1,128)} %bitcast.63, bf16[128,2048]{1,0:T(8,128)(2,1)} %bitcast.59, ...), custom_call_target="tpu_custom_call" | custom-call | flops 171798691840 | bytes 16777216 | tf_op jit(solution)/shard_map/feed_forward/pallas_call | solution.py:913
  258.0 104.0 %exit.1 = (f32[128,2048]{1,0:T(8,128)}, f32[768,256]{1,0:T(8,128)}, f32[3,256,128]{2,1,0:T(8,128)}, f32[16,256]{1,0:T(8,128)}, f32[128,256]{1,0:T(8,128)}, /*index=5*/f32[24,256]{1,0:T(8,128)}) custom-call(bf16[16,128,2048]{2,1,0:T(8,128)(2,1)} %get-tuple-element.45.out_full_ref, bf16[128,2048]{1,0:T(8,128)(2,1)} %get-tuple-element.49.attention_ref, ...), custom_call_target="tpu_custom_call" | custom-call | flops 64424509440 | bytes 16777216 | tf_op jit(solution)/shard_map/exit/pallas_call | solution.py:1545
  362.0 1.2 slice.34
  363.8 1.2 slice.38
  365.0 1.3 slice_bitcast_fusion.4
  366.3 0.7 slice.37
  367.0 0.6 reshape.160
  367.6 0.7 slice_bitcast_fusion.2
  369.5 0.8 slice.42
  370.3 2.0 slice_bitcast_fusion
  372.3 0.8 copy.44
  373.0 2.3 copy.45
  375.3 1.8 copy.46
  377.1 1.6 copy.47
  (20 shorter events, 2.7 us)
Async XLA Ops:
  8.7 87.9 %copy-start = (bf16[2,64,2048]{2,1,0:T(8,128)(2,1)S(1)}, bf16[2,64,2048]{2,1,0:T(8,128)(2,1)}, u32[]{:S(2)}) copy-start(bf16[2,64,2048]{2,1,0:T(8,128)(2,1)} %param.14) | copy-start | bytes 1572868
  258.0 111.5 %copy-start.2 = (f32[384,256]{1,0:T(8,128)S(1)}, f32[384,256]{1,0:T(8,128)}, u32[]{:S(2)}) copy-start(f32[384,256]{1,0:T(8,128)} %get-tuple-element.74) | copy-start | bytes 1179652
  258.0 114.3 %copy-start.1 = (bf16[128,2048]{1,0:T(8,128)(2,1)S(1)}, bf16[128,2048]{1,0:T(8,128)(2,1)}, u32[]{:S(2)}) copy-start(bf16[128,2048]{1,0:T(8,128)(2,1)} %get-tuple-element.48) | copy-start | bytes 1572868
